TPU v7x, 128 devices: a whole 4x4x4 slice. The times are simulated.
128 devices in a mesh: row: 8 (over y, core), col: 16 (over x, z).
Axes of the slice: x: 4, y: 4, z: 4, core: 2. Of those that a mesh axis runs over, the one named last changes fastest.
Arguments:
- child_fronts: float32 [16384, 8192], P('row', 'col'), may hold values from -3 to 28, as said below
- root_front: float32 [12288, 12288], P('row', 'col'), may hold values from -3 to 28, as said below
- child_map: int32 [2, 60], replicated, may hold values from 0 to 95, as said below
- panel_order: int32 [3], replicated, may hold values from 0 to 47, as said below
Outputs:
- child_factors: float32 [16384, 8192], P('row', 'col')
- root_factors: float32 [12288, 12288], P('row', 'col')
Inputs may be any that keep to these rules, and one draw needn't show every extreme that they name: Each row of child_map holds distinct root blocks; with t = (m mod 6) * 16 + m // 6 for an entry m, t rises by 1 or 2 from one entry of a row to the next. `panel_order`: distinct panels; the last panel of the root front is always among them. `child_fronts`: the diagonal entries lie in 14 to 28, the others in -3 to 3. `root_front`: the diagonal entries lie in 14 to 28, the others in -3 to 3.
All inputs are finite; a program needn't handle non-finite values.
Results may differ from a plain program's by a relative error of at most 0.0003.
Values sent between devices are 32-bit elements; how exact they have to be, the bound alone decides.
A program may use at most 192 MiB of HBM per device.

v0:
```python
import jax
import jax.numpy as jnp
from jax import lax
from jax.sharding import PartitionSpec as P

PANEL = 256
BLK = 128
CPAN = 2
RPAN = 3
NEWTON = 4


highest = lax.Precision.HIGHEST


def broadcast(block, axis, source):
    block = jnp.where(lax.axis_index(axis) == source, block, jnp.zeros_like(block))
    return lax.psum(block, axis)


def newton(pivot_block):
    identity = jnp.eye(pivot_block.shape[0], dtype=jnp.float32)
    inverse = jnp.diag(1.0 / jnp.diagonal(pivot_block))
    for sweep in range(NEWTON):
        inverse = jnp.dot(
            inverse,
            2.0 * identity - jnp.dot(pivot_block, inverse, precision=highest),
            precision=highest,
        )
    return inverse


def fetch_rows(row_band, is_source, slot_count, slot_index):
    selector = (jnp.arange(slot_count) == slot_index).astype(jnp.float32)
    contrib = selector[:, None, None] * jnp.where(is_source, row_band, 0.0)[None]
    totals = lax.psum(contrib, "row")
    return lax.dynamic_index_in_dim(totals, slot_index, 0, keepdims=False)


def multipliers(matrix, pivot_band, plan_entry):
    column_band = lax.dynamic_slice_in_dim(matrix, plan_entry["col_off"], PANEL, 1)
    pivot_block = lax.dynamic_slice_in_dim(pivot_band, plan_entry["col_off"], PANEL, 1)
    column_band, pivot_block = (
        broadcast(column_band, "col", plan_entry["col_owner"]),
        broadcast(pivot_block, "col", plan_entry["col_owner"]),
    )
    factor_cols = jnp.dot(column_band, newton(pivot_block), precision=highest)
    factor_cols = jnp.where(plan_entry["rest_rows"][:, None], factor_cols, 0.0)
    factor_rows = jnp.where(plan_entry["rest_cols"][None, :], pivot_band, 0.0)
    return (factor_cols, factor_rows)


def apply_update(row_band, factor_part, factor_rows, rest_part, plan_entry):
    updated = row_band - jnp.dot(factor_part, factor_rows, precision=highest)
    column_band = lax.dynamic_slice_in_dim(updated, plan_entry["col_off"], PANEL, 1)
    rewritten = lax.dynamic_update_slice_in_dim(
        updated, jnp.where(rest_part[:, None], factor_part, column_band), plan_entry["col_off"], 1
    )
    return jnp.where(plan_entry["col_mine"], rewritten, updated)


def eliminate(matrix, plan, slot_count, slot_index):
    for plan_entry in plan:
        row_band = lax.dynamic_slice_in_dim(matrix, plan_entry["row_off"], PANEL, 0)
        pivot_band = fetch_rows(row_band, plan_entry["row_mine"], slot_count, slot_index)
        factor_cols, factor_rows = multipliers(matrix, pivot_band, plan_entry)
        matrix = apply_update(matrix, factor_cols, factor_rows, plan_entry["rest_rows"], plan_entry)
    return matrix


def schur_routes(source_maps, first_block, count, skip_blocks, per_device):
    positions = jnp.arange(count)
    blocks = first_block[:, None] + positions[None, :]
    schur_index = blocks - skip_blocks
    usable = schur_index >= 0
    target = jnp.take_along_axis(
        source_maps, jnp.clip(schur_index, 0, source_maps.shape[1] - 1), axis=1
    )
    owner = target // per_device
    offset = target % per_device
    earlier = positions[None, :] < positions[:, None]
    same_owner = (owner[:, :, None] == owner[:, None, :]) & usable[:, None, :] & earlier[None]
    return (usable, owner, offset, jnp.sum(same_owner.astype(jnp.int32), axis=2))


def send_select(usable, owner, ranking, peers, capacity):
    chosen = (
        (owner[None, None, :] == jnp.arange(peers)[:, None, None])
        & (ranking[None, None, :] == jnp.arange(capacity)[None, :, None])
        & usable[None, None, :]
    )
    return chosen.astype(jnp.float32)


def receive_select(usable, owner, offset, ranking, receiver, capacity, slot_total):
    arrived = usable & (owner == receiver)
    chosen = (
        arrived[:, None, :, None]
        & (ranking[:, None, :, None] == jnp.arange(capacity)[None, :, None, None])
        & (offset[:, None, :, None] == jnp.arange(slot_total)[None, None, None, :])
    )
    return jnp.sum(chosen.astype(jnp.float32), axis=2)


def body(child_fronts, root_front, child_map, panel_order):
    row_count = lax.axis_size("row")
    col_count = lax.axis_size("col")
    my_row = lax.axis_index("row")
    my_col = lax.axis_index("col")
    group_size = row_count // 2
    child_index = my_row // group_size
    within = my_row % group_size
    row_len, col_len = child_fronts.shape
    row_index = within * row_len + jnp.arange(row_len)
    col_index = my_col * col_len + jnp.arange(col_len)
    child_plan = []
    for column_step in range(CPAN):
        panel_start = column_step * PANEL
        child_plan.append(
            {
                "row_off": panel_start % row_len,
                "row_mine": within == panel_start // row_len,
                "col_off": panel_start % col_len,
                "col_owner": panel_start // col_len,
                "col_mine": my_col == panel_start // col_len,
                "rest_rows": row_index >= panel_start + PANEL,
                "rest_cols": col_index >= panel_start + PANEL,
            }
        )
    factored = eliminate(child_fronts, child_plan, 2, child_index)
    root_rows, root_cols = root_front.shape
    col_blocks = col_len // BLK
    row_blocks = row_len // BLK
    skip_blocks = CPAN * PANEL // BLK
    root_col_blocks = root_cols // BLK
    root_row_blocks = root_rows // BLK
    col_capacity = 2 * (col_blocks - 1) // col_count + 1
    row_capacity = col_count // row_count * (2 * (row_blocks - 1) // col_count + 1)
    own_map = lax.dynamic_index_in_dim(child_map, child_index, 0, keepdims=False)
    col_maps = jnp.broadcast_to(own_map[None], (col_count, own_map.shape[0]))
    usable, owner, offset, ranking = schur_routes(
        col_maps, jnp.arange(col_count) * col_blocks, col_blocks, skip_blocks, root_col_blocks
    )
    outgoing = jnp.einsum(
        "dkj,rjb->dkrb",
        send_select(usable[my_col], owner[my_col], ranking[my_col], col_count, col_capacity),
        factored.reshape(row_len, col_blocks, BLK),
        precision=highest,
    )
    incoming = lax.all_to_all(outgoing, "col", split_axis=0, concat_axis=0, tiled=True)
    placed = jnp.einsum(
        "qkl,qkrb->rlb",
        receive_select(usable, owner, offset, ranking, my_col, col_capacity, root_col_blocks),
        incoming,
        precision=highest,
    ).reshape(row_len, root_cols)
    sources = jnp.arange(row_count)
    row_maps = jnp.take(child_map, sources // group_size, axis=0)
    usable, owner, offset, ranking = schur_routes(
        row_maps, sources % group_size * row_blocks, row_blocks, skip_blocks, root_row_blocks
    )
    outgoing = jnp.einsum(
        "dki,ibx->dkbx",
        send_select(usable[my_row], owner[my_row], ranking[my_row], row_count, row_capacity),
        placed.reshape(row_blocks, BLK, root_cols),
        precision=highest,
    )
    incoming = lax.all_to_all(outgoing, "row", split_axis=0, concat_axis=0, tiled=True)
    added = jnp.einsum(
        "skl,skbx->lbx",
        receive_select(usable, owner, offset, ranking, my_row, row_capacity, root_row_blocks),
        incoming,
        precision=highest,
    ).reshape(root_rows, root_cols)
    assembled = root_front + added
    root_row_index = my_row * root_rows + jnp.arange(root_rows)
    root_col_index = my_col * root_cols + jnp.arange(root_cols)
    root_plan = []
    for column_step in range(RPAN):
        panel_start = panel_order[column_step] * PANEL
        done_panels = panel_order[: column_step + 1]
        root_plan.append(
            {
                "row_off": panel_start % root_rows,
                "row_mine": my_row == panel_start // root_rows,
                "col_off": panel_start % root_cols,
                "col_owner": panel_start // root_cols,
                "col_mine": my_col == panel_start // root_cols,
                "rest_rows": jnp.all(
                    (root_row_index // PANEL)[:, None] != done_panels[None, :], axis=1
                ),
                "rest_cols": jnp.all(
                    (root_col_index // PANEL)[:, None] != done_panels[None, :], axis=1
                ),
            }
        )
    return (factored, eliminate(assembled, root_plan, 1, 0))


def solution(mesh):
    return jax.shard_map(
        body,
        mesh=mesh,
        in_specs=(P("row", "col"), P("row", "col"), P(), P()),
        out_specs=(P("row", "col"), P("row", "col")),
        check_vma=False,
    )
```

profile of v0, /device:TPU:1, one launch (start us, length us, event | category | flops | bytes accessed | tf_op | source)
XLA Modules:
  0.0 1470.0 jit_solution(12554686620891940084)
XLA Ops:
  9.6 3.0 slice_select_fusion.1
  12.7 62.0 %all-reduce.16.cloned.1.call-done = f32[2,256,512]{2,1,0:T(8,128)} async-done(((f32[2,256,512]{2,1,0:T(8,128)}), f32[2,256,512]{2,1,0:T(8,128)}) %all-reduce.16.cloned.1.call-update) | async-done | bytes 1048592 | tf_op jit(solution)/shard_map/psum | solution.py:36
  76.6 94.5 %all-reduce.34.cloned.1.call-done = (f32[2048,256]{1,0:T(8,128)}, f32[256,256]{1,0:T(8,128)}) async-done(((f32[2048,256]{1,0:T(8,128)}, f32[256,256]{1,0:T(8,128)}), (f32[2048,256]{1,0:T(8,128)}, f32[256,256]{1,0:T(8,128)})) %all-reduce.34.cloned.1.call-update) | async-done | bytes 2359312 | tf_op jit(solution)/shard_map/psum | solution.py:18
  171.0 2.6 gather_fusion
  180.0 3.9 convolution_subtract_fusion.4
  188.2 3.0 slice_select_fusion
  191.2 57.3 %all-reduce.18.cloned.1.call-done = f32[2,256,512]{2,1,0:T(8,128)} async-done(((f32[2,256,512]{2,1,0:T(8,128)}), f32[2,256,512]{2,1,0:T(8,128)}) %all-reduce.18.cloned.1.call-update) | async-done | bytes 1048592 | tf_op jit(solution)/shard_map/psum | solution.py:36
  252.3 92.9 %all-reduce.32.cloned.1.call-done = (f32[2048,256]{1,0:T(8,128)}, f32[256,256]{1,0:T(8,128)}) async-done(((f32[2048,256]{1,0:T(8,128)}, f32[256,256]{1,0:T(8,128)}), (f32[2048,256]{1,0:T(8,128)}, f32[256,256]{1,0:T(8,128)})) %all-reduce.32.cloned.1.call-update) | async-done | bytes 2359312 | tf_op jit(solution)/shard_map/psum | solution.py:18
  345.2 2.6 gather_fusion.1
  354.2 5.4 convolution_subtract_fusion.3
  359.6 2.8 fusion.15
  362.4 5.2 reshape.896
  367.7 9.6 convolution_bitcast_fusion
  377.3 10.7 copy.60
  387.9 5.6 all-to-all-start
  396.0 289.9 %all-to-all-done = f32[16,1,2048,128]{3,2,1,0:T(8,128)} async-done(((f32[16,1,2048,128]{3,2,1,0:T(8,128)}), f32[16,1,2048,128]{3,2,1,0:T(8,128)}, u32[]{:S(2)}, u32[]{:S(2)}) %all-to-all-start) | async-done | bytes 16777248 | tf_op jit(solution)/shard_map/all_to_all | solution.py:150
  685.9 20.1 %fusion.8 = f32[2048,6,128]{2,1,0:T(8,128)} fusion(f32[16,1,2048,128]{3,2,1,0:T(8,128)} %all-to-all-done, f32[16,6]{0,1:T(8,128)S(1)} %convert_reduce_fusion.2), kind=kOutput, calls=%fused_computation.23 | convolution fusion | flops 301989888 | bytes 23069056 | tf_op jit(solution)/shard_map/qkl,qkrb->rlb/dot_general | solution.py:151
  706.0 9.1 reshape.955
  715.1 18.5 %fusion.5 = f32[8,4,128,768]{3,1,2,0:T(4,128)} fusion(f32[16,128,768]{2,1,0:T(8,128)} %reshape.955, pred[8,4,16,1]{2,0,1,3:T(8,128)(4,1)S(1)} %and_bitcast_fusion), kind=kOutput, calls=%fused_computation.14 | convolution fusion | flops 603979776 | bytes 18874880 | tf_op jit(solution)/shard_map/dki,ibx->dkbx/dot_general | solution.py:162
  733.6 7.6 all-to-all-start.1
  742.8 137.3 %all-to-all-done.1 = f32[8,4,128,768]{3,1,2,0:T(4,128)} async-done(((f32[8,4,128,768]{3,1,2,0:T(4,128)}), f32[8,4,128,768]{3,1,2,0:T(4,128)}, u32[]{:S(2)}, u32[]{:S(2)}) %all-to-all-start.1) | async-done | bytes 12582944 | tf_op jit(solution)/shard_map/all_to_all | solution.py:168
  880.1 31.4 %fusion.11 = f32[12,128,768]{2,0,1:T(8,128)S(1)} fusion(f32[8,4,128,768]{3,1,2,0:T(4,128)} %all-to-all-done.1, f32[8,4,12]{0,2,1:T(8,128)S(1)} %convert_reduce_fusion), kind=kOutput, calls=%fused_computation.31 | convolution fusion | flops 452984832 | bytes 17303040 | tf_op jit(solution)/shard_map/skl,skbx->lbx/dot_general | solution.py:169
  911.4 2.7 copy.67
  914.2 2.8 bitcast_add_fusion
  917.0 2.2 copy-done.6
  920.2 3.4 dynamic-slice_select_fusion.2
  923.6 62.9 %all-reduce.20.cloned.1.call-done = f32[1,256,768]{2,1,0:T(8,128)} async-done(((f32[1,256,768]{2,1,0:T(8,128)}), f32[1,256,768]{2,1,0:T(8,128)}) %all-reduce.20.cloned.1.call-update) | async-done | bytes 786448 | tf_op jit(solution)/shard_map/psum | solution.py:36
  990.5 89.2 %all-reduce.30.cloned.1.call-done = (f32[1536,256]{1,0:T(8,128)}, f32[256,256]{1,0:T(8,128)}) async-done(((f32[1536,256]{1,0:T(8,128)}, f32[256,256]{1,0:T(8,128)}), (f32[1536,256]{1,0:T(8,128)}, f32[256,256]{1,0:T(8,128)})) %all-reduce.30.cloned.1.call-update) | async-done | bytes 1835024 | tf_op jit(solution)/shard_map/psum | solution.py:18
  1079.7 2.6 gather_fusion.3
  1088.0 4.8 convolution_subtract_fusion.2
  1092.8 2.2 copy-done.4
  1095.7 8.1 select_n.617
  1103.8 2.1 select_bitcast_fusion.1
  1106.0 3.4 dynamic-slice_select_fusion.1
  1109.4 57.1 %all-reduce.22.cloned.1.call-done = f32[1,256,768]{2,1,0:T(8,128)} async-done(((f32[1,256,768]{2,1,0:T(8,128)}), f32[1,256,768]{2,1,0:T(8,128)}) %all-reduce.22.cloned.1.call-update) | async-done | bytes 786448 | tf_op jit(solution)/shard_map/psum | solution.py:36
  1169.6 89.9 %all-reduce.28.cloned.1.call-done = (f32[1536,256]{1,0:T(8,128)}, f32[256,256]{1,0:T(8,128)}) async-done(((f32[1536,256]{1,0:T(8,128)}, f32[256,256]{1,0:T(8,128)}), (f32[1536,256]{1,0:T(8,128)}, f32[256,256]{1,0:T(8,128)})) %all-reduce.28.cloned.1.call-update) | async-done | bytes 1835024 | tf_op jit(solution)/shard_map/psum | solution.py:18
  1259.4 2.6 gather_fusion.4
  1267.8 4.8 convolution_subtract_fusion.1
  1272.6 2.2 copy-done.5
  1275.4 8.1 select_n.636
  1283.6 2.1 select_bitcast_fusion
  1286.0 3.1 dynamic-slice_select_fusion
  1289.2 57.1 %all-reduce.24.cloned.1.call-done = f32[1,256,768]{2,1,0:T(8,128)} async-done(((f32[1,256,768]{2,1,0:T(8,128)}), f32[1,256,768]{2,1,0:T(8,128)}) %all-reduce.24.cloned.1.call-update) | async-done | bytes 786448 | tf_op jit(solution)/shard_map/psum | solution.py:36
  1348.3 91.1 %all-reduce.26.cloned.1.call-done = (f32[1536,256]{1,0:T(8,128)}, f32[256,256]{1,0:T(8,128)}) async-done(((f32[1536,256]{1,0:T(8,128)}, f32[256,256]{1,0:T(8,128)}), (f32[1536,256]{1,0:T(8,128)}, f32[256,256]{1,0:T(8,128)})) %all-reduce.26.cloned.1.call-update) | async-done | bytes 1835024 | tf_op jit(solution)/shard_map/psum | solution.py:18
  1439.4 2.6 gather_fusion.5
  1447.7 4.8 convolution_subtract_fusion
  1452.5 2.2 copy-done.13
  1455.4 7.3 select_n.655
  (197 shorter events, 55.7 us)
Async XLA Ops:
  7.2 243.4 %copy-start = (s32[2,60]{1,0:T(2,128)S(1)}, s32[2,60]{1,0:T(2,128)}, u32[]{:S(2)}) copy-start(s32[2,60]{1,0:T(2,128)} %param.6) | copy-start | bytes 1444
  7.2 67.4 %all-reduce.16.cloned.1.call-start = ((), (), s32[]{:S(2)}) async-start(), calls=%async_computation.2 | async-start | bytes 2097152 | tf_op jit(solution)/shard_map/psum | solution.py:36
  9.5 161.5 %all-reduce.34.cloned.1.call-start = ((), (), s32[]{:S(2)}) async-start(), calls=%async_computation.11 | async-start | bytes 4718592 | tf_op jit(solution)/shard_map/psum | solution.py:18
  76.5 172.1 %all-reduce.18.cloned.1.call-start = ((), (), s32[]{:S(2)}) async-start(), calls=%async_computation.3 | async-start | bytes 2097152 | tf_op jit(solution)/shard_map/psum | solution.py:36
  171.0 4.5 copy-start.10
  175.9 1.9 copy-start.15
  177.9 2.2 copy-start.12
  184.6 2.0 copy-start.2
  187.9 157.3 %all-reduce.32.cloned.1.call-start = ((), (), s32[]{:S(2)}) async-start(), calls=%async_computation.10 | async-start | bytes 4718592 | tf_op jit(solution)/shard_map/psum | solution.py:18
  345.2 4.5 copy-start.8
  350.0 1.9 copy-start.14
  352.0 2.2 copy-start.3
  387.9 298.0 %all-to-all-start = ((f32[16,1,2048,128]{3,2,1,0:T(8,128)}), f32[16,1,2048,128]{3,2,1,0:T(8,128)}, u32[]{:S(2)}, u32[]{:S(2)}) async-start(f32[16,1,2048,128]{3,2,1,0:T(8,128)} %copy.60), calls=%async_computation | async-start | bytes 33554432 | tf_op jit(solution)/shard_map/all_to_all | solution.py:150
  733.6 7.6 copy-start.22
  733.6 146.4 %all-to-all-start.1 = ((f32[8,4,128,768]{3,1,2,0:T(4,128)}), f32[8,4,128,768]{3,1,2,0:T(4,128)}, u32[]{:S(2)}, u32[]{:S(2)}) async-start(f32[8,4,128,768]{3,1,2,0:T(4,128)} %fusion.5), calls=%async_computation.1 | async-start | bytes 25165824 | tf_op jit(solution)/shard_map/all_to_all | solution.py:168
  741.2 245.3 %all-reduce.20.cloned.1.call-start = ((), (), s32[]{:S(2)}) async-start(), calls=%async_computation.4 | async-start | bytes 1572864 | tf_op jit(solution)/shard_map/psum | solution.py:36
  917.0 2.2 copy-start.6
  920.1 159.5 %all-reduce.30.cloned.1.call-start = ((), (), s32[]{:S(2)}) async-start(), calls=%async_computation.9 | async-start | bytes 3670016 | tf_op jit(solution)/shard_map/psum | solution.py:18
  920.2 167.7 %slice-start.4 = ((s8[4718592]{0:T(1024)(128)(4,1)}), s8[524288]{0:T(1024)(128)(4,1)S(1)}, s32[]{:S(2)}) async-start(s8[4718592]{0:T(1024)(128)(4,1)} %bitcast.177), calls=%async_computation.16 | async-start | bytes 1048576
  988.4 178.1 %all-reduce.22.cloned.1.call-start = ((), (), s32[]{:S(2)}) async-start(), calls=%async_computation.5 | async-start | bytes 1572864 | tf_op jit(solution)/shard_map/psum | solution.py:36
  1079.7 4.5 copy-start.9
  1083.7 2.8 copy-start.17
  1084.2 3.8 slice-start.5
  1086.1 1.9 copy-start.20
  1092.8 2.2 copy-start.4
  1105.9 153.5 %all-reduce.28.cloned.1.call-start = ((), (), s32[]{:S(2)}) async-start(), calls=%async_computation.8 | async-start | bytes 3670016 | tf_op jit(solution)/shard_map/psum | solution.py:18
  1106.0 161.7 %slice-start = ((s8[4718592]{0:T(1024)(128)(4,1)}), s8[524288]{0:T(1024)(128)(4,1)S(1)}, s32[]{:S(2)}) async-start(s8[4718592]{0:T(1024)(128)(4,1)} %bitcast.173), calls=%async_computation.12 | async-start | bytes 1048576
  1168.4 177.8 %all-reduce.24.cloned.1.call-start = ((), (), s32[]{:S(2)}) async-start(), calls=%async_computation.6 | async-start | bytes 1572864 | tf_op jit(solution)/shard_map/psum | solution.py:36
  1259.4 4.5 copy-start.7
  1263.5 2.8 copy-start.16
  1263.9 3.8 slice-start.1
  1265.9 1.9 copy-start.19
  1272.5 2.2 copy-start.5
  1285.7 153.7 %all-reduce.26.cloned.1.call-start = ((), (), s32[]{:S(2)}) async-start(), calls=%async_computation.7 | async-start | bytes 3670016 | tf_op jit(solution)/shard_map/psum | solution.py:18
  1286.0 161.7 %slice-start.2 = ((s8[4718592]{0:T(1024)(128)(4,1)}), s8[524288]{0:T(1024)(128)(4,1)S(1)}, s32[]{:S(2)}) async-start(s8[4718592]{0:T(1024)(128)(4,1)} %bitcast.175), calls=%async_computation.14 | async-start | bytes 1048576
  1439.4 4.5 copy-start.11
  1443.5 2.8 copy-start.18
  1443.9 3.8 slice-start.3
  1445.9 1.9 copy-start.21
  1452.5 2.2 copy-start.13
  1454.7 8.0 copy-start.1
Sparse Core Ops, SparseCore 0:
  10.9 63.6 all-reduce.15
  78.7 92.3 all-reduce.33
  188.0 60.4 all-reduce.17
  252.8 92.2 all-reduce.31
  920.2 66.2 all-reduce.19
  990.2 89.4 all-reduce.29
  1106.0 60.4 all-reduce.21
  1170.0 89.4 all-reduce.27
  1285.8 60.4 all-reduce.23
  1349.9 89.4 all-reduce.25
where the time goes:
time: 1480 us; the launch traced here: 1470 us
  waiting for transfers between devices  1180 us (80%)
  matrix products  132 us (9%)
  local copies, waits for them, and re-layouts  82 us (6%)
  other arithmetic  42.8 us (3%)
  between operations  17.8 us (1%)
    psum x5, waiting for transfers between devices, broadcast(): return lax.psum(block, axis)  457 us
    psum x5, waiting for transfers between devices, fetch_rows(): totals = lax.psum(contrib, 'row')  296 us
    all_to_all x1, waiting for transfers between devices, body(): lax.all_to_all(outgoing, 'col', split_axis=0, concat_axis=0, tiled=True)  290 us
    all_to_all x1, waiting for transfers between devices, body(): lax.all_to_all(outgoing, 'row', split_axis=0, concat_axis=0, tiled=True)  137 us
    dot_general x1, matrix products, body(): jnp.einsum('skl,skbx->lbx', receive_select(usable, owner, offset, ranking...  31.4 us
  transfers between devices with their start and end apart: 12, of which 12 were waited for; matrix products, arithmetic and copies ran while one was open for 2% of the time, Pallas kernels for 0%

commit v1 on v0

v1 whole, which is shorter than its diff:
```python
import functools

import jax
import jax.numpy as jnp
from jax import lax
from jax.experimental import pallas as pl
from jax.experimental.pallas import tpu as pltpu
from jax.sharding import Mesh
from jax.sharding import PartitionSpec as P

PANEL = 256
BLK = 128
CPAN = 2
RPAN = 3
NEWTON = 4


ROW = ("y", "core")
COL = ("x", "z")
MESH = pl.DeviceIdType.MESH

highest = lax.Precision.HIGHEST


def broadcast(block, axis, source):
    block = jnp.where(lax.axis_index(axis) == source, block, jnp.zeros_like(block))
    return lax.psum(block, axis)


def newton(pivot_block):
    identity = jnp.eye(pivot_block.shape[0], dtype=jnp.float32)
    inverse = jnp.diag(1.0 / jnp.diagonal(pivot_block))
    for sweep in range(NEWTON):
        inverse = jnp.dot(
            inverse,
            2.0 * identity - jnp.dot(pivot_block, inverse, precision=highest),
            precision=highest,
        )
    return inverse


def fetch_rows(row_band, is_source, slot_count, slot_index):
    selector = (jnp.arange(slot_count) == slot_index).astype(jnp.float32)
    contrib = selector[:, None, None] * jnp.where(is_source, row_band, 0.0)[None]
    totals = lax.psum(contrib, ROW)
    return lax.dynamic_index_in_dim(totals, slot_index, 0, keepdims=False)


def multipliers(matrix, pivot_band, plan_entry):
    column_band = lax.dynamic_slice_in_dim(matrix, plan_entry["col_off"], PANEL, 1)
    pivot_block = lax.dynamic_slice_in_dim(pivot_band, plan_entry["col_off"], PANEL, 1)
    column_band, pivot_block = (
        broadcast(column_band, COL, plan_entry["col_owner"]),
        broadcast(pivot_block, COL, plan_entry["col_owner"]),
    )
    factor_cols = jnp.dot(column_band, newton(pivot_block), precision=highest)
    factor_cols = jnp.where(plan_entry["rest_rows"][:, None], factor_cols, 0.0)
    factor_rows = jnp.where(plan_entry["rest_cols"][None, :], pivot_band, 0.0)
    return (factor_cols, factor_rows)


def apply_update(row_band, factor_part, factor_rows, rest_part, plan_entry):
    updated = row_band - jnp.dot(factor_part, factor_rows, precision=highest)
    column_band = lax.dynamic_slice_in_dim(updated, plan_entry["col_off"], PANEL, 1)
    rewritten = lax.dynamic_update_slice_in_dim(
        updated, jnp.where(rest_part[:, None], factor_part, column_band), plan_entry["col_off"], 1
    )
    return jnp.where(plan_entry["col_mine"], rewritten, updated)


def eliminate(matrix, plan, slot_count, slot_index):
    for plan_entry in plan:
        row_band = lax.dynamic_slice_in_dim(matrix, plan_entry["row_off"], PANEL, 0)
        pivot_band = fetch_rows(row_band, plan_entry["row_mine"], slot_count, slot_index)
        factor_cols, factor_rows = multipliers(matrix, pivot_band, plan_entry)
        matrix = apply_update(matrix, factor_cols, factor_rows, plan_entry["rest_rows"], plan_entry)
    return matrix


def peers_of(axes):
    if axes == ROW:
        me = 2 * lax.axis_index("y") + lax.axis_index("core")
        return me, 8, lambda p: {"y": p // 2, "core": lax.rem(p, 2)}
    return lax.axis_index(axes), 4, lambda p: {axes: p}


def exchange(arrays, axes, collective_id):
    n = len(arrays)

    def kernel(*refs):
        ins, outs = refs[:n], refs[n : 2 * n]
        send_sem, recv_sem, own_sem = refs[2 * n :]
        barrier = pltpu.get_barrier_semaphore()
        total = 0
        for ax in axes:
            me, size, ident = peers_of(ax)
            for d in range(1, size):
                pl.semaphore_signal(
                    barrier, inc=1, device_id=ident(lax.rem(me + d, size)), device_id_type=MESH
                )
            total += size - 1
        own = []
        for i, ax in enumerate(axes):
            me, size, ident = peers_of(ax)
            copy = pltpu.make_async_copy(ins[i].at[me], outs[i].at[me], own_sem.at[i])
            copy.start()
            own.append(copy)
        pl.semaphore_wait(barrier, total)
        copies = []
        for i, ax in enumerate(axes):
            me, size, ident = peers_of(ax)
            for d in sorted(range(1, size), key=lambda d: -min(d, size - d)):
                p = lax.rem(me + d, size)
                copy = pltpu.make_async_remote_copy(
                    src_ref=ins[i].at[p],
                    dst_ref=outs[i].at[me],
                    send_sem=send_sem.at[i, d],
                    recv_sem=recv_sem.at[i, d],
                    device_id=ident(p),
                    device_id_type=MESH,
                )
                copy.start()
                copies.append(copy)
        for copy in own + copies:
            copy.wait()

    return pl.pallas_call(
        kernel,
        out_shape=[jax.ShapeDtypeStruct(a.shape, a.dtype) for a in arrays],
        in_specs=[pl.BlockSpec(memory_space=pl.ANY)] * n,
        out_specs=[pl.BlockSpec(memory_space=pl.ANY)] * n,
        scratch_shapes=[
            pltpu.SemaphoreType.DMA((n, 8)),
            pltpu.SemaphoreType.DMA((n, 8)),
            pltpu.SemaphoreType.DMA((n,)),
        ],
        compiler_params=pltpu.CompilerParams(collective_id=collective_id, has_side_effects=True),
    )(*arrays)


def rank_in(key, group, valid):
    n = key.shape[1]
    earlier = jnp.arange(n)[None, :] < jnp.arange(n)[:, None]
    same = (key[:, :, None] == key[:, None, :]) & (group[:, None] == group[None, :])[None]
    return jnp.sum((same & valid[:, None, :] & earlier[None]).astype(jnp.int32), axis=2)


def find(match, value):
    return jnp.sum(jnp.where(match, value + 1, 0), axis=-1) - 1


def routes(child_map):
    y, core = lax.axis_index("y"), lax.axis_index("core")
    x, z = lax.axis_index("x"), lax.axis_index("z")
    my_child, within = y // 2, lax.rem(y, 2) * 2 + core
    r, o = 2 * y + core, 4 * x + z
    blocks = jnp.arange(64)
    skip = CPAN * PANEL // BLK
    cyclic = (child_map % 6) * 16 + child_map // 6
    t = jnp.concatenate([jnp.zeros((2, skip), jnp.int32), cyclic], axis=1)
    valid = jnp.broadcast_to(blocks >= skip, (2, 64))
    kz = rank_in(t % 4, blocks // 4, valid)
    kx = rank_in(t % 16, blocks // 16, valid)
    kr = rank_in(t % 16 // 2, blocks // 16, valid)
    four, two = jnp.arange(4), jnp.arange(2)

    mine = valid & (blocks // 4 == o)[None]
    z_pick = find(
        mine[:, None, None]
        & ((t % 4)[:, None, None] == four[None, :, None, None])
        & (kz[:, None, None] == two[None, None, :, None]),
        blocks % 4,
    )
    mine = valid & (blocks // 16 == x)[None] & (t % 4 == z)
    x_pick = find(
        mine[:, None, None]
        & ((t % 16 // 4)[:, None, None] == four[None, :, None, None])
        & (kx[:, None, None] == two[None, None, :, None]),
        ((blocks // 4 % 4)[None] * 2 + kz)[:, None, None],
    )
    slots = jnp.arange(6)
    col_from = find(
        valid[:, None] & (t[:, None] == (slots * 16 + o)[None, :, None]),
        ((blocks // 16)[None] * 2 + kx)[:, None],
    )
    mine = valid & (blocks // 16 == within)[None]
    own = lambda a: lax.dynamic_index_in_dim(a, my_child, 0, keepdims=False)
    r_pick = find(
        own(mine)[None, None]
        & (own(t % 16 // 2)[None, None] == jnp.arange(8)[:, None, None])
        & (own(kr)[None, None] == four[None, :, None]),
        blocks % 16,
    )
    slots = jnp.arange(12)
    row_from = find(
        valid[:, None] & (t[:, None] == (slots % 6 * 16 + 2 * r + slots // 6)[None, :, None]),
        ((jnp.arange(2)[:, None] * 4 + (blocks // 16)[None]) * 4 + kr)[:, None],
    )
    return own(z_pick), z_pick, x_pick, own(x_pick), col_from, own(col_from), r_pick, row_from


Z_OWN, Z_PICK, X_PICK, X_OWN, COL_FROM, COL_OWN, R_PICK, ROW_FROM = 0, 8, 24, 40, 48, 60, 66, 98


def whole(shape):
    return pl.BlockSpec(shape, lambda g, tab: (0,) * len(shape))


def part(shape):
    return pl.BlockSpec((1,) + shape, lambda g, tab: (g,) + (0,) * len(shape))


def local_call(kernel, grid, table, operands, in_specs, out_shapes, out_specs):
    return pl.pallas_call(
        kernel,
        grid_spec=pltpu.PrefetchScalarGridSpec(
            num_scalar_prefetch=1, grid=(grid,), in_specs=in_specs, out_specs=out_specs
        ),
        out_shape=[jax.ShapeDtypeStruct(s, jnp.float32) for s in out_shapes],
        compiler_params=pltpu.CompilerParams(vmem_limit_bytes=56 * 1024 * 1024),
    )(table, *operands)


def at_least_zero(v):
    return jnp.maximum(v, 0)


def lanes(block):
    return pl.ds(pl.multiple_of(block * BLK, BLK), BLK)


def pack_first(tab, front, za, yb):
    g = pl.program_id(0)
    za[0] = front[:, 0:64, lanes(at_least_zero(tab[Z_OWN + g]))]
    for k in range(4):
        yb[0, k] = front[at_least_zero(tab[R_PICK + g * 4 + k]), 64:128, :]


def pack_second(tab, zin, yin, xa, zb):
    g = pl.program_id(0)
    xa[0] = zin[at_least_zero(tab[X_OWN + g])]
    for c in range(2):
        column = lanes(at_least_zero(tab[Z_PICK + c * 8 + g]))
        for i in range(12):
            source = at_least_zero(tab[ROW_FROM + c * 12 + i])
            zb[0, c * 12 + i] = yin[source, :, column]


def pack_third(tab, xin, zin, ya, xb):
    g = pl.program_id(0)
    for c in range(2):
        source = at_least_zero(tab[X_PICK + c * 8 + g])
        xb[0, c * 12 : c * 12 + 12] = zin[source, c * 12 : c * 12 + 12]
    for k in range(4):
        i = at_least_zero(tab[R_PICK + g * 4 + k])
        for slot in range(6):
            source = at_least_zero(tab[COL_OWN + slot])
            ya[0, k, :, slot * BLK : slot * BLK + BLK] = xin[source, i]


def add_all(tab, root, yin, xin, out):
    i = pl.program_id(0)
    for slot in range(6):
        columns = slice(slot * BLK, slot * BLK + BLK)
        upper, lower = root[0, 0:64, columns], root[0, 64:128, columns]
        for c in range(2):
            row, col = tab[ROW_FROM + c * 12 + i], tab[COL_FROM + c * 6 + slot]
            there = jnp.logical_and(row >= 0, col >= 0)
            upper += jnp.where(there, yin[at_least_zero(row), :, columns], 0.0)
            lower += jnp.where(there, xin[at_least_zero(col), c * 12 + i], 0.0)
        out[0, 0:64, columns] = upper
        out[0, 64:128, columns] = lower


def extend_add(factored, root_front, child_map):
    table = jnp.concatenate([a.reshape(-1) for a in routes(child_map)])
    front = factored.reshape(16, BLK, 512)
    za, yb = local_call(
        pack_first, 8, table, (front,), [whole((16, BLK, 512))],
        [(8, 16, 64, BLK), (8, 4, 64, 512)], [part((16, 64, BLK)), part((4, 64, 512))],
    )
    za, yb = exchange([za.reshape(4, 2, 16, 64, BLK), yb], ["z", ROW], 1)
    xa, zb = local_call(
        pack_second, 8, table, (za.reshape(8, 16, 64, BLK), yb.reshape(32, 64, 512)),
        [whole((8, 16, 64, BLK)), whole((32, 64, 512))],
        [(8, 16, 64, BLK), (8, 24, 64, BLK)], [part((16, 64, BLK)), part((24, 64, BLK))],
    )
    xa, zb = exchange(
        [xa.reshape(4, 2, 16, 64, BLK), zb.reshape(4, 2, 24, 64, BLK)], ["x", "z"], 2
    )
    ya, xb = local_call(
        pack_third, 8, table, (xa.reshape(8, 16, 64, BLK), zb.reshape(8, 24, 64, BLK)),
        [whole((8, 16, 64, BLK)), whole((8, 24, 64, BLK))],
        [(8, 4, 64, 768), (8, 24, 64, BLK)], [part((4, 64, 768)), part((24, 64, BLK))],
    )
    ya, xb = exchange([ya, xb.reshape(4, 2, 24, 64, BLK)], [ROW, "x"], 3)
    (assembled,) = local_call(
        add_all, 12, table,
        (root_front.reshape(12, BLK, 768), ya.reshape(32, 64, 768), xb.reshape(8, 24, 64, BLK)),
        [part((BLK, 768)), whole((32, 64, 768)), whole((8, 24, 64, BLK))],
        [(12, BLK, 768)], [part((BLK, 768))],
    )
    return assembled.reshape(root_front.shape)


def body(child_fronts, root_front, child_map, panel_order):
    row_count = lax.axis_size(ROW)
    col_count = lax.axis_size(COL)
    my_row = lax.axis_index(ROW)
    my_col = lax.axis_index(COL)
    group_size = row_count // 2
    child_index = my_row // group_size
    within = my_row % group_size
    row_len, col_len = child_fronts.shape
    row_index = within * row_len + jnp.arange(row_len)
    col_index = my_col * col_len + jnp.arange(col_len)
    child_plan = []
    for column_step in range(CPAN):
        panel_start = column_step * PANEL
        child_plan.append(
            {
                "row_off": panel_start % row_len,
                "row_mine": within == panel_start // row_len,
                "col_off": panel_start % col_len,
                "col_owner": panel_start // col_len,
                "col_mine": my_col == panel_start // col_len,
                "rest_rows": row_index >= panel_start + PANEL,
                "rest_cols": col_index >= panel_start + PANEL,
            }
        )
    factored = eliminate(child_fronts, child_plan, 2, child_index)
    root_rows, root_cols = root_front.shape
    assembled = extend_add(factored, root_front, child_map)
    root_row_index = my_row * root_rows + jnp.arange(root_rows)
    root_col_index = my_col * root_cols + jnp.arange(root_cols)
    root_plan = []
    for column_step in range(RPAN):
        panel_start = panel_order[column_step] * PANEL
        done_panels = panel_order[: column_step + 1]
        root_plan.append(
            {
                "row_off": panel_start % root_rows,
                "row_mine": my_row == panel_start // root_rows,
                "col_off": panel_start % root_cols,
                "col_owner": panel_start // root_cols,
                "col_mine": my_col == panel_start // root_cols,
                "rest_rows": jnp.all(
                    (root_row_index // PANEL)[:, None] != done_panels[None, :], axis=1
                ),
                "rest_cols": jnp.all(
                    (root_col_index // PANEL)[:, None] != done_panels[None, :], axis=1
                ),
            }
        )
    return (factored, eliminate(assembled, root_plan, 1, 0))


def solution(mesh):
    grid = Mesh(mesh.devices.reshape(4, 2, 4, 4), ("y", "core", "x", "z"))
    return jax.shard_map(
        body,
        mesh=grid,
        in_specs=(P(ROW, COL), P(ROW, COL), P(), P()),
        out_specs=(P(ROW, COL), P(ROW, COL)),
        check_vma=False,
    )
```

time: 1480 us -> 1160 us (0.78)
  waiting for transfers between devices: 1180 us -> 741 us
  Pallas kernels: 0 us -> 246 us
  matrix products: 132 us -> 50.3 us
  local copies, waits for them, and re-layouts: 82 us -> 52.2 us
    all_to_all x2 -> x0, waiting for transfers between devices: 427 us -> none  [the longest x1 290 us: body(): lax.all_to_all(outgoing, 'col', split_axis=0, concat_axis=0, tiled=True)]
    pallas_call x0 -> x7, Pallas kernels: none -> 246 us  [the longest x3 206 us: exchange(): pl.pallas_call(kernel, out_shape=[jax.ShapeDtypeStruct(a.shape, a.dtype)...]
    dot_general x4 -> x0, matrix products: 79.5 us -> none  [the longest x1 31.4 us: body(): jnp.einsum('skl,skbx->lbx', receive_select(usable, owner, offset, ranking...]
  transfers between devices with their start and end apart: 12 -> 10, of which waited for: 12 -> 10; matrix products, arithmetic and copies ran while one was open for 2% -> 2% of each run, Pallas kernels for 0% -> 0%
where the time goes in v1:
time: 1160 us; the launch traced here: 1150 us
  waiting for transfers between devices  741 us (64%)
  Pallas kernels  246 us (21%)
  local copies, waits for them, and re-layouts  52.2 us (4%)
  matrix products  50.3 us (4%)
  other arithmetic  39.6 us (3%)
  between operations  17.6 us (2%)
    psum x5, waiting for transfers between devices, broadcast(): return lax.psum(block, axis)  454 us
    psum x5, waiting for transfers between devices, fetch_rows(): totals = lax.psum(contrib, ROW)  286 us
    pallas_call x3, Pallas kernels, exchange(): pl.pallas_call(kernel, out_shape=[jax.ShapeDtypeStruct(a.shape, a.dtype)...  206 us
    pallas_call x4, Pallas kernels, local_call(): pl.pallas_call(kernel, grid_spec=pltpu.PrefetchScalarGridSpec(num_scalar_...  40.5 us
  transfers between devices with their start and end apart: 10, of which 10 were waited for; matrix products, arithmetic and copies ran while one was open for 2% of the time, Pallas kernels for 0%

profile of v1, /device:TPU:1, one launch (start us, length us, event | category | flops | bytes accessed | tf_op | source)
XLA Modules:
  0.0 1148.5 jit_solution(17037857780251779666)
XLA Ops:
  10.4 3.0 slice_select_fusion.1
  13.5 61.2 %all-reduce.17.cloned.1.call-done = f32[2,256,512]{2,1,0:T(8,128)} async-done(((f32[2,256,512]{2,1,0:T(8,128)}), f32[2,256,512]{2,1,0:T(8,128)}) %all-reduce.17.cloned.1.call-update) | async-done | bytes 1048592 | tf_op jit(solution)/shard_map/psum | solution.py:45
  77.2 93.8 %all-reduce.35.cloned.1.call-done = (f32[2048,256]{1,0:T(8,128)}, f32[256,256]{1,0:T(8,128)}) async-done(((f32[2048,256]{1,0:T(8,128)}, f32[256,256]{1,0:T(8,128)}), (f32[2048,256]{1,0:T(8,128)}, f32[256,256]{1,0:T(8,128)})) %all-reduce.35.cloned.1.call-update) | async-done | bytes 2359312 | tf_op jit(solution)/shard_map/psum | solution.py:27
  171.0 2.6 gather_fusion
  177.9 1.9 convolution_select_fusion.4
  180.0 3.7 convolution_subtract_fusion.4
  184.5 2.0 copy-done
  187.8 3.0 slice_select_fusion
  190.8 57.5 %all-reduce.19.cloned.1.call-done = f32[2,256,512]{2,1,0:T(8,128)} async-done(((f32[2,256,512]{2,1,0:T(8,128)}), f32[2,256,512]{2,1,0:T(8,128)}) %all-reduce.19.cloned.1.call-update) | async-done | bytes 1048592 | tf_op jit(solution)/shard_map/psum | solution.py:45
  254.5 90.4 %all-reduce.33.cloned.1.call-done = (f32[2048,256]{1,0:T(8,128)}, f32[256,256]{1,0:T(8,128)}) async-done(((f32[2048,256]{1,0:T(8,128)}, f32[256,256]{1,0:T(8,128)}), (f32[2048,256]{1,0:T(8,128)}, f32[256,256]{1,0:T(8,128)})) %all-reduce.33.cloned.1.call-update) | async-done | bytes 2359312 | tf_op jit(solution)/shard_map/psum | solution.py:27
  344.9 2.6 gather_fusion.1
  351.8 1.9 convolution_select_fusion.3
  353.9 4.0 convolution_subtract_fusion.3
  358.7 2.0 copy-done.4
  360.7 7.4 shard_map.59
  368.2 52.2 %shard_map.60 = (f32[4,2,16,64,128]{4,3,2,1,0:T(8,128)}, f32[8,4,64,512]{3,2,1,0:T(8,128)}) custom-call(f32[4,2,16,64,128]{4,3,2,1,0:T(8,128)} %bitcast.165, f32[8,4,64,512]{3,2,1,0:T(8,128)} %get-tuple-element.15.refs_1_), custom_call_target="tpu_custom_call" | custom-call | tf_op jit(solution)/shard_map/pallas_call | solution.py:127
  420.4 9.4 shard_map.61
  429.8 80.8 %shard_map.62 = (f32[4,2,16,64,128]{4,3,2,1,0:T(8,128)}, f32[4,2,24,64,128]{4,3,2,1,0:T(8,128)}) custom-call(f32[4,2,16,64,128]{4,3,2,1,0:T(8,128)} %bitcast.163, f32[4,2,24,64,128]{4,3,2,1,0:T(8,128)} %bitcast.155), custom_call_target="tpu_custom_call" | custom-call | tf_op jit(solution)/shard_map/pallas_call | solution.py:127
  510.6 10.4 shard_map.63
  521.0 72.9 %shard_map.64 = (f32[8,4,64,768]{3,2,1,0:T(8,128)}, f32[4,2,24,64,128]{4,3,2,1,0:T(8,128)}) custom-call(f32[8,4,64,768]{3,2,1,0:T(8,128)} %get-tuple-element.22.refs_0_, f32[4,2,24,64,128]{4,3,2,1,0:T(8,128)} %bitcast.156), custom_call_target="tpu_custom_call" | custom-call | tf_op jit(solution)/shard_map/pallas_call | solution.py:127
  594.0 13.3 %shard_map.65 = f32[12,128,768]{2,1,0:T(8,128)} custom-call(s32[122]{0:T(128)} %concatenate.16.tab, f32[12,128,768]{2,1,0:T(8,128)} %bitcast.160, f32[32,64,768]{2,1,0:T(8,128)} %bitcast.158, f32[8,24,64,128]{3,2,1,0:T(8,128)} %bitcast.159), custom_call_target="tpu_custom_call" | custom-call | tf_op jit(solution)/shard_map/pallas_call | solution.py:214
  607.2 2.1 select_bitcast_fusion.2
  609.7 3.4 dynamic-slice_select_fusion.2
  613.1 53.1 %all-reduce.21.cloned.1.call-done = f32[1,256,768]{2,1,0:T(8,128)} async-done(((f32[1,256,768]{2,1,0:T(8,128)}), f32[1,256,768]{2,1,0:T(8,128)}) %all-reduce.21.cloned.1.call-update) | async-done | bytes 786448 | tf_op jit(solution)/shard_map/psum | solution.py:45
  666.2 1.9 select_bitcast_fusion.5
  670.0 89.3 %all-reduce.31.cloned.1.call-done = (f32[1536,256]{1,0:T(8,128)}, f32[256,256]{1,0:T(8,128)}) async-done(((f32[1536,256]{1,0:T(8,128)}, f32[256,256]{1,0:T(8,128)}), (f32[1536,256]{1,0:T(8,128)}, f32[256,256]{1,0:T(8,128)})) %all-reduce.31.cloned.1.call-update) | async-done | bytes 1835024 | tf_op jit(solution)/shard_map/psum | solution.py:27
  759.3 2.6 gather_fusion.2
  767.7 4.7 convolution_subtract_fusion.2
  772.4 2.2 copy-done.2
  775.2 8.1 select_n.576
  783.4 2.1 select_bitcast_fusion.1
  785.6 3.1 dynamic-slice_select_fusion.1
  788.7 57.4 %all-reduce.23.cloned.1.call-done = f32[1,256,768]{2,1,0:T(8,128)} async-done(((f32[1,256,768]{2,1,0:T(8,128)}), f32[1,256,768]{2,1,0:T(8,128)}) %all-reduce.23.cloned.1.call-update) | async-done | bytes 786448 | tf_op jit(solution)/shard_map/psum | solution.py:45
  846.1 1.8 select_bitcast_fusion.4
  849.3 89.7 %all-reduce.29.cloned.1.call-done = (f32[1536,256]{1,0:T(8,128)}, f32[256,256]{1,0:T(8,128)}) async-done(((f32[1536,256]{1,0:T(8,128)}, f32[256,256]{1,0:T(8,128)}), (f32[1536,256]{1,0:T(8,128)}, f32[256,256]{1,0:T(8,128)})) %all-reduce.29.cloned.1.call-update) | async-done | bytes 1835024 | tf_op jit(solution)/shard_map/psum | solution.py:27
  939.0 2.6 gather_fusion.3
  947.4 4.7 convolution_subtract_fusion.1
  952.1 2.2 copy-done.3
  955.0 7.3 select_n.595
  962.3 2.1 select_bitcast_fusion
  964.7 3.1 dynamic-slice_select_fusion
  967.8 57.3 %all-reduce.25.cloned.1.call-done = f32[1,256,768]{2,1,0:T(8,128)} async-done(((f32[1,256,768]{2,1,0:T(8,128)}), f32[1,256,768]{2,1,0:T(8,128)}) %all-reduce.25.cloned.1.call-update) | async-done | bytes 786448 | tf_op jit(solution)/shard_map/psum | solution.py:45
  1025.1 1.8 select_bitcast_fusion.3
  1027.1 91.1 %all-reduce.27.cloned.1.call-done = (f32[1536,256]{1,0:T(8,128)}, f32[256,256]{1,0:T(8,128)}) async-done(((f32[1536,256]{1,0:T(8,128)}, f32[256,256]{1,0:T(8,128)}), (f32[1536,256]{1,0:T(8,128)}, f32[256,256]{1,0:T(8,128)})) %all-reduce.27.cloned.1.call-update) | async-done | bytes 1835024 | tf_op jit(solution)/shard_map/psum | solution.py:27
  1118.2 2.6 gather_fusion.4
  1126.5 4.7 convolution_subtract_fusion
  1131.3 2.2 copy-done.11
  1134.1 7.3 select_n.614
  (206 shorter events, 44.0 us)
Async XLA Ops:
  7.2 2.6 copy-start.21
  7.2 67.4 %all-reduce.17.cloned.1.call-start = ((), (), s32[]{:S(2)}) async-start(), calls=%async_computation | async-start | bytes 2097152 | tf_op jit(solution)/shard_map/psum | solution.py:45
  9.5 161.5 %all-reduce.35.cloned.1.call-start = ((), (), s32[]{:S(2)}) async-start(), calls=%async_computation.9 | async-start | bytes 4718592 | tf_op jit(solution)/shard_map/psum | solution.py:27
  76.5 171.9 %all-reduce.19.cloned.1.call-start = ((), (), s32[]{:S(2)}) async-start(), calls=%async_computation.1 | async-start | bytes 2097152 | tf_op jit(solution)/shard_map/psum | solution.py:45
  171.0 4.5 copy-start.7
  175.9 1.9 copy-start.13
  177.8 2.2 copy-start.10
  184.5 2.0 copy-start
  187.7 157.2 %all-reduce.33.cloned.1.call-start = ((), (), s32[]{:S(2)}) async-start(), calls=%async_computation.8 | async-start | bytes 4718592 | tf_op jit(solution)/shard_map/psum | solution.py:27
  190.8 59.6 %copy-start.20 = (s32[3]{0:T(128)S(1)}, s32[3]{0:T(128)}, u32[]{:S(2)}) copy-start(s32[3]{0:T(128)} %param.7) | copy-start | bytes 40
  250.2 416.0 %all-reduce.21.cloned.1.call-start = ((), (), s32[]{:S(2)}) async-start(), calls=%async_computation.2 | async-start | bytes 1572864 | tf_op jit(solution)/shard_map/psum | solution.py:45
  344.9 4.5 copy-start.5
  349.8 1.9 copy-start.12
  351.8 2.2 copy-start.1
  358.7 2.0 copy-start.4
  609.4 150.0 %all-reduce.31.cloned.1.call-start = ((), (), s32[]{:S(2)}) async-start(), calls=%async_computation.7 | async-start | bytes 3670016 | tf_op jit(solution)/shard_map/psum | solution.py:27
  609.7 158.0 %slice-start.4 = ((s8[4718592]{0:T(1024)(128)(4,1)}), s8[524288]{0:T(1024)(128)(4,1)S(1)}, s32[]{:S(2)}) async-start(s8[4718592]{0:T(1024)(128)(4,1)} %bitcast.151), calls=%async_computation.14 | async-start | bytes 1048576
  668.1 178.1 %all-reduce.23.cloned.1.call-start = ((), (), s32[]{:S(2)}) async-start(), calls=%async_computation.3 | async-start | bytes 1572864 | tf_op jit(solution)/shard_map/psum | solution.py:45
  759.3 4.5 copy-start.8
  763.4 2.8 copy-start.15
  763.8 3.8 slice-start.5
  765.8 1.9 copy-start.18
  772.4 2.2 copy-start.2
  785.5 153.5 %all-reduce.29.cloned.1.call-start = ((), (), s32[]{:S(2)}) async-start(), calls=%async_computation.6 | async-start | bytes 3670016 | tf_op jit(solution)/shard_map/psum | solution.py:27
  785.6 161.7 %slice-start = ((s8[4718592]{0:T(1024)(128)(4,1)}), s8[524288]{0:T(1024)(128)(4,1)S(1)}, s32[]{:S(2)}) async-start(s8[4718592]{0:T(1024)(128)(4,1)} %bitcast.145), calls=%async_computation.10 | async-start | bytes 1048576
  848.0 177.1 %all-reduce.25.cloned.1.call-start = ((), (), s32[]{:S(2)}) async-start(), calls=%async_computation.4 | async-start | bytes 1572864 | tf_op jit(solution)/shard_map/psum | solution.py:45
  939.0 4.5 copy-start.6
  943.1 2.8 copy-start.14
  943.5 3.8 slice-start.1
  945.5 1.9 copy-start.17
  952.1 2.2 copy-start.3
  964.4 153.8 %all-reduce.27.cloned.1.call-start = ((), (), s32[]{:S(2)}) async-start(), calls=%async_computation.5 | async-start | bytes 3670016 | tf_op jit(solution)/shard_map/psum | solution.py:27
  964.7 161.8 %slice-start.2 = ((s8[4718592]{0:T(1024)(128)(4,1)}), s8[524288]{0:T(1024)(128)(4,1)S(1)}, s32[]{:S(2)}) async-start(s8[4718592]{0:T(1024)(128)(4,1)} %bitcast.147), calls=%async_computation.12 | async-start | bytes 1048576
  1118.2 4.5 copy-start.9
  1122.3 2.8 copy-start.16
  1122.7 3.8 slice-start.3
  1124.7 1.9 copy-start.19
  1131.2 2.2 copy-start.11
Sparse Core Ops, SparseCore 0:
  10.9 63.6 all-reduce.16
  78.7 92.3 all-reduce.34
  187.8 60.4 all-reduce.18
  252.7 92.2 all-reduce.32
  609.5 56.6 all-reduce.20
  669.9 89.4 all-reduce.30
  785.6 60.4 all-reduce.22
  849.6 89.4 all-reduce.28
  964.5 60.4 all-reduce.24
  1028.7 89.4 all-reduce.26

commit v2 on v1

v2 whole, which is shorter than its diff:
```python
import functools

import jax
import jax.numpy as jnp
from jax import lax
from jax.experimental import pallas as pl
from jax.experimental.pallas import tpu as pltpu
from jax.sharding import Mesh
from jax.sharding import PartitionSpec as P

PANEL = 256
BLK = 128
CPAN = 2
RPAN = 3

ROW = ("y", "core")
COL = ("x", "z")
MESH = pl.DeviceIdType.MESH
NEVER = 99

HIGH = lax.Precision.HIGH
HIGHEST = lax.Precision.HIGHEST


def peers_of(axes):
    y, core = lax.axis_index("y"), lax.axis_index("core")
    if axes == ROW:
        return 2 * y + core, 8, lambda p: {"y": p // 2, "core": lax.rem(p, 2)}
    if axes == "child":
        pair = y // 2 * 2
        me = lax.rem(y, 2) * 2 + core
        return me, 4, lambda p: {"y": pair + p // 2, "core": lax.rem(p, 2)}
    return lax.axis_index(axes), 4, lambda p: {axes: p}


def swap(array, axes):
    return (array, axes, lambda ref, p: ref.at[p], lambda ref, p: ref.at[p], array.shape)


def swap_inner(array, axes):
    shape = (array.shape[1], array.shape[0]) + array.shape[2:]
    return (array, axes, lambda ref, p: ref.at[:, p], lambda ref, p: ref.at[p], shape)


def swap_half(array, axes, half):
    return (
        array, axes, lambda ref, p: ref.at[half, p], lambda ref, p: ref.at[p], array.shape[1:]
    )


def share(array, axes, size):
    return (array, axes, lambda ref, p: ref, lambda ref, p: ref.at[p], (size,) + array.shape)


def share_inner(array, axes, size):
    shape = (array.shape[0], size) + array.shape[1:]
    return (array, axes, lambda ref, p: ref, lambda ref, p: ref.at[:, p], shape)


def exchange(moves, collective_id):
    n = len(moves)
    greeted = list(dict.fromkeys(m[1] for m in moves))

    def kernel(*refs):
        ins, outs = refs[:n], refs[n : 2 * n]
        send_sem, recv_sem, own_sem = refs[2 * n :]
        barrier = pltpu.get_barrier_semaphore()
        total = 0
        for ax in greeted:
            me, size, ident = peers_of(ax)
            for d in range(1, size):
                pl.semaphore_signal(
                    barrier, inc=1, device_id=ident(lax.rem(me + d, size)), device_id_type=MESH
                )
            total += size - 1
        own = []
        for i, (_, ax, src, dst, _) in enumerate(moves):
            me = peers_of(ax)[0]
            copy = pltpu.make_async_copy(src(ins[i], me), dst(outs[i], me), own_sem.at[i])
            copy.start()
            own.append(copy)
        pl.semaphore_wait(barrier, total)
        copies = []
        for i, (_, ax, src, dst, _) in enumerate(moves):
            me, size, ident = peers_of(ax)
            for d in sorted(range(1, size), key=lambda d: -min(d, size - d)):
                p = lax.rem(me + d, size)
                copy = pltpu.make_async_remote_copy(
                    src_ref=src(ins[i], p),
                    dst_ref=dst(outs[i], me),
                    send_sem=send_sem.at[i, d],
                    recv_sem=recv_sem.at[i, d],
                    device_id=ident(p),
                    device_id_type=MESH,
                )
                copy.start()
                copies.append(copy)
        for copy in own + copies:
            copy.wait()

    return pl.pallas_call(
        kernel,
        out_shape=[jax.ShapeDtypeStruct(m[4], jnp.float32) for m in moves],
        in_specs=[pl.BlockSpec(memory_space=pl.ANY)] * n,
        out_specs=[pl.BlockSpec(memory_space=pl.ANY)] * n,
        scratch_shapes=[
            pltpu.SemaphoreType.DMA((n, 8)),
            pltpu.SemaphoreType.DMA((n, 8)),
            pltpu.SemaphoreType.DMA((n,)),
        ],
        compiler_params=pltpu.CompilerParams(collective_id=collective_id, has_side_effects=True),
    )(*[m[0] for m in moves])


def rank_in(key, group, valid):
    n = key.shape[1]
    earlier = jnp.arange(n)[None, :] < jnp.arange(n)[:, None]
    same = (key[:, :, None] == key[:, None, :]) & (group[:, None] == group[None, :])[None]
    return jnp.sum((same & valid[:, None, :] & earlier[None]).astype(jnp.int32), axis=2)


def find(match, value):
    return jnp.sum(jnp.where(match, value + 1, 0), axis=-1) - 1


def routes(child_map):
    y, core = lax.axis_index("y"), lax.axis_index("core")
    x, z = lax.axis_index("x"), lax.axis_index("z")
    my_child, within = y // 2, lax.rem(y, 2) * 2 + core
    r, o = 2 * y + core, 4 * x + z
    blocks = jnp.arange(64)
    skip = CPAN * PANEL // BLK
    cyclic = (child_map % 6) * 16 + child_map // 6
    t = jnp.concatenate([jnp.zeros((2, skip), jnp.int32), cyclic], axis=1)
    valid = jnp.broadcast_to(blocks >= skip, (2, 64))
    kz = rank_in(t % 4, blocks // 4, valid)
    kx = rank_in(t % 16, blocks // 16, valid)
    kr = rank_in(t % 16 // 2, blocks // 16, valid)
    four, two = jnp.arange(4), jnp.arange(2)

    mine = valid & (blocks // 4 == o)[None]
    z_pick = find(
        mine[:, None, None]
        & ((t % 4)[:, None, None] == four[None, :, None, None])
        & (kz[:, None, None] == two[None, None, :, None]),
        blocks % 4,
    )
    mine = valid & (blocks // 16 == x)[None] & (t % 4 == z)
    x_pick = find(
        mine[:, None, None]
        & ((t % 16 // 4)[:, None, None] == four[None, :, None, None])
        & (kx[:, None, None] == two[None, None, :, None]),
        ((blocks // 4 % 4)[None] * 2 + kz)[:, None, None],
    )
    slots = jnp.arange(6)
    col_from = find(
        valid[:, None] & (t[:, None] == (slots * 16 + o)[None, :, None]),
        ((blocks // 16)[None] * 2 + kx)[:, None],
    )
    mine = valid & (blocks // 16 == within)[None]
    own = lambda a: lax.dynamic_index_in_dim(a, my_child, 0, keepdims=False)
    r_pick = find(
        own(mine)[None, None]
        & (own(t % 16 // 2)[None, None] == jnp.arange(8)[:, None, None])
        & (own(kr)[None, None] == four[None, :, None]),
        blocks % 16,
    )
    slots = jnp.arange(12)
    row_from = find(
        valid[:, None] & (t[:, None] == (slots % 6 * 16 + 2 * r + slots // 6)[None, :, None]),
        ((jnp.arange(2)[:, None] * 4 + (blocks // 16)[None]) * 4 + kr)[:, None],
    )
    return own(z_pick), z_pick, x_pick, own(x_pick), col_from, own(col_from), r_pick, row_from


Z_OWN, Z_PICK, X_PICK, X_OWN, COL_FROM, COL_OWN, R_PICK, ROW_FROM = 0, 8, 24, 40, 48, 60, 66, 98


def whole(shape):
    return pl.BlockSpec(shape, lambda g, tab: (0,) * len(shape))


def part(shape):
    return pl.BlockSpec((1,) + shape, lambda g, tab: (g,) + (0,) * len(shape))


def local_call(kernel, grid, table, operands, in_specs, out_shapes, out_specs, scratch=()):
    return pl.pallas_call(
        kernel,
        grid_spec=pltpu.PrefetchScalarGridSpec(
            num_scalar_prefetch=1, grid=(grid,), in_specs=in_specs, out_specs=out_specs,
            scratch_shapes=list(scratch),
        ),
        out_shape=[jax.ShapeDtypeStruct(s, jnp.float32) for s in out_shapes],
        compiler_params=pltpu.CompilerParams(vmem_limit_bytes=56 * 1024 * 1024),
    )(table, *operands)


def at_least_zero(v):
    return jnp.maximum(v, 0)


def lanes(block):
    return pl.ds(pl.multiple_of(block * BLK, BLK), BLK)


def pack_first(tab, front, za, yb):
    g = pl.program_id(0)
    za[0] = front[:, 0:64, lanes(at_least_zero(tab[Z_OWN + g]))]
    for k in range(4):
        yb[0, k] = front[at_least_zero(tab[R_PICK + g * 4 + k]), 64:128, :]


def pack_second(tab, zin, yin, xa, zb):
    g = pl.program_id(0)
    xa[0] = zin[at_least_zero(tab[X_OWN + g])]
    for c in range(2):
        column = lanes(at_least_zero(tab[Z_PICK + c * 8 + g]))
        for i in range(12):
            source = at_least_zero(tab[ROW_FROM + c * 12 + i])
            zb[0, c * 12 + i] = yin[source, :, column]


def pack_third(tab, xin, zin, ya, xb):
    g = pl.program_id(0)
    for c in range(2):
        source = at_least_zero(tab[X_PICK + c * 8 + g])
        xb[0, c * 12 : c * 12 + 12] = zin[source, c * 12 : c * 12 + 12]
    for k in range(4):
        i = at_least_zero(tab[R_PICK + g * 4 + k])
        for slot in range(6):
            source = at_least_zero(tab[COL_OWN + slot])
            ya[0, k, :, slot * BLK : slot * BLK + BLK] = xin[source, i]


def add_all(tab, root, yin, xin, out):
    i = pl.program_id(0)
    for slot in range(6):
        columns = slice(slot * BLK, slot * BLK + BLK)
        upper, lower = root[0, 0:64, columns], root[0, 64:128, columns]
        for c in range(2):
            row, col = tab[ROW_FROM + c * 12 + i], tab[COL_FROM + c * 6 + slot]
            there = jnp.logical_and(row >= 0, col >= 0)
            upper += jnp.where(there, yin[at_least_zero(row), :, columns], 0.0)
            lower += jnp.where(there, xin[at_least_zero(col), c * 12 + i], 0.0)
        out[0, 0:64, columns] = upper
        out[0, 64:128, columns] = lower


def extend_add(factored, root_front, child_map):
    table = jnp.concatenate([a.reshape(-1) for a in routes(child_map)])
    front = factored.reshape(16, BLK, 512)
    za, yb = local_call(
        pack_first, 8, table, (front,), [whole((16, BLK, 512))],
        [(8, 16, 64, BLK), (8, 4, 64, 512)], [part((16, 64, BLK)), part((4, 64, 512))],
    )
    za, yb = exchange([swap(za.reshape(4, 2, 16, 64, BLK), "z"), swap(yb, ROW)], 1)
    xa, zb = local_call(
        pack_second, 8, table, (za.reshape(8, 16, 64, BLK), yb.reshape(32, 64, 512)),
        [whole((8, 16, 64, BLK)), whole((32, 64, 512))],
        [(8, 16, 64, BLK), (8, 24, 64, BLK)], [part((16, 64, BLK)), part((24, 64, BLK))],
    )
    xa, zb = exchange(
        [swap(xa.reshape(4, 2, 16, 64, BLK), "x"), swap(zb.reshape(4, 2, 24, 64, BLK), "z")], 2
    )
    ya, xb = local_call(
        pack_third, 8, table, (xa.reshape(8, 16, 64, BLK), zb.reshape(8, 24, 64, BLK)),
        [whole((8, 16, 64, BLK)), whole((8, 24, 64, BLK))],
        [(8, 4, 64, 768), (8, 24, 64, BLK)], [part((4, 64, 768)), part((24, 64, BLK))],
    )
    ya, xb = exchange([swap(ya, ROW), swap(xb.reshape(4, 2, 24, 64, BLK), "x")], 3)
    (assembled,) = local_call(
        add_all, 12, table,
        (root_front.reshape(12, BLK, 768), ya.reshape(32, 64, 768), xb.reshape(8, 24, 64, BLK)),
        [part((BLK, 768)), whole((32, 64, 768)), whole((8, 24, 64, BLK))],
        [(12, BLK, 768)], [part((BLK, 768))],
    )
    return assembled.reshape(root_front.shape)


def pick(arrived, owners):
    parts = [
        lax.dynamic_index_in_dim(arrived[..., q * PANEL : (q + 1) * PANEL], owner, 0, keepdims=False)
        for q, owner in enumerate(owners)
    ]
    return jnp.concatenate(parts, axis=-1)


def gather_bands(cols, rows, col_off, xs, zs, row_owners, axes, size, first_id):
    count, width = cols.shape
    panels, _, span = rows.shape
    piece = PANEL // size
    cols = cols.reshape(2, 4, count // 8, width)
    rows = rows.reshape(panels, size, piece, span)
    first, second, slices = exchange(
        [swap_half(cols, "z", 0), swap_half(cols, "x", 1), swap_inner(rows, axes)], first_id
    )
    first, second = pick(first, zs), pick(second, xs)
    slices = jnp.stack(
        [lax.dynamic_index_in_dim(slices[:, k], owner, 0, keepdims=False) for k, owner in enumerate(row_owners)]
    )
    cross = jnp.concatenate(
        [lax.dynamic_slice_in_dim(slices, off, PANEL, 2) for off in col_off], axis=2
    )
    split = lambda a: a.reshape(4, count // 32, width)
    half = span // 2
    first, second, cross, left = exchange(
        [
            swap(split(first), "x"), swap(split(second), "z"), share(cross, "z", 4),
            share_inner(slices[..., :half], axes, size),
        ],
        first_id + 1,
    )
    first, second, cross = pick(first, xs), pick(second, zs), pick(cross, zs)
    first, second, cross, right = exchange(
        [
            share(first, "x", 4), share(second, "z", 4), share(cross, "x", 4),
            share_inner(slices[..., half:], axes, size),
        ],
        first_id + 2,
    )
    cross = pick(cross, xs)
    join = lambda a: a.reshape(count // 8, width)
    first, second, cross = exchange(
        [share(join(first), "z", 4), share(join(second), "x", 4), share_inner(cross, axes, size)],
        first_id + 3,
    )
    halves = [a.reshape(count // 2, width) for a in (first, second)]
    left, right = (a.reshape(width, half) for a in (left, right))
    return halves, left, right, cross.reshape(width, width)


def dot(a, b, precision=HIGH):
    return jnp.dot(a, b, precision=precision, preferred_element_type=jnp.float32)


def newton(block):
    shape = (PANEL, PANEL)
    eye = lax.broadcasted_iota(jnp.int32, shape, 0) == lax.broadcasted_iota(jnp.int32, shape, 1)
    kept = jnp.where(eye, block, 0.0)
    by_col = 1.0 / jnp.sum(kept, axis=0, keepdims=True)
    by_row = 1.0 / jnp.sum(kept, axis=1, keepdims=True)
    identity = jnp.where(eye, 1.0, 0.0)
    error = identity - block * by_col
    product = identity + error
    for _ in range(3):
        error = dot(error, error, HIGHEST)
        product = product + dot(product, error, HIGHEST)
    return product * by_row


def panel(k):
    return slice(k * PANEL, (k + 1) * PANEL)


def finish_kernel(n, row_panels, col_panels, precision, tab, front, upper, lower, left, right, cross, out,
                  work, inverse, pivots):
    g = pl.program_id(0)

    @pl.when(g == 0)
    def _():
        work[...] = cross[...]
        span = left.shape[1]
        pivots[:, :span] = left[...]
        pivots[:, span:] = right[...]
        for k in range(n):
            inverse[k] = newton(work[panel(k), panel(k)])
            for p in range(k + 1, n):
                factor = dot(work[panel(p), panel(k)], inverse[k], HIGHEST)
                for q in range(k + 1, n):
                    work[panel(p), panel(q)] -= dot(factor, work[panel(k), panel(q)], HIGHEST)
                pivots[panel(p), :] -= dot(factor, pivots[panel(k), :], HIGHEST)
        for j in range(col_panels):
            for k in range(n):
                pivots[panel(k), panel(j)] = jnp.where(
                    tab[row_panels + j] > k, pivots[panel(k), panel(j)], 0.0
                )

    mine = jnp.where(g < row_panels // 2, upper[...], lower[...])
    band = [mine[:, panel(k)] for k in range(n)]
    for k in range(n):
        band[k] = dot(band[k], inverse[k], HIGHEST)
        for q in range(k + 1, n):
            band[q] = band[q] - dot(band[k], work[panel(k), panel(q)], HIGHEST)
    band = [jnp.where(tab[g] > k, band[k], 0.0) for k in range(n)]
    factors = jnp.concatenate(band, axis=1)
    for j in range(col_panels):
        new = front[:, panel(j)] - dot(factors, pivots[:, panel(j)], precision)
        for k in range(n):
            here = jnp.logical_and(tab[row_panels + j] == k, tab[g] > k)
            new = jnp.where(here, band[k], new)
        out[:, panel(j)] = new


def finish(front, halves, left, right, cross, row_step, col_step, precision):
    rows, cols = front.shape
    width = cross.shape[0]
    n, row_panels, col_panels = width // PANEL, rows // PANEL, cols // PANEL
    half = row_panels // 2
    keep = lambda shape: pl.BlockSpec(shape, lambda g, tab: (0, 0))
    (out,) = local_call(
        functools.partial(finish_kernel, n, row_panels, col_panels, precision),
        row_panels,
        jnp.concatenate([row_step, col_step]).astype(jnp.int32),
        (front, *halves, left, right, cross),
        [
            pl.BlockSpec((PANEL, cols), lambda g, tab: (g, 0)),
            pl.BlockSpec((PANEL, width), lambda g, tab: (jnp.minimum(g, half - 1), 0)),
            pl.BlockSpec((PANEL, width), lambda g, tab: (jnp.maximum(g - half, 0), 0)),
            keep(left.shape), keep(right.shape), keep(cross.shape),
        ],
        [front.shape],
        [pl.BlockSpec((PANEL, cols), lambda g, tab: (g, 0))],
        scratch=[
            pltpu.VMEM((width, width), jnp.float32),
            pltpu.VMEM((n, PANEL, PANEL), jnp.float32),
            pltpu.VMEM((width, cols), jnp.float32),
        ],
    )
    return out


def body(child_fronts, root_front, child_map, panel_order):
    y, core = lax.axis_index("y"), lax.axis_index("core")
    r, o = 2 * y + core, 4 * lax.axis_index("x") + lax.axis_index("z")
    within = lax.rem(y, 2) * 2 + core

    zeros = [0] * CPAN
    bands = gather_bands(
        child_fronts, child_fronts[: CPAN * PANEL].reshape(CPAN, PANEL, -1),
        [k * PANEL for k in range(CPAN)], zeros, zeros, zeros, "child", 4, 10,
    )
    row_panel, col_panel = within * 8 + jnp.arange(8), o * 2 + jnp.arange(2)
    row_step = jnp.where(row_panel < CPAN, row_panel, NEVER)
    col_step = jnp.where(col_panel < CPAN, col_panel, NEVER)
    halves, left, right, cross = bands
    factored = finish(child_fronts, halves, left, right, cross, row_step, col_step, HIGHEST)

    assembled = extend_add(factored, root_front, child_map)

    row_panels, col_panels = 6, 3
    order = [panel_order[k] for k in range(RPAN)]
    col_off = [p % col_panels * PANEL for p in order]
    row_off = [p % row_panels * PANEL for p in order]
    owner = [p // col_panels for p in order]
    cols = jnp.concatenate([lax.dynamic_slice_in_dim(assembled, off, PANEL, 1) for off in col_off], 1)
    rows = jnp.stack([lax.dynamic_slice_in_dim(assembled, off, PANEL, 0) for off in row_off])
    halves, left, right, cross = gather_bands(
        cols, rows, col_off, [c // 4 for c in owner], [c % 4 for c in owner],
        [p // row_panels for p in order], ROW, 8, 20,
    )

    def steps(places):
        match = places[:, None] == panel_order[None, :]
        return jnp.min(jnp.where(match, jnp.arange(RPAN)[None, :], NEVER), axis=1)

    row_step = steps(r * row_panels + jnp.arange(row_panels))
    col_step = steps(o * col_panels + jnp.arange(col_panels))
    return factored, finish(assembled, halves, left, right, cross, row_step, col_step, HIGH)


def solution(mesh):
    grid = Mesh(mesh.devices.reshape(4, 2, 4, 4), ("y", "core", "x", "z"))
    return jax.shard_map(
        body,
        mesh=grid,
        in_specs=(P(ROW, COL), P(ROW, COL), P(), P()),
        out_specs=(P(ROW, COL), P(ROW, COL)),
        check_vma=False,
    )
```

time: 1160 us -> 642 us (0.55)
  waiting for transfers between devices: 741 us -> 0 us
  Pallas kernels: 246 us -> 580 us
  matrix products: 50.3 us -> 0 us
  other arithmetic: 39.6 us -> 18.7 us
  local copies, waits for them, and re-layouts: 52.2 us -> 31.7 us
    psum x10 -> x0, waiting for transfers between devices: 741 us -> none  [the longest x5 454 us: broadcast(): return lax.psum(block, axis)]
    pallas_call x3 -> x11, Pallas kernels: 206 us -> 476 us  [exchange(): pl.pallas_call(kernel, out_shape=[jax.ShapeDtypeStruct(m[4], jnp.float32)...]
    pallas_call x4 -> x6, Pallas kernels: 40.5 us -> 103 us  [local_call(): pl.pallas_call(kernel, grid_spec=pltpu.PrefetchScalarGridSpec(num_scalar_...]
    dot_general x50 -> x0, matrix products: 50.3 us -> none  [the longest x5 21.8 us: apply_update(): updated = row_band - jnp.dot(factor_part, factor_rows, precision=highest)]
    select_n x19 -> x3, other arithmetic: 27.3 us -> 0.01 us  [the longest x1 0.01 us: body(): col_step = jnp.where(col_panel < CPAN, col_panel, NEVER)]
    select_n x3 -> x0, local copies, waits for them, and re-layouts: 22.8 us -> none  [apply_update(): return jnp.where(plan_entry['col_mine'], rewritten, updated)]
    concatenate x1 -> x16, other arithmetic: 0.01 us -> 13.5 us  [the longest x12 9.02 us: pick(): return jnp.concatenate(parts, axis=-1)]
    gather x5 -> x0, local copies, waits for them, and re-layouts: 13.2 us -> none  [newton(): inverse = jnp.diag(1.0 / jnp.diagonal(pivot_block))]
  transfers between devices with their start and end apart: 10 -> 0, of which waited for: 10 -> 0; matrix products, arithmetic and copies ran while one was open for 2% -> 0% of each run, Pallas kernels for 0% -> 0%
where the time goes in v2:
time: 642 us; the launch traced here: 641 us
  Pallas kernels  580 us (90%)
  local copies, waits for them, and re-layouts  31.7 us (5%)
  other arithmetic  18.7 us (3%)
  between operations  10.6 us (2%)
    pallas_call x11, Pallas kernels, exchange(): pl.pallas_call(kernel, out_shape=[jax.ShapeDtypeStruct(m[4], jnp.float32)...  476 us
    pallas_call x6, Pallas kernels, local_call(): pl.pallas_call(kernel, grid_spec=pltpu.PrefetchScalarGridSpec(num_scalar_...  103 us

profile of v2, /device:TPU:1, one launch (start us, length us, event | category | flops | bytes accessed | tf_op | source)
XLA Modules:
  0.0 640.6 jit_solution(117019477630985255)
XLA Ops:
  1.2 2.3 slice.126
  3.5 41.3 %shard_map.59 = (f32[4,256,512]{2,1,0:T(8,128)}, f32[4,256,512]{2,1,0:T(8,128)}, f32[4,2,64,512]{3,2,1,0:T(8,128)}) custom-call(f32[2,4,256,512]{3,2,1,0:T(8,128)} %bitcast.115, f32[2,4,256,512]{3,2,1,0:T(8,128)} %bitcast.116, f32[2,4,64,512]{3,2,1,0:T(8,128)} %bitcast.126), custom_call_target="tpu_custom_call" | custom-call | tf_op jit(solution)/shard_map/pallas_call | solution.py:101
  44.8 1.3 fusion.22
  46.1 0.9 pad_maximum_fusion.4.refs_0_
  46.9 0.9 pad_maximum_fusion.5.refs_1_
  47.8 1.0 slice_bitcast_fusion.5
  50.2 26.1 %shard_map.60 = (f32[4,64,512]{2,1,0:T(8,128)}, f32[4,64,512]{2,1,0:T(8,128)}, f32[4,2,64,512]{3,2,1,0:T(8,128)}, f32[2,4,64,256]{3,2,1,0:T(8,128)}) custom-call(f32[4,64,512]{2,1,0:T(8,128)} %pad_maximum_fusion.4.refs_0_, f32[4,64,512]{2,1,0:T(8,128)} %pad_maximum_fusion.5.refs_1_, f32[2,64,512]{2,1,0:T(8,128)} %pad_maximum_fusion.6.refs_2_, ...), custom_call_target="tpu_custom_call" | custom-call | tf_op jit(solution)/shard_map/pallas_call | solution.py:101
  76.3 0.9 slice_bitcast_fusion.9
  77.9 0.9 slice_bitcast_fusion.7
  79.4 1.0 slice_bitcast_fusion.3
  81.1 21.6 %shard_map.61 = (f32[4,64,512]{2,1,0:T(8,128)}, f32[4,64,512]{2,1,0:T(8,128)}, f32[4,2,64,512]{3,2,1,0:T(8,128)}, f32[2,4,64,256]{3,2,1,0:T(8,128)}) custom-call(f32[64,512]{1,0:T(8,128)} %pad_maximum_fusion.15.refs_0_, f32[64,512]{1,0:T(8,128)} %pad_maximum_fusion.16.refs_1_, f32[2,64,512]{2,1,0:T(8,128)} %pad_maximum_fusion.11.refs_2_, ...), custom_call_target="tpu_custom_call" | custom-call | tf_op jit(solution)/shard_map/pallas_call | solution.py:101
  102.7 1.0 slice_bitcast_fusion.1
  104.5 41.3 %shard_map.62 = (f32[4,256,512]{2,1,0:T(8,128)}, f32[4,256,512]{2,1,0:T(8,128)}, f32[2,4,64,512]{3,2,1,0:T(8,128)}) custom-call(f32[256,512]{1,0:T(8,128)} %bitcast.157, f32[256,512]{1,0:T(8,128)} %bitcast.158, f32[2,64,512]{2,1,0:T(8,128)} %pad_maximum_fusion.12.refs_2_), custom_call_target="tpu_custom_call" | custom-call | tf_op jit(solution)/shard_map/pallas_call | solution.py:101
  145.8 27.3 %shard_map.63 = f32[2048,512]{1,0:T(8,128)} custom-call(s32[10]{0:T(128)} %pad_add_fusion.tab, f32[2048,512]{1,0:T(8,128)} %front.1, f32[1024,512]{1,0:T(8,128)} %bitcast.138, f32[1024,512]{1,0:T(8,128)} %bitcast.139, f32[512,256]{1,0:T(8,128)} %bitcast.155, f32[512,256]{1,0:T(8,128)} %bitcast.156, f32[512,512]{1,0:T(8,128)} %bitcast.142), custom_call_target="tpu_custom_call" | custom-call | tf_op jit(solution)/shard_map/pallas_call | solution.py:188
  178.1 7.4 %shard_map.64 = (f32[8,16,64,128]{3,2,1,0:T(8,128)}, f32[8,4,64,512]{3,2,1,0:T(8,128)}) custom-call(s32[122]{0:T(128)} %concatenate.93.tab, f32[16,128,512]{2,1,0:T(8,128)} %bitcast.119), custom_call_target="tpu_custom_call" | custom-call | tf_op jit(solution)/shard_map/pallas_call | solution.py:188
  185.6 51.5 %shard_map.65 = (f32[4,2,16,64,128]{4,3,2,1,0:T(8,128)}, f32[8,4,64,512]{3,2,1,0:T(8,128)}) custom-call(f32[4,2,16,64,128]{4,3,2,1,0:T(8,128)} %bitcast.131, f32[8,4,64,512]{3,2,1,0:T(8,128)} %get-tuple-element.57.refs_1_), custom_call_target="tpu_custom_call" | custom-call | tf_op jit(solution)/shard_map/pallas_call | solution.py:101
  237.0 9.4 %shard_map.66 = (f32[8,16,64,128]{3,2,1,0:T(8,128)}, f32[8,24,64,128]{3,2,1,0:T(8,128)}) custom-call(s32[122]{0:T(128)} %concatenate.93.tab, f32[8,16,64,128]{3,2,1,0:T(8,128)} %bitcast.127, f32[32,64,512]{2,1,0:T(8,128)} %bitcast.128), custom_call_target="tpu_custom_call" | custom-call | tf_op jit(solution)/shard_map/pallas_call | solution.py:188
  246.4 80.8 %shard_map.67 = (f32[4,2,16,64,128]{4,3,2,1,0:T(8,128)}, f32[4,2,24,64,128]{4,3,2,1,0:T(8,128)}) custom-call(f32[4,2,16,64,128]{4,3,2,1,0:T(8,128)} %bitcast.129, f32[4,2,24,64,128]{4,3,2,1,0:T(8,128)} %bitcast.120), custom_call_target="tpu_custom_call" | custom-call | tf_op jit(solution)/shard_map/pallas_call | solution.py:101
  327.2 10.4 %shard_map.68 = (f32[8,4,64,768]{3,2,1,0:T(8,128)}, f32[8,24,64,128]{3,2,1,0:T(8,128)}) custom-call(s32[122]{0:T(128)} %concatenate.93.tab, f32[8,16,64,128]{3,2,1,0:T(8,128)} %bitcast.130, f32[8,24,64,128]{3,2,1,0:T(8,128)} %bitcast.122), custom_call_target="tpu_custom_call" | custom-call | tf_op jit(solution)/shard_map/pallas_call | solution.py:188
  337.6 72.9 %shard_map.69 = (f32[8,4,64,768]{3,2,1,0:T(8,128)}, f32[4,2,24,64,128]{4,3,2,1,0:T(8,128)}) custom-call(f32[8,4,64,768]{3,2,1,0:T(8,128)} %get-tuple-element.64.refs_0_, f32[4,2,24,64,128]{4,3,2,1,0:T(8,128)} %bitcast.121), custom_call_target="tpu_custom_call" | custom-call | tf_op jit(solution)/shard_map/pallas_call | solution.py:101
  410.6 13.3 %shard_map.70 = f32[12,128,768]{2,1,0:T(8,128)} custom-call(s32[122]{0:T(128)} %concatenate.93.tab, f32[12,128,768]{2,1,0:T(8,128)} %bitcast.125, f32[32,64,768]{2,1,0:T(8,128)} %bitcast.123, f32[8,24,64,128]{3,2,1,0:T(8,128)} %bitcast.124), custom_call_target="tpu_custom_call" | custom-call | tf_op jit(solution)/shard_map/pallas_call | solution.py:188
  426.3 2.7 constant_dynamic-slice_fusion.14
  429.0 2.5 pad_maximum_fusion
  433.3 1.8 constant_dynamic-slice_fusion.11
  435.1 1.6 pad_maximum_fusion.1.refs_2_
  436.7 46.3 %shard_map.71 = (f32[4,192,768]{2,1,0:T(8,128)}, f32[4,192,768]{2,1,0:T(8,128)}, f32[8,3,32,768]{3,2,1,0:T(8,128)}) custom-call(f32[2,4,192,768]{3,2,1,0:T(8,128)} %bitcast.117, f32[2,4,192,768]{3,2,1,0:T(8,128)} %bitcast.118, f32[3,8,32,768]{3,2,1,0:T(8,128)} %pad_maximum_fusion.1.refs_2_), custom_call_target="tpu_custom_call" | custom-call | tf_op jit(solution)/shard_map/pallas_call | solution.py:101
  483.0 3.0 fusion.21
  487.3 0.9 constant_dynamic-slice_fusion.6
  489.6 0.9 constant_dynamic-slice_fusion.7
  491.7 0.9 pad_maximum_fusion.2.refs_0_
  492.6 1.4 fusion.20
  493.9 1.1 constant_dynamic-slice_fusion.3
  495.1 0.9 constant_dynamic-slice_fusion.4
  496.1 0.9 pad_maximum_fusion.3.refs_1_
  496.9 1.4 fusion.19
  498.9 0.9 dynamic-slice_bitcast_fusion.6
  500.5 0.9 dynamic-slice_bitcast_fusion.7
  502.0 0.7 pad_maximum_fusion.8.refs_2_
  502.8 0.7 fusion.28
  503.5 24.1 %shard_map.72 = (f32[4,48,768]{2,1,0:T(8,128)}, f32[4,48,768]{2,1,0:T(8,128)}, f32[4,3,32,768]{3,2,1,0:T(8,128)}, f32[3,8,32,384]{3,2,1,0:T(8,128)}) custom-call(f32[4,48,768]{2,1,0:T(8,128)} %pad_maximum_fusion.2.refs_0_, f32[4,48,768]{2,1,0:T(8,128)} %pad_maximum_fusion.3.refs_1_, f32[3,32,768]{2,1,0:T(8,128)} %pad_maximum_fusion.8.refs_2_, ...), custom_call_target="tpu_custom_call" | custom-call | tf_op jit(solution)/shard_map/pallas_call | solution.py:101
  527.6 1.3 fusion.27
  529.6 1.2 fusion.26
  531.7 0.7 pad_maximum_fusion.9.refs_2_
  532.4 24.2 %shard_map.73 = (f32[4,48,768]{2,1,0:T(8,128)}, f32[4,48,768]{2,1,0:T(8,128)}, f32[4,3,32,768]{3,2,1,0:T(8,128)}, f32[3,8,32,384]{3,2,1,0:T(8,128)}) custom-call(f32[48,768]{1,0:T(8,128)} %pad_maximum_fusion.13.refs_0_, f32[48,768]{1,0:T(8,128)} %pad_maximum_fusion.14.refs_1_, f32[3,32,768]{2,1,0:T(8,128)} %pad_maximum_fusion.9.refs_2_, ...), custom_call_target="tpu_custom_call" | custom-call | tf_op jit(solution)/shard_map/pallas_call | solution.py:101
  556.7 1.4 fusion.24
  558.1 0.7 pad_maximum_fusion.10.refs_2_
  558.9 46.3 %shard_map.74 = (f32[4,192,768]{2,1,0:T(8,128)}, f32[4,192,768]{2,1,0:T(8,128)}, f32[3,8,32,768]{3,2,1,0:T(8,128)}) custom-call(f32[192,768]{1,0:T(8,128)} %bitcast.153, f32[192,768]{1,0:T(8,128)} %bitcast.154, f32[3,32,768]{2,1,0:T(8,128)} %pad_maximum_fusion.10.refs_2_), custom_call_target="tpu_custom_call" | custom-call | tf_op jit(solution)/shard_map/pallas_call | solution.py:101
  605.1 35.4 %shard_map.75 = f32[1536,768]{1,0:T(8,128)} custom-call(s32[9]{0:T(128)} %pad_add_fusion.1.tab, f32[1536,768]{1,0:T(8,128)} %bitcast.114, f32[768,768]{1,0:T(8,128)} %bitcast.135, f32[768,768]{1,0:T(8,128)} %bitcast.136, f32[768,384]{1,0:T(8,128)} %bitcast.140, f32[768,384]{1,0:T(8,128)} %bitcast.141, f32[768,768]{1,0:T(8,128)} %bitcast.137), custom_call_target="tpu_custom_call" | custom-call | tf_op jit(solution)/shard_map/pallas_call | solution.py:188
  (102 shorter events, 12.0 us)
Async XLA Ops:
  145.8 27.3 %copy-start.3 = (s32[3]{0:T(128)S(1)}, s32[3]{0:T(128)}, u32[]{:S(2)}) copy-start(s32[3]{0:T(128)} %param.7) | copy-start | bytes 40
  145.8 28.3 %copy-start.4 = (s32[2,60]{1,0:T(2,128)S(1)}, s32[2,60]{1,0:T(2,128)}, u32[]{:S(2)}) copy-start(s32[2,60]{1,0:T(2,128)} %param.6) | copy-start | bytes 1444
  486.0 6.6 %copy-start.1 = (f32[4,192,768]{2,1,0:T(8,128)S(1)}, f32[4,192,768]{2,1,0:T(8,128)}, u32[]{:S(2)}) copy-start(f32[4,192,768]{2,1,0:T(8,128)} %get-tuple-element.69) | copy-start | bytes 7077892
  493.9 3.0 copy-start
  527.6 3.9 copy-start.2

commit v3 on v2

--- a/solution.py
+++ b/solution.py
@@ -34,27 +34,30 @@
 
 
 def swap(array, axes):
-    return (array, axes, lambda ref, p: ref.at[p], lambda ref, p: ref.at[p], array.shape)
+    return (array, axes, lambda ref, p: ref.at[p], lambda ref, p: ref.at[p], array.shape, array.shape[1:])
 
 
 def swap_inner(array, axes):
     shape = (array.shape[1], array.shape[0]) + array.shape[2:]
-    return (array, axes, lambda ref, p: ref.at[:, p], lambda ref, p: ref.at[p], shape)
+    return (array, axes, lambda ref, p: ref.at[:, p], lambda ref, p: ref.at[p], shape, shape[1:])
 
 
 def swap_half(array, axes, half):
     return (
-        array, axes, lambda ref, p: ref.at[half, p], lambda ref, p: ref.at[p], array.shape[1:]
+        array, axes, lambda ref, p: ref.at[half, p], lambda ref, p: ref.at[p], array.shape[1:],
+        array.shape[2:],
     )
 
 
 def share(array, axes, size):
-    return (array, axes, lambda ref, p: ref, lambda ref, p: ref.at[p], (size,) + array.shape)
+    return (
+        array, axes, lambda ref, p: ref, lambda ref, p: ref.at[p], (size,) + array.shape, array.shape
+    )
 
 
 def share_inner(array, axes, size):
     shape = (array.shape[0], size) + array.shape[1:]
-    return (array, axes, lambda ref, p: ref, lambda ref, p: ref.at[:, p], shape)
+    return (array, axes, lambda ref, p: ref, lambda ref, p: ref.at[:, p], shape, array.shape)
 
 
 def exchange(moves, collective_id):
@@ -63,7 +66,8 @@
 
     def kernel(*refs):
         ins, outs = refs[:n], refs[n : 2 * n]
-        send_sem, recv_sem, own_sem = refs[2 * n :]
+        send_sem, recv_sem, own_sem = refs[2 * n : 2 * n + 3]
+        stages = refs[2 * n + 3 :]
         barrier = pltpu.get_barrier_semaphore()
         total = 0
         for ax in greeted:
@@ -73,15 +77,16 @@
                     barrier, inc=1, device_id=ident(lax.rem(me + d, size)), device_id_type=MESH
                 )
             total += size - 1
-        own = []
-        for i, (_, ax, src, dst, _) in enumerate(moves):
+        loads, stores = [], []
+        for i, (_, ax, src, dst, _, _) in enumerate(moves):
             me = peers_of(ax)[0]
-            copy = pltpu.make_async_copy(src(ins[i], me), dst(outs[i], me), own_sem.at[i])
+            loads.append(pltpu.make_async_copy(src(ins[i], me), stages[i], own_sem.at[i]))
+            stores.append(pltpu.make_async_copy(stages[i], dst(outs[i], me), own_sem.at[i]))
+        for copy in loads:
             copy.start()
-            own.append(copy)
         pl.semaphore_wait(barrier, total)
         copies = []
-        for i, (_, ax, src, dst, _) in enumerate(moves):
+        for i, (_, ax, src, dst, _, _) in enumerate(moves):
             me, size, ident = peers_of(ax)
             for d in sorted(range(1, size), key=lambda d: -min(d, size - d)):
                 p = lax.rem(me + d, size)
@@ -95,7 +100,10 @@
                 )
                 copy.start()
                 copies.append(copy)
-        for copy in own + copies:
+        for load, store in zip(loads, stores):
+            load.wait()
+            store.start()
+        for copy in stores + copies:
             copy.wait()
 
     return pl.pallas_call(
@@ -107,8 +115,11 @@
             pltpu.SemaphoreType.DMA((n, 8)),
             pltpu.SemaphoreType.DMA((n, 8)),
             pltpu.SemaphoreType.DMA((n,)),
+            *[pltpu.VMEM(m[5], jnp.float32) for m in moves],
         ],
-        compiler_params=pltpu.CompilerParams(collective_id=collective_id, has_side_effects=True),
+        compiler_params=pltpu.CompilerParams(
+            collective_id=collective_id, has_side_effects=True, vmem_limit_bytes=32 * 1024 * 1024
+        ),
     )(*[m[0] for m in moves])
 
 
@@ -330,6 +341,259 @@
     return halves, left, right, cross.reshape(width, width)
 
 
+PARENT = {
+    (3, 0): (0, 0), (3, 3): (3, 0), (3, 1): (3, 0), (2, 0): (3, 0), (2, 3): (2, 0),
+    (3, 2): (3, 1), (0, 1): (3, 1), (0, 3): (3, 3), (2, 1): (3, 1), (1, 0): (2, 0),
+    (2, 2): (3, 2), (1, 1): (2, 1), (0, 2): (3, 2), (1, 3): (2, 3), (1, 2): (2, 2),
+}
+
+
+def turned(place, quarter_turns):
+    for _ in range(quarter_turns):
+        place = (-place[1] % 4, place[0])
+    return place
+
+
+def tree_children(turn):
+    children = [[] for _ in range(16)]
+    for child, parent in PARENT.items():
+        child, parent = turned(child, turn), turned(parent, turn)
+        children[4 * parent[0] + parent[1]].append(4 * child[0] + child[1])
+    return children
+
+
+def tree_depth(turn):
+    depth = [0] * 16
+    for place in PARENT:
+        node, hops = place, 0
+        while node != (0, 0):
+            node, hops = PARENT[node], hops + 1
+        place = turned(place, turn)
+        depth[4 * place[0] + place[1]] = hops
+    return depth
+
+
+def lookup(values, index):
+    result = jnp.int32(values[0])
+    for k in range(1, len(values)):
+        result = jnp.where(index == k, jnp.int32(values[k]), result)
+    return result
+
+
+CHUNK = 32
+CHUNKS = 2048 // (4 * CHUNK)
+CROSS = CPAN * PANEL // (4 * CHUNK)
+U_PARTS = 4
+DEPTH = 5
+SLACK = 2
+
+
+def spread_kernel(front, cols, rows, cross, recv, send, cross_recv, cross_send, rows_recv,
+                  rows_send, own_sem, stage):
+    y, core = lax.axis_index("y"), lax.axis_index("core")
+    x, z = lax.axis_index("x"), lax.axis_index("z")
+    place, within = 4 * x + z, lax.rem(y, 2) * 2 + core
+    is_root = place == 0
+    tables = [tree_children(turn) for turn in range(4)]
+    target = [
+        [lookup([(t[k] + [-1, -1, -1])[s] for k in range(16)], place) for s in range(3)]
+        for t in tables
+    ]
+    depth = [lookup(tree_depth(turn), place) for turn in range(4)]
+    sibling = {"core": 1 - core}
+    above = {"y": y // 2 * 2 + 1 - lax.rem(y, 2)}
+
+    barrier = pltpu.get_barrier_semaphore()
+    for ident in (
+        {"x": lax.rem(x + 1, 4)}, {"x": lax.rem(x + 3, 4)},
+        {"z": lax.rem(z + 1, 4)}, {"z": lax.rem(z + 3, 4)}, sibling, above,
+    ):
+        pl.semaphore_signal(barrier, inc=1, device_id=ident, device_id_type=MESH)
+
+    part = CPAN * PANEL // U_PARTS
+    whole_band = pl.ds(0, CPAN * PANEL)
+    load_own = pltpu.make_async_copy(front, stage, own_sem.at[0])
+    own_cols = pltpu.make_async_copy(stage, cols, own_sem.at[0])
+    own_rows = pltpu.make_async_copy(stage.at[whole_band], rows, own_sem.at[1])
+    load_own.start()
+    pl.semaphore_wait(barrier, 6)
+
+    def rows_copy(src, k, way, ident):
+        span = pl.ds(k * part, part)
+        return pltpu.make_async_remote_copy(
+            src_ref=src.at[span], dst_ref=rows.at[span], send_sem=rows_send.at[way, k],
+            recv_sem=rows_recv.at[k], device_id=ident, device_id_type=MESH,
+        )
+
+    def band(c, q):
+        return pl.ds(pl.multiple_of((c * 4 + q) * CHUNK, CHUNK), CHUNK)
+
+    def cols_copy(src, c, q, s):
+        span = band(c, q)
+        there = jnp.maximum(target[q][s], 0)
+        return pltpu.make_async_remote_copy(
+            src_ref=src.at[span], dst_ref=cols.at[span], send_sem=send.at[q, s, c],
+            recv_sem=recv.at[q, c], device_id={"x": there // 4, "z": lax.rem(there, 4)},
+            device_id_type=MESH,
+        )
+
+    def cross_copy(src, c, q, way, ident):
+        span = band(c, q)
+        return pltpu.make_async_remote_copy(
+            src_ref=src.at[span], dst_ref=cross.at[span], send_sem=cross_send.at[way, q, c],
+            recv_sem=cross_recv.at[q, c], device_id=ident, device_id_type=MESH,
+        )
+
+    @pl.when(within == 0)
+    def _():
+        for k in range(U_PARTS):
+            rows_copy(front, k, 0, above).start()
+            rows_copy(front, k, 1, sibling).start()
+
+    load_own.wait()
+
+    @pl.when(is_root)
+    def _():
+        own_cols.start()
+
+    @pl.when(within == 0)
+    def _():
+        own_rows.start()
+
+    def both(first, second):
+        return jnp.logical_and(first, second)
+
+    def pass_cols(c, q):
+        @pl.when(is_root)
+        def _():
+            cols_copy(front, c, q, 0).start()
+
+            @pl.when(both(within == 0, c < CROSS))
+            def _():
+                cross_copy(front, c, q, 0, above).start()
+                cross_copy(front, c, q, 1, sibling).start()
+
+        @pl.when(jnp.logical_not(is_root))
+        def _():
+            cols_copy(cols, c, q, 0).wait_recv()
+            for s in range(3):
+
+                @pl.when(target[q][s] >= 0)
+                def _():
+                    cols_copy(cols, c, q, s).start()
+
+            @pl.when(both(within == 0, c < CROSS))
+            def _():
+                cross_copy(cols, c, q, 0, above).start()
+                cross_copy(cols, c, q, 1, sibling).start()
+
+    def loop(lo, hi, body):
+        lax.fori_loop(lo, hi, lambda c, _: (body(c), 0)[1], 0)
+
+    def step(turn):
+        for q in range(4):
+            c = turn - SLACK * depth[q]
+
+            @pl.when(both(c >= 0, c < CHUNKS))
+            def _():
+                pass_cols(c, q)
+
+        for q in range(4):
+            late = turn - SLACK * (depth[q] + 1)
+
+            @pl.when(both(within == 2, both(late >= 0, late < CROSS)))
+            def _():
+                cross_copy(cross, late, q, 0, above).wait_recv()
+                cross_copy(cross, late, q, 1, sibling).start()
+
+    loop(0, CHUNKS + SLACK * DEPTH, step)
+
+    @pl.when(within == 2)
+    def _():
+        for k in range(U_PARTS):
+            rows_copy(rows, k, 0, above).wait_recv()
+            rows_copy(rows, k, 1, sibling).start()
+
+    @pl.when(within == 0)
+    def _():
+        own_rows.wait()
+        for k in range(U_PARTS):
+            rows_copy(front, k, 0, above).wait_send()
+            rows_copy(front, k, 1, sibling).wait_send()
+
+        def send_done(c):
+            for q in range(4):
+                cross_copy(front, c, q, 0, above).wait_send()
+                cross_copy(front, c, q, 1, sibling).wait_send()
+
+        loop(0, CROSS, send_done)
+
+    @pl.when(within == 2)
+    def _():
+        for k in range(U_PARTS):
+            rows_copy(rows, k, 1, sibling).wait_send()
+
+        def send_done(c):
+            for q in range(4):
+                cross_copy(cross, c, q, 1, sibling).wait_send()
+
+        loop(0, CROSS, send_done)
+
+    @pl.when(lax.rem(within, 2) == 1)
+    def _():
+        for k in range(U_PARTS):
+            rows_copy(rows, k, 0, sibling).wait_recv()
+
+        def arrived(c):
+            for q in range(4):
+                cross_copy(cross, c, q, 0, sibling).wait_recv()
+
+        loop(0, CROSS, arrived)
+
+    def cols_done(c):
+        for q in range(4):
+            for s in range(3):
+
+                @pl.when(target[q][s] >= 0)
+                def _():
+                    cols_copy(front, c, q, s).wait_send()
+
+    loop(0, CHUNKS, cols_done)
+
+    @pl.when(is_root)
+    def _():
+        own_cols.wait()
+
+    @pl.when(within == 0)
+    def _():
+        load = pltpu.make_async_copy(cols.at[whole_band], stage.at[whole_band], own_sem.at[0])
+        load.start()
+        load.wait()
+        store = pltpu.make_async_copy(stage.at[whole_band], cross, own_sem.at[0])
+        store.start()
+        store.wait()
+
+
+def spread(front, collective_id):
+    rows, cols = front.shape
+    width = CPAN * PANEL
+    shapes = [(rows, width), (width, cols), (width, width)]
+    dma = pltpu.SemaphoreType.DMA
+    return pl.pallas_call(
+        spread_kernel,
+        out_shape=[jax.ShapeDtypeStruct(s, jnp.float32) for s in shapes],
+        in_specs=[pl.BlockSpec(memory_space=pl.ANY)],
+        out_specs=[pl.BlockSpec(memory_space=pl.ANY)] * 3,
+        scratch_shapes=[
+            dma((4, CHUNKS)), dma((4, 3, CHUNKS)), dma((4, CROSS)), dma((2, 4, CROSS)),
+            dma((U_PARTS,)), dma((2, U_PARTS)), dma((2,)), pltpu.VMEM(front.shape, jnp.float32),
+        ],
+        compiler_params=pltpu.CompilerParams(
+            collective_id=collective_id, has_side_effects=True, vmem_limit_bytes=32 * 1024 * 1024
+        ),
+    )(front)
+
+
 def dot(a, b, precision=HIGH):
     return jnp.dot(a, b, precision=precision, preferred_element_type=jnp.float32)
 
@@ -353,16 +617,18 @@
     return slice(k * PANEL, (k + 1) * PANEL)
 
 
-def finish_kernel(n, row_panels, col_panels, precision, tab, front, upper, lower, left, right, cross, out,
-                  work, inverse, pivots):
+def finish_kernel(n, row_panels, col_panels, precision, bands, tab, front, *refs):
+    cols, rows, cross, out, work, inverse, pivots = (
+        refs[:bands], refs[bands:-5], refs[-5], *refs[-4:]
+    )
     g = pl.program_id(0)
 
     @pl.when(g == 0)
     def _():
         work[...] = cross[...]
-        span = left.shape[1]
-        pivots[:, :span] = left[...]
-        pivots[:, span:] = right[...]
+        for i, part in enumerate(rows):
+            span = part.shape[1]
+            pivots[:, i * span : (i + 1) * span] = part[...]
         for k in range(n):
             inverse[k] = newton(work[panel(k), panel(k)])
             for p in range(k + 1, n):
@@ -376,7 +642,9 @@
                     tab[row_panels + j] > k, pivots[panel(k), panel(j)], 0.0
                 )
 
-    mine = jnp.where(g < row_panels // 2, upper[...], lower[...])
+    mine = cols[0][...]
+    if bands == 2:
+        mine = jnp.where(g < row_panels // 2, mine, cols[1][...])
     band = [mine[:, panel(k)] for k in range(n)]
     for k in range(n):
         band[k] = dot(band[k], inverse[k], HIGHEST)
@@ -392,22 +660,29 @@
         out[:, panel(j)] = new
 
 
-def finish(front, halves, left, right, cross, row_step, col_step, precision):
+def finish(front, bands, pivot_rows, cross, row_step, col_step, precision):
     rows, cols = front.shape
     width = cross.shape[0]
     n, row_panels, col_panels = width // PANEL, rows // PANEL, cols // PANEL
     half = row_panels // 2
     keep = lambda shape: pl.BlockSpec(shape, lambda g, tab: (0, 0))
+    if len(bands) == 1:
+        band_specs = [pl.BlockSpec((PANEL, width), lambda g, tab: (g, 0))]
+    else:
+        band_specs = [
+            pl.BlockSpec((PANEL, width), lambda g, tab: (jnp.minimum(g, half - 1), 0)),
+            pl.BlockSpec((PANEL, width), lambda g, tab: (jnp.maximum(g - half, 0), 0)),
+        ]
     (out,) = local_call(
-        functools.partial(finish_kernel, n, row_panels, col_panels, precision),
+        functools.partial(finish_kernel, n, row_panels, col_panels, precision, len(bands)),
         row_panels,
         jnp.concatenate([row_step, col_step]).astype(jnp.int32),
-        (front, *halves, left, right, cross),
+        (front, *bands, *pivot_rows, cross),
         [
             pl.BlockSpec((PANEL, cols), lambda g, tab: (g, 0)),
-            pl.BlockSpec((PANEL, width), lambda g, tab: (jnp.minimum(g, half - 1), 0)),
-            pl.BlockSpec((PANEL, width), lambda g, tab: (jnp.maximum(g - half, 0), 0)),
-            keep(left.shape), keep(right.shape), keep(cross.shape),
+            *band_specs,
+            *[keep(p.shape) for p in pivot_rows],
+            keep(cross.shape),
         ],
         [front.shape],
         [pl.BlockSpec((PANEL, cols), lambda g, tab: (g, 0))],
@@ -425,16 +700,13 @@
     r, o = 2 * y + core, 4 * lax.axis_index("x") + lax.axis_index("z")
     within = lax.rem(y, 2) * 2 + core
 
-    zeros = [0] * CPAN
-    bands = gather_bands(
-        child_fronts, child_fronts[: CPAN * PANEL].reshape(CPAN, PANEL, -1),
-        [k * PANEL for k in range(CPAN)], zeros, zeros, zeros, "child", 4, 10,
-    )
+    pivot_cols, pivot_rows, cross = spread(child_fronts, 10)
     row_panel, col_panel = within * 8 + jnp.arange(8), o * 2 + jnp.arange(2)
     row_step = jnp.where(row_panel < CPAN, row_panel, NEVER)
     col_step = jnp.where(col_panel < CPAN, col_panel, NEVER)
-    halves, left, right, cross = bands
-    factored = finish(child_fronts, halves, left, right, cross, row_step, col_step, HIGHEST)
+    factored = finish(
+        child_fronts, [pivot_cols], [pivot_rows], cross, row_step, col_step, HIGHEST
+    )
 
     assembled = extend_add(factored, root_front, child_map)
 
@@ -456,7 +728,7 @@
 
     row_step = steps(r * row_panels + jnp.arange(row_panels))
     col_step = steps(o * col_panels + jnp.arange(col_panels))
-    return factored, finish(assembled, halves, left, right, cross, row_step, col_step, HIGH)
+    return factored, finish(assembled, halves, [left, right], cross, row_step, col_step, HIGH)
 
 
 def solution(mesh):

time: 642 us -> 558 us (0.87)
  Pallas kernels: 580 us -> 475 us
  local copies, waits for them, and re-layouts: 31.7 us -> 63.8 us
  other arithmetic: 18.7 us -> 7.24 us
    pallas_call x11 -> x7, Pallas kernels: 476 us -> 343 us  [exchange(): pl.pallas_call(kernel, out_shape=[jax.ShapeDtypeStruct(m[4], jnp.float32)...]
    unnamed x11 -> x49, local copies, waits for them, and re-layouts: 0.12 us -> 40.7 us
    pallas_call x0 -> x1, Pallas kernels: none -> 29.6 us  [spread(): pl.pallas_call(spread_kernel, out_shape=[jax.ShapeDtypeStruct(s, jnp.floa...]
    concatenate x12 -> x6, other arithmetic: 9.02 us -> 1.17 us  [pick(): return jnp.concatenate(parts, axis=-1)]
where the time goes in v3:
time: 558 us; the launch traced here: 557 us
  Pallas kernels  475 us (85%)
  local copies, waits for them, and re-layouts  63.8 us (11%)
  between operations  10.9 us (2%)
  other arithmetic  7.24 us (1%)
    pallas_call x7, Pallas kernels, exchange(): pl.pallas_call(kernel, out_shape=[jax.ShapeDtypeStruct(m[4], jnp.float32)...  343 us
    pallas_call x6, Pallas kernels, local_call(): pl.pallas_call(kernel, grid_spec=pltpu.PrefetchScalarGridSpec(num_scalar_...  103 us
    unnamed x49, local copies, waits for them, and re-layouts  40.7 us
    pallas_call x1, Pallas kernels, spread(): pl.pallas_call(spread_kernel, out_shape=[jax.ShapeDtypeStruct(s, jnp.floa...  29.6 us

profile of v3, /device:TPU:1, one launch (start us, length us, event | category | flops | bytes accessed | tf_op | source)
XLA Modules:
  0.0 557.0 jit_solution(9744511312139770408)
XLA Ops:
  1.3 2.2 copy-done.1
  3.4 29.6 %shard_map.59 = (f32[2048,512]{1,0:T(8,128)S(1)}, f32[512,512]{1,0:T(8,128)S(1)}, f32[512,512]{1,0:T(8,128)S(1)}) custom-call(f32[2048,512]{1,0:T(8,128)S(1)} %copy-done.1), custom_call_target="tpu_custom_call" | custom-call | tf_op jit(solution)/shard_map/pallas_call | solution.py:582
  33.1 2.0 copy-done.7
  35.1 1.0 copy-done.20
  36.1 1.0 copy-done.21
  37.0 26.7 %shard_map.60 = f32[2048,512]{1,0:T(8,128)} custom-call(s32[10]{0:T(128)} %pad_add_fusion.tab, f32[2048,512]{1,0:T(8,128)} %front.3, f32[2048,512]{1,0:T(8,128)} %copy-done.7, f32[512,512]{1,0:T(8,128)} %copy-done.20, f32[512,512]{1,0:T(8,128)} %copy-done.21), custom_call_target="tpu_custom_call" | custom-call | tf_op jit(solution)/shard_map/pallas_call | solution.py:199
  68.8 7.4 %shard_map.61 = (f32[8,16,64,128]{3,2,1,0:T(8,128)}, f32[8,4,64,512]{3,2,1,0:T(8,128)}) custom-call(s32[122]{0:T(128)} %concatenate.54.tab, f32[16,128,512]{2,1,0:T(8,128)} %bitcast.100), custom_call_target="tpu_custom_call" | custom-call | tf_op jit(solution)/shard_map/pallas_call | solution.py:199
  76.2 2.2 copy-done.12
  78.4 2.2 copy-done.13
  80.6 85.4 %shard_map.62 = (f32[4,2,16,64,128]{4,3,2,1,0:T(8,128)S(1)}, f32[8,4,64,512]{3,2,1,0:T(8,128)S(1)}) custom-call(f32[4,2,16,64,128]{4,3,2,1,0:T(8,128)S(1)} %bitcast.89, f32[8,4,64,512]{3,2,1,0:T(8,128)S(1)} %copy-done.13), custom_call_target="tpu_custom_call" | custom-call | tf_op jit(solution)/shard_map/pallas_call | solution.py:109
  166.0 2.0 copy-done.8
  168.0 2.0 copy-done.9
  170.1 9.4 %shard_map.63 = (f32[8,16,64,128]{3,2,1,0:T(8,128)}, f32[8,24,64,128]{3,2,1,0:T(8,128)}) custom-call(s32[122]{0:T(128)} %concatenate.54.tab, f32[8,16,64,128]{3,2,1,0:T(8,128)} %bitcast.85, f32[32,64,512]{2,1,0:T(8,128)} %bitcast.86), custom_call_target="tpu_custom_call" | custom-call | tf_op jit(solution)/shard_map/pallas_call | solution.py:199
  179.5 2.8 copy-done.2
  182.3 2.2 copy-done.10
  184.5 76.0 %shard_map.64 = (f32[4,2,16,64,128]{4,3,2,1,0:T(8,128)S(1)}, f32[4,2,24,64,128]{4,3,2,1,0:T(8,128)S(1)}) custom-call(f32[4,2,16,64,128]{4,3,2,1,0:T(8,128)S(1)} %bitcast.87, f32[4,2,24,64,128]{4,3,2,1,0:T(8,128)S(1)} %bitcast.81), custom_call_target="tpu_custom_call" | custom-call | tf_op jit(solution)/shard_map/pallas_call | solution.py:109
  260.5 2.7 copy-done.4
  263.1 2.0 copy-done.11
  265.2 10.4 %shard_map.65 = (f32[8,4,64,768]{3,2,1,0:T(8,128)}, f32[8,24,64,128]{3,2,1,0:T(8,128)}) custom-call(s32[122]{0:T(128)} %concatenate.54.tab, f32[8,16,64,128]{3,2,1,0:T(8,128)} %bitcast.88, f32[8,24,64,128]{3,2,1,0:T(8,128)} %bitcast.82), custom_call_target="tpu_custom_call" | custom-call | tf_op jit(solution)/shard_map/pallas_call | solution.py:199
  275.6 2.8 copy-done.3
  278.4 72.1 %shard_map.66 = (f32[8,4,64,768]{3,2,1,0:T(8,128)S(1)}, f32[4,2,24,64,128]{4,3,2,1,0:T(8,128)S(1)}) custom-call(f32[8,4,64,768]{3,2,1,0:T(8,128)S(1)} %copy-done.3, f32[4,2,24,64,128]{4,3,2,1,0:T(8,128)} %bitcast.101), custom_call_target="tpu_custom_call" | custom-call | tf_op jit(solution)/shard_map/pallas_call | solution.py:109
  350.5 2.7 copy-done.5
  353.2 2.6 copy-done.6
  355.8 13.3 %shard_map.67 = f32[12,128,768]{2,1,0:T(8,128)} custom-call(s32[122]{0:T(128)} %concatenate.54.tab, f32[12,128,768]{2,1,0:T(8,128)} %bitcast.102, f32[32,64,768]{2,1,0:T(8,128)} %bitcast.83, f32[8,24,64,128]{3,2,1,0:T(8,128)} %bitcast.84), custom_call_target="tpu_custom_call" | custom-call | tf_op jit(solution)/shard_map/pallas_call | solution.py:199
  371.7 3.0 constant_dynamic-slice_fusion.14
  374.7 2.5 pad_maximum_fusion
  379.1 1.9 constant_dynamic-slice_fusion.11
  381.3 2.2 copy-done
  383.4 30.3 %shard_map.68 = (f32[4,192,768]{2,1,0:T(8,128)S(1)}, f32[4,192,768]{2,1,0:T(8,128)S(1)}, f32[8,3,32,768]{3,2,1,0:T(8,128)S(1)}) custom-call(f32[2,4,192,768]{3,2,1,0:T(8,128)S(1)} %bitcast.79, f32[2,4,192,768]{3,2,1,0:T(8,128)S(1)} %bitcast.80, f32[3,8,32,768]{3,2,1,0:T(8,128)S(1)} %pad_maximum_fusion.1.refs_2_), custom_call_target="tpu_custom_call" | custom-call | tf_op jit(solution)/shard_map/pallas_call | solution.py:109
  413.7 1.6 fusion.19
  416.8 0.9 constant_dynamic-slice_fusion.6
  419.2 0.9 constant_dynamic-slice_fusion.7
  421.5 3.1 fusion.18
  424.6 1.6 constant_dynamic-slice_fusion.3
  426.2 1.6 constant_dynamic-slice_fusion.4
  427.8 0.9 constant_dynamic-slice_fusion.5
  428.8 1.1 pad_maximum_fusion.3.refs_1_
  429.8 1.5 fusion.17
  431.9 0.9 dynamic-slice_bitcast_fusion.6
  433.5 0.9 dynamic-slice_bitcast_fusion.7
  435.0 0.9 dynamic-slice_bitcast_fusion.8
  436.1 24.5 %shard_map.69 = (f32[4,48,768]{2,1,0:T(8,128)S(1)}, f32[4,48,768]{2,1,0:T(8,128)S(1)}, f32[4,3,32,768]{3,2,1,0:T(8,128)S(1)}, f32[3,8,32,384]{3,2,1,0:T(8,128)S(1)}) custom-call(f32[4,48,768]{2,1,0:T(8,128)S(1)} %pad_maximum_fusion.2.refs_0_, f32[4,48,768]{2,1,0:T(8,128)S(1)} %pad_maximum_fusion.3.refs_1_, f32[3,32,768]{2,1,0:T(8,128)S(1)} %pad_maximum_fusion.5.refs_2_, ...), custom_call_target="tpu_custom_call" | custom-call | tf_op jit(solution)/shard_map/pallas_call | solution.py:109
  461.7 24.2 %shard_map.70 = (f32[4,48,768]{2,1,0:T(8,128)S(1)}, f32[4,48,768]{2,1,0:T(8,128)S(1)}, f32[4,3,32,768]{3,2,1,0:T(8,128)S(1)}, f32[3,8,32,384]{3,2,1,0:T(8,128)S(1)}) custom-call(f32[48,768]{1,0:T(8,128)S(1)} %pad_maximum_fusion.8.refs_0_, f32[48,768]{1,0:T(8,128)S(1)} %pad_maximum_fusion.9.refs_1_, f32[3,32,768]{2,1,0:T(8,128)S(1)} %pad_maximum_fusion.6.refs_2_, ...), custom_call_target="tpu_custom_call" | custom-call | tf_op jit(solution)/shard_map/pallas_call | solution.py:109
  487.0 30.2 %shard_map.71 = (f32[4,192,768]{2,1,0:T(8,128)S(1)}, f32[4,192,768]{2,1,0:T(8,128)S(1)}, f32[3,8,32,768]{3,2,1,0:T(8,128)S(1)}) custom-call(f32[192,768]{1,0:T(8,128)S(1)} %bitcast.95, f32[192,768]{1,0:T(8,128)S(1)} %bitcast.96, f32[3,32,768]{2,1,0:T(8,128)S(1)} %pad_maximum_fusion.7.refs_2_), custom_call_target="tpu_custom_call" | custom-call | tf_op jit(solution)/shard_map/pallas_call | solution.py:109
  517.3 1.4 copy-done.15
  518.7 1.4 copy-done.16
  520.1 1.5 copy-done.17
  521.5 35.4 %shard_map.72 = f32[1536,768]{1,0:T(8,128)} custom-call(s32[9]{0:T(128)} %pad_add_fusion.1.tab, f32[1536,768]{1,0:T(8,128)} %bitcast.99, f32[768,768]{1,0:T(8,128)} %bitcast.90, f32[768,768]{1,0:T(8,128)} %bitcast.91, f32[768,384]{1,0:T(8,128)} %bitcast.93, f32[768,384]{1,0:T(8,128)} %bitcast.94, f32[768,768]{1,0:T(8,128)} %bitcast.92), custom_call_target="tpu_custom_call" | custom-call | tf_op jit(solution)/shard_map/pallas_call | solution.py:199
  (122 shorter events, 8.9 us)
Async XLA Ops:
  1.2 2.2 copy-start.1
  33.0 2.0 copy-start.7
  35.1 1.0 copy-start.20
  36.1 1.0 copy-start.21
  37.0 26.7 %copy-start.22 = (s32[3]{0:T(128)S(1)}, s32[3]{0:T(128)}, u32[]{:S(2)}) copy-start(s32[3]{0:T(128)} %param.7) | copy-start | bytes 40
  37.0 27.6 %copy-start.23 = (s32[2,60]{1,0:T(2,128)S(1)}, s32[2,60]{1,0:T(2,128)}, u32[]{:S(2)}) copy-start(s32[2,60]{1,0:T(2,128)} %param.6) | copy-start | bytes 1444
  76.2 2.2 copy-start.12
  78.4 2.2 copy-start.13
  166.0 2.0 copy-start.8
  168.0 2.0 copy-start.9
  179.5 2.8 copy-start.2
  182.3 2.2 copy-start.10
  260.5 2.7 copy-start.4
  263.1 2.0 copy-start.11
  275.6 2.8 copy-start.3
  350.5 2.7 copy-start.5
  353.2 2.6 copy-start.6
  381.1 2.3 copy-start
  413.7 1.9 copy-start.14
  460.5 1.1 copy-start.18
  485.9 1.1 copy-start.19
  517.3 1.4 copy-start.15
  518.7 1.4 copy-start.16
  520.1 1.5 copy-start.17

commit v4 on v3

--- a/solution.py
+++ b/solution.py
@@ -130,15 +130,10 @@
     return jnp.sum((same & valid[:, None, :] & earlier[None]).astype(jnp.int32), axis=2)
 
 
-def find(match, value):
-    return jnp.sum(jnp.where(match, value + 1, 0), axis=-1) - 1
-
-
 def routes(child_map):
     y, core = lax.axis_index("y"), lax.axis_index("core")
     x, z = lax.axis_index("x"), lax.axis_index("z")
-    my_child, within = y // 2, lax.rem(y, 2) * 2 + core
-    r, o = 2 * y + core, 4 * x + z
+    within, r, o = lax.rem(y, 2) * 2 + core, 2 * y + core, 4 * x + z
     blocks = jnp.arange(64)
     skip = CPAN * PANEL // BLK
     cyclic = (child_map % 6) * 16 + child_map // 6
@@ -147,44 +142,23 @@
     kz = rank_in(t % 4, blocks // 4, valid)
     kx = rank_in(t % 16, blocks // 16, valid)
     kr = rank_in(t % 16 // 2, blocks // 16, valid)
-    four, two = jnp.arange(4), jnp.arange(2)
-
-    mine = valid & (blocks // 4 == o)[None]
-    z_pick = find(
-        mine[:, None, None]
-        & ((t % 4)[:, None, None] == four[None, :, None, None])
-        & (kz[:, None, None] == two[None, None, :, None]),
-        blocks % 4,
-    )
-    mine = valid & (blocks // 16 == x)[None] & (t % 4 == z)
-    x_pick = find(
-        mine[:, None, None]
-        & ((t % 16 // 4)[:, None, None] == four[None, :, None, None])
-        & (kx[:, None, None] == two[None, None, :, None]),
-        ((blocks // 4 % 4)[None] * 2 + kz)[:, None, None],
-    )
-    slots = jnp.arange(6)
-    col_from = find(
-        valid[:, None] & (t[:, None] == (slots * 16 + o)[None, :, None]),
-        ((blocks // 16)[None] * 2 + kx)[:, None],
-    )
-    mine = valid & (blocks // 16 == within)[None]
-    own = lambda a: lax.dynamic_index_in_dim(a, my_child, 0, keepdims=False)
-    r_pick = find(
-        own(mine)[None, None]
-        & (own(t % 16 // 2)[None, None] == jnp.arange(8)[:, None, None])
-        & (own(kr)[None, None] == four[None, :, None]),
-        blocks % 16,
-    )
-    slots = jnp.arange(12)
-    row_from = find(
-        valid[:, None] & (t[:, None] == (slots % 6 * 16 + 2 * r + slots // 6)[None, :, None]),
-        ((jnp.arange(2)[:, None] * 4 + (blocks // 16)[None]) * 4 + kr)[:, None],
-    )
-    return own(z_pick), z_pick, x_pick, own(x_pick), col_from, own(col_from), r_pick, row_from
-
-
-Z_OWN, Z_PICK, X_PICK, X_OWN, COL_FROM, COL_OWN, R_PICK, ROW_FROM = 0, 8, 24, 40, 48, 60, 66, 98
+    child = jnp.arange(2)[:, None]
+    device, group = (blocks // 4)[None], (blocks // 16)[None]
+    kinds = [
+        (device == o, t % 4 * 2 + kz, blocks[None] % 4),
+        ((group == x) & (t % 4 == z), t % 16 // 4 * 2 + kx, device % 4 * 2 + kz),
+        (t % 16 == o, t // 16, group * 2 + kx),
+        (group == within, t % 16 // 2 * 4 + kr, blocks[None] % 16),
+        (t % 16 // 2 == r, t % 2 * 6 + t // 16, (child * 4 + group) * 4 + kr),
+    ]
+    lists = lambda k: jnp.stack([jnp.broadcast_to(a, (2, 64)) for a in k])
+    place = jnp.where(lists([valid & k[0] for k in kinds]), lists([k[1] for k in kinds]), -1)
+    says = lists([k[2] for k in kinds]) + 1
+    match = place[:, :, None, :] == jnp.arange(32)[None, None, :, None]
+    return (jnp.sum(jnp.where(match, says[:, :, None, :], 0), axis=3) - 1).reshape(-1)
+
+
+Z_PICK, X_PICK, COL_FROM, R_PICK, ROW_FROM = (64 * k for k in range(5))
 
 
 def whole(shape):
@@ -215,75 +189,199 @@
     return pl.ds(pl.multiple_of(block * BLK, BLK), BLK)
 
 
-def pack_first(tab, front, za, yb):
-    g = pl.program_id(0)
-    za[0] = front[:, 0:64, lanes(at_least_zero(tab[Z_OWN + g]))]
-    for k in range(4):
-        yb[0, k] = front[at_least_zero(tab[R_PICK + g * 4 + k]), 64:128, :]
-
-
-def pack_second(tab, zin, yin, xa, zb):
-    g = pl.program_id(0)
-    xa[0] = zin[at_least_zero(tab[X_OWN + g])]
-    for c in range(2):
-        column = lanes(at_least_zero(tab[Z_PICK + c * 8 + g]))
-        for i in range(12):
-            source = at_least_zero(tab[ROW_FROM + c * 12 + i])
-            zb[0, c * 12 + i] = yin[source, :, column]
-
-
-def pack_third(tab, xin, zin, ya, xb):
-    g = pl.program_id(0)
-    for c in range(2):
-        source = at_least_zero(tab[X_PICK + c * 8 + g])
-        xb[0, c * 12 : c * 12 + 12] = zin[source, c * 12 : c * 12 + 12]
-    for k in range(4):
-        i = at_least_zero(tab[R_PICK + g * 4 + k])
-        for slot in range(6):
-            source = at_least_zero(tab[COL_OWN + slot])
-            ya[0, k, :, slot * BLK : slot * BLK + BLK] = xin[source, i]
-
-
-def add_all(tab, root, yin, xin, out):
+QUARTER = BLK // 4
+
+
+def extend_kernel(tab, front, *refs):
+    ya_in, xb_in = refs[0:2], refs[2:4]
+    send_sem, recv_sem, own_sem = refs[-3:]
+    za_out, za_in, xa_out, xa_in, ya_out, yb_out, yb_in, zb_out, zb_in, xb_out = (
+        refs[4 + 2 * i : 6 + 2 * i] for i in range(10)
+    )
+    barrier = pltpu.get_barrier_semaphore()
+    total = 0
+    for ax in ("z", "x", ROW):
+        me, size, ident = peers_of(ax)
+        for d in range(1, size):
+            pl.semaphore_signal(
+                barrier, inc=1, device_id=ident(lax.rem(me + d, size)), device_id_type=MESH
+            )
+        total += size - 1
+
+    started = []
+
+    def send(number, src, dst, axes, count):
+        me, size, ident = peers_of(axes)
+        slot = lambda p: pl.ds(p * count, count)
+        own = pltpu.make_async_copy(src.at[slot(me)], dst.at[slot(me)], own_sem.at[number])
+        own.start()
+        copies = []
+        for d in sorted(range(1, size), key=lambda d: -min(d, size - d)):
+            p = lax.rem(me + d, size)
+            copy = pltpu.make_async_remote_copy(
+                src_ref=src.at[slot(p)],
+                dst_ref=dst.at[slot(me)],
+                send_sem=send_sem.at[number, d],
+                recv_sem=recv_sem.at[number, d],
+                device_id=ident(p),
+                device_id_type=MESH,
+            )
+            copy.start()
+            copies.append(copy)
+        started.extend(copies)
+        return own, copies
+
+    def arrive(transfer):
+        own, copies = transfer
+        own.wait()
+        for copy in copies:
+            copy.wait_recv()
+
+    def each(count, body):
+        lax.fori_loop(0, count, lambda g, _: (body(g), 0)[1], 0)
+
+    own = 32 * (lax.axis_index("y") // 2)
+
+    def entry(at):
+        return tab[at]
+
+    def pack_za(ch):
+        rows = slice(ch * QUARTER, (ch + 1) * QUARTER)
+
+        def body(g):
+            za_out[ch][g] = front[entry(Z_PICK + own + g), :, rows, :]
+
+        each(8, body)
+
+    def pack_yb(ch):
+        rows = slice((2 + ch) * QUARTER, (3 + ch) * QUARTER)
+
+        def body(g):
+            yb_out[ch][g] = front[:, entry(R_PICK + own + g), rows, :]
+
+        each(32, body)
+
+    def pack_xa(ch):
+        def body(g):
+            xa_out[ch][g] = za_in[ch][entry(X_PICK + own + g)]
+
+        each(8, body)
+
+    def pack_zb(ch):
+        def body(g):
+            for c in range(2):
+                column = entry(Z_PICK + c * 32 + g)
+                for i in range(12):
+                    source = entry(ROW_FROM + c * 32 + i)
+                    zb_out[ch][g, c * 12 + i] = yb_in[ch][source, column]
+
+        each(8, body)
+
+    def pack_ya(ch):
+        def body(g):
+            i = entry(R_PICK + own + g)
+            for slot in range(6):
+                columns = slice(slot * BLK, slot * BLK + BLK)
+                ya_out[ch][g, :, columns] = xa_in[ch][entry(COL_FROM + own + slot), i]
+
+        each(32, body)
+
+    def pack_xb(ch):
+        def body(g):
+            for c in range(2):
+                rows = slice(c * 12, c * 12 + 12)
+                xb_out[ch][g, rows] = zb_in[ch][entry(X_PICK + c * 32 + g), rows]
+
+        each(8, body)
+
+    za = lambda ch: send(0 + ch, za_out[ch], za_in[ch], "z", 2)
+    xa = lambda ch: send(2 + ch, xa_out[ch], xa_in[ch], "x", 2)
+    ya = lambda ch: send(4 + ch, ya_out[ch], ya_in[ch], ROW, 4)
+    yb = lambda ch: send(6 + ch, yb_out[ch], yb_in[ch], ROW, 4)
+    zb = lambda ch: send(8 + ch, zb_out[ch], zb_in[ch], "z", 2)
+    xb = lambda ch: send(10 + ch, xb_out[ch], xb_in[ch], "x", 2)
+
+    pack_za(0)
+    pl.semaphore_wait(barrier, total)
+    za0 = za(0)
+    pack_yb(0)
+    yb0 = yb(0)
+    pack_za(1)
+    pack_yb(1)
+    arrive(za0)
+    za1 = za(1)
+    pack_xa(0)
+    xa0 = xa(0)
+    arrive(yb0)
+    yb1 = yb(1)
+    pack_zb(0)
+    zb0 = zb(0)
+    arrive(xa0)
+    pack_ya(0)
+    ya0 = ya(0)
+    arrive(za1)
+    pack_xa(1)
+    xa1 = xa(1)
+    arrive(yb1)
+    pack_zb(1)
+    zb1 = zb(1)
+    arrive(xa1)
+    pack_ya(1)
+    ya1 = ya(1)
+    arrive(zb0)
+    pack_xb(0)
+    xb0 = xb(0)
+    arrive(zb1)
+    pack_xb(1)
+    xb1 = xb(1)
+    for last in (ya0, ya1, xb0, xb1):
+        arrive(last)
+    for copy in started:
+        copy.wait_send()
+
+
+def add_all(tab, root, ya0, ya1, xb0, xb1, out):
     i = pl.program_id(0)
     for slot in range(6):
         columns = slice(slot * BLK, slot * BLK + BLK)
-        upper, lower = root[0, 0:64, columns], root[0, 64:128, columns]
+        sums = [root[0, q * QUARTER : (q + 1) * QUARTER, columns] for q in range(4)]
         for c in range(2):
-            row, col = tab[ROW_FROM + c * 12 + i], tab[COL_FROM + c * 6 + slot]
+            row, col = tab[ROW_FROM + c * 32 + i], tab[COL_FROM + c * 32 + slot]
             there = jnp.logical_and(row >= 0, col >= 0)
-            upper += jnp.where(there, yin[at_least_zero(row), :, columns], 0.0)
-            lower += jnp.where(there, xin[at_least_zero(col), c * 12 + i], 0.0)
-        out[0, 0:64, columns] = upper
-        out[0, 64:128, columns] = lower
-
-
-def extend_add(factored, root_front, child_map):
-    table = jnp.concatenate([a.reshape(-1) for a in routes(child_map)])
-    front = factored.reshape(16, BLK, 512)
-    za, yb = local_call(
-        pack_first, 8, table, (front,), [whole((16, BLK, 512))],
-        [(8, 16, 64, BLK), (8, 4, 64, 512)], [part((16, 64, BLK)), part((4, 64, 512))],
-    )
-    za, yb = exchange([swap(za.reshape(4, 2, 16, 64, BLK), "z"), swap(yb, ROW)], 1)
-    xa, zb = local_call(
-        pack_second, 8, table, (za.reshape(8, 16, 64, BLK), yb.reshape(32, 64, 512)),
-        [whole((8, 16, 64, BLK)), whole((32, 64, 512))],
-        [(8, 16, 64, BLK), (8, 24, 64, BLK)], [part((16, 64, BLK)), part((24, 64, BLK))],
-    )
-    xa, zb = exchange(
-        [swap(xa.reshape(4, 2, 16, 64, BLK), "x"), swap(zb.reshape(4, 2, 24, 64, BLK), "z")], 2
-    )
-    ya, xb = local_call(
-        pack_third, 8, table, (xa.reshape(8, 16, 64, BLK), zb.reshape(8, 24, 64, BLK)),
-        [whole((8, 16, 64, BLK)), whole((8, 24, 64, BLK))],
-        [(8, 4, 64, 768), (8, 24, 64, BLK)], [part((4, 64, 768)), part((24, 64, BLK))],
-    )
-    ya, xb = exchange([swap(ya, ROW), swap(xb.reshape(4, 2, 24, 64, BLK), "x")], 3)
+            row, col = at_least_zero(row), at_least_zero(col)
+            arrived = [
+                ya0[row, :, columns], ya1[row, :, columns], xb0[col, c * 12 + i], xb1[col, c * 12 + i]
+            ]
+            sums = [s + jnp.where(there, a, 0.0) for s, a in zip(sums, arrived)]
+        for q in range(4):
+            out[0, q * QUARTER : (q + 1) * QUARTER, columns] = sums[q]
+
+
+def extend_add(front, root_front, child_map):
+    table = routes(child_map)
+    blocks, rows, wide = (8, 16, QUARTER, BLK), (32, QUARTER, 768), (8, 24, QUARTER, BLK)
+    band = (32, 4, QUARTER, BLK)
+    buffers = [blocks] * 8 + [rows] * 2 + [band] * 4 + [wide] * 6
+    arrived = pl.pallas_call(
+        extend_kernel,
+        out_shape=[jax.ShapeDtypeStruct(s, jnp.float32) for s in (rows, rows, wide, wide)],
+        in_specs=[
+            pl.BlockSpec(memory_space=pltpu.SMEM), pl.BlockSpec(memory_space=pltpu.VMEM),
+        ],
+        out_specs=[pl.BlockSpec(memory_space=pl.ANY)] * 4,
+        scratch_shapes=[
+            *[pltpu.VMEM(s, jnp.float32) for s in buffers],
+            pltpu.SemaphoreType.DMA((12, 8)),
+            pltpu.SemaphoreType.DMA((12, 8)),
+            pltpu.SemaphoreType.DMA((12,)),
+        ],
+        compiler_params=pltpu.CompilerParams(
+            collective_id=1, has_side_effects=True, vmem_limit_bytes=58 * 1024 * 1024
+        ),
+    )(jnp.maximum(table, 0), front.reshape(4, 16, BLK, BLK))
     (assembled,) = local_call(
-        add_all, 12, table,
-        (root_front.reshape(12, BLK, 768), ya.reshape(32, 64, 768), xb.reshape(8, 24, 64, BLK)),
-        [part((BLK, 768)), whole((32, 64, 768)), whole((8, 24, 64, BLK))],
+        add_all, 12, table, (root_front.reshape(12, BLK, 768), *arrived),
+        [part((BLK, 768)), whole(rows), whole(rows), whole(wide), whole(wide)],
         [(12, BLK, 768)], [part((BLK, 768))],
     )
     return assembled.reshape(root_front.shape)
@@ -315,22 +413,25 @@
     )
     split = lambda a: a.reshape(4, count // 32, width)
     half = span // 2
-    first, second, cross, left = exchange(
+    first, second, upper, lower, left = exchange(
         [
-            swap(split(first), "x"), swap(split(second), "z"), share(cross, "z", 4),
+            swap(split(first), "x"), swap(split(second), "z"),
+            share(cross[:, : piece // 2], "z", 4), share(cross[:, piece // 2 :], "x", 4),
             share_inner(slices[..., :half], axes, size),
         ],
         first_id + 1,
     )
-    first, second, cross = pick(first, xs), pick(second, zs), pick(cross, zs)
-    first, second, cross, right = exchange(
+    first, second = pick(first, xs), pick(second, zs)
+    upper, lower = pick(upper, zs), pick(lower, xs)
+    first, second, upper, lower, right = exchange(
         [
-            share(first, "x", 4), share(second, "z", 4), share(cross, "x", 4),
+            share(first, "x", 4), share(second, "z", 4),
+            share(upper, "x", 4), share(lower, "z", 4),
             share_inner(slices[..., half:], axes, size),
         ],
         first_id + 2,
     )
-    cross = pick(cross, xs)
+    cross = jnp.concatenate([pick(upper, xs), pick(lower, zs)], axis=1)
     join = lambda a: a.reshape(count // 8, width)
     first, second, cross = exchange(
         [share(join(first), "z", 4), share(join(second), "x", 4), share_inner(cross, axes, size)],
@@ -607,20 +708,20 @@
     identity = jnp.where(eye, 1.0, 0.0)
     error = identity - block * by_col
     product = identity + error
-    for _ in range(3):
-        error = dot(error, error, HIGHEST)
-        product = product + dot(product, error, HIGHEST)
-    return product * by_row
+    error = dot(error, error, HIGHEST)
+    for _ in range(2):
+        both = dot(jnp.concatenate([error, product], axis=0), error, HIGHEST)
+        error, product = both[:PANEL], product + both[PANEL:]
+    return (product + dot(product, error, HIGHEST)) * by_row
 
 
 def panel(k):
     return slice(k * PANEL, (k + 1) * PANEL)
 
 
-def finish_kernel(n, row_panels, col_panels, precision, bands, tab, front, *refs):
-    cols, rows, cross, out, work, inverse, pivots = (
-        refs[:bands], refs[bands:-5], refs[-5], *refs[-4:]
-    )
+def finish_kernel(n, row_panels, col_panels, precision, bands, tail, tab, front, *refs):
+    cols, rows, cross, outs = refs[:bands], refs[bands:tail], refs[tail], refs[tail + 1 : -3]
+    work, inverse, pivots = refs[-3:]
     g = pl.program_id(0)
 
     @pl.when(g == 0)
@@ -657,10 +758,13 @@
         for k in range(n):
             here = jnp.logical_and(tab[row_panels + j] == k, tab[g] > k)
             new = jnp.where(here, band[k], new)
-        out[:, panel(j)] = new
-
-
-def finish(front, bands, pivot_rows, cross, row_step, col_step, precision):
+        outs[0][:, panel(j)] = new
+        if len(outs) == 2:
+            outs[1][2 * j] = new[:, :BLK]
+            outs[1][2 * j + 1] = new[:, BLK:]
+
+
+def finish(front, bands, pivot_rows, cross, row_step, col_step, precision, blocked=False):
     rows, cols = front.shape
     width = cross.shape[0]
     n, row_panels, col_panels = width // PANEL, rows // PANEL, cols // PANEL
@@ -673,8 +777,8 @@
             pl.BlockSpec((PANEL, width), lambda g, tab: (jnp.minimum(g, half - 1), 0)),
             pl.BlockSpec((PANEL, width), lambda g, tab: (jnp.maximum(g - half, 0), 0)),
         ]
-    (out,) = local_call(
-        functools.partial(finish_kernel, n, row_panels, col_panels, precision, len(bands)),
+    return local_call(
+        functools.partial(finish_kernel, n, row_panels, col_panels, precision, len(bands), len(bands) + len(pivot_rows)),
         row_panels,
         jnp.concatenate([row_step, col_step]).astype(jnp.int32),
         (front, *bands, *pivot_rows, cross),
@@ -684,15 +788,15 @@
             *[keep(p.shape) for p in pivot_rows],
             keep(cross.shape),
         ],
-        [front.shape],
-        [pl.BlockSpec((PANEL, cols), lambda g, tab: (g, 0))],
+        [front.shape] + [(cols // BLK, rows, BLK)] * blocked,
+        [pl.BlockSpec((PANEL, cols), lambda g, tab: (g, 0))]
+        + [pl.BlockSpec((cols // BLK, PANEL, BLK), lambda g, tab: (0, g, 0))] * blocked,
         scratch=[
             pltpu.VMEM((width, width), jnp.float32),
             pltpu.VMEM((n, PANEL, PANEL), jnp.float32),
             pltpu.VMEM((width, cols), jnp.float32),
         ],
     )
-    return out
 
 
 def body(child_fronts, root_front, child_map, panel_order):
@@ -704,11 +808,11 @@
     row_panel, col_panel = within * 8 + jnp.arange(8), o * 2 + jnp.arange(2)
     row_step = jnp.where(row_panel < CPAN, row_panel, NEVER)
     col_step = jnp.where(col_panel < CPAN, col_panel, NEVER)
-    factored = finish(
-        child_fronts, [pivot_cols], [pivot_rows], cross, row_step, col_step, HIGHEST
-    )
-
-    assembled = extend_add(factored, root_front, child_map)
+    factored, blocks = finish(
+        child_fronts, [pivot_cols], [pivot_rows], cross, row_step, col_step, HIGHEST, True
+    )
+
+    assembled = extend_add(blocks, root_front, child_map)
 
     row_panels, col_panels = 6, 3
     order = [panel_order[k] for k in range(RPAN)]
@@ -728,7 +832,7 @@
 
     row_step = steps(r * row_panels + jnp.arange(row_panels))
     col_step = steps(o * col_panels + jnp.arange(col_panels))
-    return factored, finish(assembled, halves, [left, right], cross, row_step, col_step, HIGH)
+    return factored, finish(assembled, halves, [left, right], cross, row_step, col_step, HIGH)[0]
 
 
 def solution(mesh):

time: 558 us -> 443 us (0.79)
  Pallas kernels: 475 us -> 406 us
  local copies, waits for them, and re-layouts: 63.8 us -> 19.3 us
    pallas_call x7 -> x4, Pallas kernels: 343 us -> 99.3 us  [exchange(): pl.pallas_call(kernel, out_shape=[jax.ShapeDtypeStruct(m[4], jnp.float32)...]
    pallas_call x0 -> x1, Pallas kernels: none -> 198 us  [extend_add(): pl.pallas_call(extend_kernel, out_shape=[jax.ShapeDtypeStruct(s, jnp.floa...]
    unnamed x49 -> x26, local copies, waits for them, and re-layouts: 40.7 us -> 14.1 us
    pallas_call x6 -> x3, Pallas kernels: 103 us -> 79 us  [local_call(): pl.pallas_call(kernel, grid_spec=pltpu.PrefetchScalarGridSpec(num_scalar_...]
    dynamic_slice x6, local copies, waits for them, and re-layouts: 6.08 us -> 0.14 us  [pick(): lax.dynamic_index_in_dim(arrived[..., q * PANEL:(q + 1) * PANEL], owner,...]
where the time goes in v4:
time: 443 us; the launch traced here: 442 us
  Pallas kernels  406 us (92%)
  local copies, waits for them, and re-layouts  19.3 us (4%)
  between operations  11.4 us (3%)
  other arithmetic  6.11 us (1%)
    pallas_call x1, Pallas kernels, extend_add(): pl.pallas_call(extend_kernel, out_shape=[jax.ShapeDtypeStruct(s, jnp.floa...  198 us
    pallas_call x4, Pallas kernels, exchange(): pl.pallas_call(kernel, out_shape=[jax.ShapeDtypeStruct(m[4], jnp.float32)...  99.3 us
    pallas_call x3, Pallas kernels, local_call(): pl.pallas_call(kernel, grid_spec=pltpu.PrefetchScalarGridSpec(num_scalar_...  79 us
    pallas_call x1, Pallas kernels, spread(): pl.pallas_call(spread_kernel, out_shape=[jax.ShapeDtypeStruct(s, jnp.floa...  29.6 us
    unnamed x26, local copies, waits for them, and re-layouts  14.1 us

profile of v4, /device:TPU:1, one launch (start us, length us, event | category | flops | bytes accessed | tf_op | source)
XLA Modules:
  0.0 442.5 jit_solution(10806366606026734970)
XLA Ops:
  0.7 0.7 select_reduce_fusion.2
  1.4 0.6 pad_add_fusion.tab
  2.0 0.8 select_reduce_fusion.1
  2.9 0.7 pad_add_fusion.1.tab
  3.6 0.7 fusion.1
  4.3 1.4 fusion.15
  15.8 0.1 constant_dynamic-update-slice_fusion.3
  15.9 0.1 constant_dynamic-update-slice_fusion.2
  16.1 0.1 broadcast_compare_fusion.1
  16.1 0.1 broadcast_compare_fusion
  16.2 0.3 convert_reduce_fusion
  16.6 0.1 constant_dynamic-update-slice_fusion.7
  16.7 0.1 constant_dynamic-update-slice_fusion.6
  16.7 0.1 constant_dynamic-update-slice_fusion.5
  16.8 0.3 select_reduce_fusion
  17.1 0.1 sub.97.tab
  17.2 0.6 broadcast_maximum_fusion.tab
  17.8 2.2 copy-done
  20.0 29.6 %shard_map.59 = (f32[2048,512]{1,0:T(8,128)S(1)}, f32[512,512]{1,0:T(8,128)S(1)}, f32[512,512]{1,0:T(8,128)S(1)}) custom-call(f32[2048,512]{1,0:T(8,128)S(1)} %copy-done), custom_call_target="tpu_custom_call" | custom-call | tf_op jit(solution)/shard_map/pallas_call | solution.py:683
  49.6 0.0 copy-start.1
  49.6 2.0 copy-done.1
  51.6 1.0 copy-done.7
  52.6 1.0 copy-done.8
  53.6 28.1 %shard_map.60 = (f32[2048,512]{1,0:T(8,128)}, f32[4,2048,128]{2,1,0:T(8,128)}) custom-call(s32[10]{0:T(128)} %pad_add_fusion.tab, f32[2048,512]{1,0:T(8,128)} %front.3, f32[2048,512]{1,0:T(8,128)} %copy-done.1, f32[512,512]{1,0:T(8,128)} %copy-done.7, f32[512,512]{1,0:T(8,128)} %copy-done.8), custom_call_target="tpu_custom_call" | custom-call | tf_op jit(solution)/shard_map/pallas_call | solution.py:173
  81.7 197.8 %shard_map.61 = (f32[32,32,768]{2,1,0:T(8,128)}, f32[32,32,768]{2,1,0:T(8,128)}, f32[8,24,32,128]{3,2,1,0:T(8,128)}, f32[8,24,32,128]{3,2,1,0:T(8,128)}) custom-call(s32[320]{0:T(512)} %broadcast_maximum_fusion.tab, f32[4,16,128,128]{3,2,1,0:T(8,128)} %bitcast.118), custom_call_target="tpu_custom_call" | custom-call | tf_op jit(solution)/shard_map/pallas_call | solution.py:365
  279.5 13.4 %shard_map.62 = f32[12,128,768]{2,1,0:T(8,128)} custom-call(s32[320]{0:T(512)} %copy-done.10, f32[12,128,768]{2,1,0:T(8,128)} %bitcast.117, f32[32,32,768]{2,1,0:T(8,128)} %get-tuple-element.32.ya0, f32[32,32,768]{2,1,0:T(8,128)} %get-tuple-element.33.ya1, f32[8,24,32,128]{3,2,1,0:T(8,128)} %get-tuple-element.34.xb0, f32[8,24,32,128]{3,2,1,0:T(8,128)} %get-tuple-element.35.xb1), custom_call_target="tpu_custom_call" | custom-call | tf_op jit(solution)/shard_map/pallas_call | solution.py:173
  292.9 1.9 constant_dynamic-slice_fusion.11
  294.7 0.2 pad_maximum_fusion.1.refs_2_
  295.0 2.1 copy-done.9
  297.1 0.4 constant_dynamic-slice_fusion.14
  297.5 0.3 pad_maximum_fusion
  297.8 32.8 %shard_map.63 = (f32[4,192,768]{2,1,0:T(8,128)S(1)}, f32[4,192,768]{2,1,0:T(8,128)S(1)}, f32[8,3,32,768]{3,2,1,0:T(8,128)S(1)}) custom-call(f32[2,4,192,768]{3,2,1,0:T(8,128)S(1)} %bitcast.105, f32[2,4,192,768]{3,2,1,0:T(8,128)S(1)} %bitcast.106, f32[3,8,32,768]{3,2,1,0:T(8,128)S(1)} %pad_maximum_fusion.1.refs_2_), custom_call_target="tpu_custom_call" | custom-call | tf_op jit(solution)/shard_map/pallas_call | solution.py:109
  330.6 0.2 fusion.6
  331.0 0.2 fusion.5
  331.4 0.2 fusion.4
  331.8 17.9 %shard_map.64 = (f32[4,48,768]{2,1,0:T(8,128)S(1)}, f32[4,48,768]{2,1,0:T(8,128)S(1)}, f32[4,3,16,768]{3,2,1,0:T(8,128)S(1)}, f32[4,3,16,768]{3,2,1,0:T(8,128)S(1)}, f32[3,8,32,384]{3,2,1,0:T(8,128)S(1)}) custom-call(f32[4,48,768]{2,1,0:T(8,128)S(1)} %pad_maximum_fusion.2.refs_0_, f32[4,48,768]{2,1,0:T(8,128)S(1)} %pad_maximum_fusion.3.refs_1_, ...), custom_call_target="tpu_custom_call" | custom-call | tf_op jit(solution)/shard_map/pallas_call | solution.py:109
  350.0 0.1 fusion.10
  350.1 0.7 copy-done.5
  350.9 0.1 fusion.9
  351.0 18.0 %shard_map.65 = (f32[4,48,768]{2,1,0:T(8,128)S(1)}, f32[4,48,768]{2,1,0:T(8,128)S(1)}, f32[4,3,16,768]{3,2,1,0:T(8,128)S(1)}, f32[4,3,16,768]{3,2,1,0:T(8,128)S(1)}, f32[3,8,32,384]{3,2,1,0:T(8,128)S(1)}) custom-call(f32[48,768]{1,0:T(8,128)S(1)} %pad_maximum_fusion.6.refs_0_, f32[48,768]{1,0:T(8,128)S(1)} %pad_maximum_fusion.7.refs_1_, ...), custom_call_target="tpu_custom_call" | custom-call | tf_op jit(solution)/shard_map/pallas_call | solution.py:109
  369.1 0.1 fusion.7
  369.2 0.1 fusion.8
  369.3 0.8 copy-done.6
  370.1 30.6 %shard_map.66 = (f32[4,192,768]{2,1,0:T(8,128)S(1)}, f32[4,192,768]{2,1,0:T(8,128)S(1)}, f32[3,8,32,768]{3,2,1,0:T(8,128)S(1)}) custom-call(f32[192,768]{1,0:T(8,128)S(1)} %bitcast.112, f32[192,768]{1,0:T(8,128)S(1)} %bitcast.113, f32[3,32,768]{2,1,0:T(8,128)S(1)} %maximum_maximum_fusion.refs_2_), custom_call_target="tpu_custom_call" | custom-call | tf_op jit(solution)/shard_map/pallas_call | solution.py:109
  400.7 1.4 copy-done.2
  402.1 1.5 copy-done.3
  403.6 1.4 copy-done.4
  405.0 37.5 %shard_map.67 = f32[1536,768]{1,0:T(8,128)} custom-call(s32[9]{0:T(128)} %pad_add_fusion.1.tab, f32[1536,768]{1,0:T(8,128)} %bitcast.115, f32[768,768]{1,0:T(8,128)} %bitcast.107, f32[768,768]{1,0:T(8,128)} %bitcast.108, f32[768,384]{1,0:T(8,128)} %bitcast.110, f32[768,384]{1,0:T(8,128)} %bitcast.111, f32[768,768]{1,0:T(8,128)} %bitcast.109), custom_call_target="tpu_custom_call" | custom-call | tf_op jit(solution)/shard_map/pallas_call | solution.py:173
  (73 shorter events, 0.9 us)
Async XLA Ops:
  17.2 64.5 %copy-start.10 = (s32[320]{0:T(512)}, s32[320]{0:T(512)S(1)}, u32[]{:S(2)}) copy-start(s32[320]{0:T(512)S(1)} %sub.97.tab) | copy-start | bytes 3844
  17.8 2.2 copy-start
  49.6 2.0 copy-start.1
  51.6 1.0 copy-start.7
  52.6 1.0 copy-start.8
  294.7 2.3 copy-start.9
  349.7 1.1 copy-start.5
  369.1 1.0 copy-start.6
  400.7 1.4 copy-start.2
  402.1 1.5 copy-start.3
  403.6 1.4 copy-start.4

commit v5 on v4

--- a/solution.py
+++ b/solution.py
@@ -189,14 +189,15 @@
     return pl.ds(pl.multiple_of(block * BLK, BLK), BLK)
 
 
-QUARTER = BLK // 4
+PARTS = 4
+SLICE = BLK // (2 * PARTS)
 
 
 def extend_kernel(tab, front, *refs):
-    ya_in, xb_in = refs[0:2], refs[2:4]
+    ya_in, xb_in = refs[:PARTS], refs[PARTS : 2 * PARTS]
     send_sem, recv_sem, own_sem = refs[-3:]
     za_out, za_in, xa_out, xa_in, ya_out, yb_out, yb_in, zb_out, zb_in, xb_out = (
-        refs[4 + 2 * i : 6 + 2 * i] for i in range(10)
+        refs[(2 + i) * PARTS : (3 + i) * PARTS] for i in range(10)
     )
     barrier = pltpu.get_barrier_semaphore()
     total = 0
@@ -246,7 +247,7 @@
         return tab[at]
 
     def pack_za(ch):
-        rows = slice(ch * QUARTER, (ch + 1) * QUARTER)
+        rows = slice(ch * SLICE, (ch + 1) * SLICE)
 
         def body(g):
             za_out[ch][g] = front[entry(Z_PICK + own + g), :, rows, :]
@@ -254,7 +255,7 @@
         each(8, body)
 
     def pack_yb(ch):
-        rows = slice((2 + ch) * QUARTER, (3 + ch) * QUARTER)
+        rows = slice((PARTS + ch) * SLICE, (PARTS + ch + 1) * SLICE)
 
         def body(g):
             yb_out[ch][g] = front[:, entry(R_PICK + own + g), rows, :]
@@ -294,95 +295,95 @@
 
         each(8, body)
 
-    za = lambda ch: send(0 + ch, za_out[ch], za_in[ch], "z", 2)
-    xa = lambda ch: send(2 + ch, xa_out[ch], xa_in[ch], "x", 2)
-    ya = lambda ch: send(4 + ch, ya_out[ch], ya_in[ch], ROW, 4)
-    yb = lambda ch: send(6 + ch, yb_out[ch], yb_in[ch], ROW, 4)
-    zb = lambda ch: send(8 + ch, zb_out[ch], zb_in[ch], "z", 2)
-    xb = lambda ch: send(10 + ch, xb_out[ch], xb_in[ch], "x", 2)
+    stages = {
+        "A": [
+            (pack_za, "z", za_out, za_in, 2, 2), (pack_xa, "x", xa_out, xa_in, 2, 2),
+            (pack_ya, ROW, ya_out, ya_in, 4, 3),
+        ],
+        "B": [
+            (pack_yb, ROW, yb_out, yb_in, 4, 2), (pack_zb, "z", zb_out, zb_in, 2, 3),
+            (pack_xb, "x", xb_out, xb_in, 2, 3),
+        ],
+    }
+    free, pending, number = {"z": 0, "x": 0, ROW: 0}, [], 0
+
+    def begin(time, half, ch, stage, packed=False):
+        nonlocal number
+        pack, axes, out, arriving, count, cost = stages[half][stage]
+        if not packed:
+            pack(ch)
+        free[axes] = max(time, free[axes]) + cost
+        pending.append((free[axes], number, half, ch, stage, send(number, out[ch], arriving[ch], axes, count)))
+        number += 1
 
     pack_za(0)
     pl.semaphore_wait(barrier, total)
-    za0 = za(0)
-    pack_yb(0)
-    yb0 = yb(0)
-    pack_za(1)
-    pack_yb(1)
-    arrive(za0)
-    za1 = za(1)
-    pack_xa(0)
-    xa0 = xa(0)
-    arrive(yb0)
-    yb1 = yb(1)
-    pack_zb(0)
-    zb0 = zb(0)
-    arrive(xa0)
-    pack_ya(0)
-    ya0 = ya(0)
-    arrive(za1)
-    pack_xa(1)
-    xa1 = xa(1)
-    arrive(yb1)
-    pack_zb(1)
-    zb1 = zb(1)
-    arrive(xa1)
-    pack_ya(1)
-    ya1 = ya(1)
-    arrive(zb0)
-    pack_xb(0)
-    xb0 = xb(0)
-    arrive(zb1)
-    pack_xb(1)
-    xb1 = xb(1)
-    for last in (ya0, ya1, xb0, xb1):
-        arrive(last)
+    begin(0, "A", 0, 0, packed=True)
+    begin(0, "B", 0, 0)
+    for ch in range(1, PARTS):
+        pack_za(ch)
+        pack_yb(ch)
+    while pending:
+        pending.sort(key=lambda p: p[:2])
+        time, _, half, ch, stage, transfer = pending.pop(0)
+        arrive(transfer)
+        if stage == 0 and ch + 1 < PARTS:
+            begin(time, half, ch + 1, 0, packed=True)
+        if stage < 2:
+            begin(time, half, ch, stage + 1)
     for copy in started:
         copy.wait_send()
 
 
-def add_all(tab, root, ya0, ya1, xb0, xb1, out):
+def add_all(tab, root, *refs):
     i = pl.program_id(0)
+    out = refs[-1]
     for slot in range(6):
         columns = slice(slot * BLK, slot * BLK + BLK)
-        sums = [root[0, q * QUARTER : (q + 1) * QUARTER, columns] for q in range(4)]
+        sums = [root[0, q * SLICE : (q + 1) * SLICE, columns] for q in range(2 * PARTS)]
         for c in range(2):
+            mine = refs[c * 2 * PARTS : (c + 1) * 2 * PARTS]
             row, col = tab[ROW_FROM + c * 32 + i], tab[COL_FROM + c * 32 + slot]
             there = jnp.logical_and(row >= 0, col >= 0)
-            row, col = at_least_zero(row), at_least_zero(col)
-            arrived = [
-                ya0[row, :, columns], ya1[row, :, columns], xb0[col, c * 12 + i], xb1[col, c * 12 + i]
-            ]
+            col = at_least_zero(col)
+            arrived = [m[0, :, columns] for m in mine[:PARTS]] + [m[col, 0] for m in mine[PARTS:]]
             sums = [s + jnp.where(there, a, 0.0) for s, a in zip(sums, arrived)]
-        for q in range(4):
-            out[0, q * QUARTER : (q + 1) * QUARTER, columns] = sums[q]
+        for q in range(2 * PARTS):
+            out[0, q * SLICE : (q + 1) * SLICE, columns] = sums[q]
 
 
 def extend_add(front, root_front, child_map):
     table = routes(child_map)
-    blocks, rows, wide = (8, 16, QUARTER, BLK), (32, QUARTER, 768), (8, 24, QUARTER, BLK)
-    band = (32, 4, QUARTER, BLK)
-    buffers = [blocks] * 8 + [rows] * 2 + [band] * 4 + [wide] * 6
+    blocks, rows, wide = (8, 16, SLICE, BLK), (32, SLICE, 768), (8, 24, SLICE, BLK)
+    band = (32, 4, SLICE, BLK)
+    buffers = [blocks] * (4 * PARTS) + [rows] * PARTS + [band] * (2 * PARTS) + [wide] * (3 * PARTS)
     arrived = pl.pallas_call(
         extend_kernel,
-        out_shape=[jax.ShapeDtypeStruct(s, jnp.float32) for s in (rows, rows, wide, wide)],
+        out_shape=[jax.ShapeDtypeStruct(s, jnp.float32) for s in [rows] * PARTS + [wide] * PARTS],
         in_specs=[
             pl.BlockSpec(memory_space=pltpu.SMEM), pl.BlockSpec(memory_space=pltpu.VMEM),
         ],
-        out_specs=[pl.BlockSpec(memory_space=pl.ANY)] * 4,
+        out_specs=[pl.BlockSpec(memory_space=pl.ANY)] * (2 * PARTS),
         scratch_shapes=[
             *[pltpu.VMEM(s, jnp.float32) for s in buffers],
-            pltpu.SemaphoreType.DMA((12, 8)),
-            pltpu.SemaphoreType.DMA((12, 8)),
-            pltpu.SemaphoreType.DMA((12,)),
+            pltpu.SemaphoreType.DMA((6 * PARTS, 8)),
+            pltpu.SemaphoreType.DMA((6 * PARTS, 8)),
+            pltpu.SemaphoreType.DMA((6 * PARTS,)),
         ],
         compiler_params=pltpu.CompilerParams(
             collective_id=1, has_side_effects=True, vmem_limit_bytes=58 * 1024 * 1024
         ),
     )(jnp.maximum(table, 0), front.reshape(4, 16, BLK, BLK))
+    operands, specs = [], []
+    for c in range(2):
+        from_rows = lambda g, tab, c=c: (at_least_zero(tab[ROW_FROM + c * 32 + g]), 0, 0)
+        from_wide = lambda g, tab, c=c: (0, c * 12 + g, 0, 0)
+        operands += arrived
+        specs += [pl.BlockSpec((1,) + rows[1:], from_rows)] * PARTS
+        specs += [pl.BlockSpec((8, 1, SLICE, BLK), from_wide)] * PARTS
     (assembled,) = local_call(
-        add_all, 12, table, (root_front.reshape(12, BLK, 768), *arrived),
-        [part((BLK, 768)), whole(rows), whole(rows), whole(wide), whole(wide)],
-        [(12, BLK, 768)], [part((BLK, 768))],
+        add_all, 12, table, (root_front.reshape(12, BLK, 768), *operands),
+        [part((BLK, 768)), *specs], [(12, BLK, 768)], [part((BLK, 768))],
     )
     return assembled.reshape(root_front.shape)
 
@@ -487,6 +488,7 @@
 U_PARTS = 4
 DEPTH = 5
 SLACK = 2
+U_TURN = 8
 
 
 def spread_kernel(front, cols, rows, cross, recv, send, cross_recv, cross_send, rows_recv,
@@ -517,6 +519,10 @@
     own_cols = pltpu.make_async_copy(stage, cols, own_sem.at[0])
     own_rows = pltpu.make_async_copy(stage.at[whole_band], rows, own_sem.at[1])
     load_own.start()
+    load_cross = pltpu.make_async_copy(
+        cols.at[whole_band], stage.at[whole_band], own_sem.at[2]
+    )
+    store_cross = pltpu.make_async_copy(stage.at[whole_band], cross, own_sem.at[2])
     pl.semaphore_wait(barrier, 6)
 
     def rows_copy(src, k, way, ident):
@@ -560,6 +566,11 @@
     @pl.when(within == 0)
     def _():
         own_rows.start()
+        own_rows.wait()
+
+    @pl.when(is_root)
+    def _():
+        own_cols.wait()
 
     def both(first, second):
         return jnp.logical_and(first, second)
@@ -607,17 +618,26 @@
                 cross_copy(cross, late, q, 0, above).wait_recv()
                 cross_copy(cross, late, q, 1, sibling).start()
 
+        for k in range(U_PARTS):
+
+            @pl.when(both(within == 2, turn == U_TURN + k))
+            def _():
+                rows_copy(rows, k, 0, above).wait_recv()
+                rows_copy(rows, k, 1, sibling).start()
+
+        @pl.when(both(within == 0, turn == CROSS + SLACK * DEPTH))
+        def _():
+            load_cross.start()
+
+        @pl.when(both(within == 0, turn == CROSS + SLACK * DEPTH + 3))
+        def _():
+            load_cross.wait()
+            store_cross.start()
+
     loop(0, CHUNKS + SLACK * DEPTH, step)
-
-    @pl.when(within == 2)
-    def _():
-        for k in range(U_PARTS):
-            rows_copy(rows, k, 0, above).wait_recv()
-            rows_copy(rows, k, 1, sibling).start()
 
     @pl.when(within == 0)
     def _():
-        own_rows.wait()
         for k in range(U_PARTS):
             rows_copy(front, k, 0, above).wait_send()
             rows_copy(front, k, 1, sibling).wait_send()
@@ -661,18 +681,9 @@
 
     loop(0, CHUNKS, cols_done)
 
-    @pl.when(is_root)
-    def _():
-        own_cols.wait()
-
     @pl.when(within == 0)
     def _():
-        load = pltpu.make_async_copy(cols.at[whole_band], stage.at[whole_band], own_sem.at[0])
-        load.start()
-        load.wait()
-        store = pltpu.make_async_copy(stage.at[whole_band], cross, own_sem.at[0])
-        store.start()
-        store.wait()
+        store_cross.wait()
 
 
 def spread(front, collective_id):
@@ -687,7 +698,7 @@
         out_specs=[pl.BlockSpec(memory_space=pl.ANY)] * 3,
         scratch_shapes=[
             dma((4, CHUNKS)), dma((4, 3, CHUNKS)), dma((4, CROSS)), dma((2, 4, CROSS)),
-            dma((U_PARTS,)), dma((2, U_PARTS)), dma((2,)), pltpu.VMEM(front.shape, jnp.float32),
+            dma((U_PARTS,)), dma((2, U_PARTS)), dma((3,)), pltpu.VMEM(front.shape, jnp.float32),
         ],
         compiler_params=pltpu.CompilerParams(
             collective_id=collective_id, has_side_effects=True, vmem_limit_bytes=32 * 1024 * 1024
@@ -708,11 +719,10 @@
     identity = jnp.where(eye, 1.0, 0.0)
     error = identity - block * by_col
     product = identity + error
-    error = dot(error, error, HIGHEST)
-    for _ in range(2):
-        both = dot(jnp.concatenate([error, product], axis=0), error, HIGHEST)
-        error, product = both[:PANEL], product + both[PANEL:]
-    return (product + dot(product, error, HIGHEST)) * by_row
+    for _ in range(3):
+        error = dot(error, error, HIGHEST)
+        product = product + dot(product, error, HIGHEST)
+    return product * by_row
 
 
 def panel(k):
@@ -815,15 +825,16 @@
     assembled = extend_add(blocks, root_front, child_map)
 
     row_panels, col_panels = 6, 3
-    order = [panel_order[k] for k in range(RPAN)]
-    col_off = [p % col_panels * PANEL for p in order]
-    row_off = [p % row_panels * PANEL for p in order]
-    owner = [p // col_panels for p in order]
+    order = panel_order.astype(jnp.uint32)
+    each = lambda a: [a[k] for k in range(RPAN)]
+    col_off = each(order % col_panels * PANEL)
+    row_off = each(order % row_panels * PANEL)
+    owner_x, owner_z = each(order // (4 * col_panels)), each(order // col_panels % 4)
+    owner_row = each(order // row_panels)
     cols = jnp.concatenate([lax.dynamic_slice_in_dim(assembled, off, PANEL, 1) for off in col_off], 1)
     rows = jnp.stack([lax.dynamic_slice_in_dim(assembled, off, PANEL, 0) for off in row_off])
     halves, left, right, cross = gather_bands(
-        cols, rows, col_off, [c // 4 for c in owner], [c % 4 for c in owner],
-        [p // row_panels for p in order], ROW, 8, 20,
+        cols, rows, col_off, owner_x, owner_z, owner_row, ROW, 8, 20,
     )
 
     def steps(places):

time: 443 us -> 430 us (0.971)
  Pallas kernels: 406 us -> 381 us
  local copies, waits for them, and re-layouts: 19.3 us -> 42.4 us
  between operations: 11.4 us -> 1.28 us
    pallas_call x1, Pallas kernels: 198 us -> 181 us  [extend_add(): pl.pallas_call(extend_kernel, out_shape=[jax.ShapeDtypeStruct(s, jnp.floa...]
    squeeze x18, local copies, waits for them, and re-layouts: 0.22 us -> 12.1 us  [pick(): lax.dynamic_index_in_dim(arrived[..., q * PANEL:(q + 1) * PANEL], owner,...]
    dynamic_slice x1, local copies, waits for them, and re-layouts: 0.38 us -> 6.25 us  [body(): lax.dynamic_slice_in_dim(assembled, off, PANEL, 1)]
    pallas_call x3, Pallas kernels: 79 us -> 73.7 us  [local_call(): pl.pallas_call(kernel, grid_spec=pltpu.PrefetchScalarGridSpec(num_scalar_...]
    unnamed x26 -> x32, local copies, waits for them, and re-layouts: 14.1 us -> 10.6 us
where the time goes in v5:
time: 430 us; the launch traced here: 429 us
  Pallas kernels  381 us (89%)
  local copies, waits for them, and re-layouts  42.4 us (10%)
    pallas_call x1, Pallas kernels, extend_add(): pl.pallas_call(extend_kernel, out_shape=[jax.ShapeDtypeStruct(s, jnp.floa...  181 us
    pallas_call x4, Pallas kernels, exchange(): pl.pallas_call(kernel, out_shape=[jax.ShapeDtypeStruct(m[4], jnp.float32)...  96.9 us
    pallas_call x3, Pallas kernels, local_call(): pl.pallas_call(kernel, grid_spec=pltpu.PrefetchScalarGridSpec(num_scalar_...  73.7 us
    pallas_call x1, Pallas kernels, spread(): pl.pallas_call(spread_kernel, out_shape=[jax.ShapeDtypeStruct(s, jnp.floa...  29.6 us
    squeeze x18, local copies, waits for them, and re-layouts, pick(): lax.dynamic_index_in_dim(arrived[..., q * PANEL:(q + 1) * PANEL], owner,...  12.1 us
    unnamed x32, local copies, waits for them, and re-layouts  10.6 us

profile of v5, /device:TPU:1, one launch (start us, length us, event | category | flops | bytes accessed | tf_op | source)
XLA Modules:
  0.0 428.7 jit_solution(14968936826647516940)
XLA Ops:
  1.3 2.2 copy-done
  3.4 29.6 %shard_map.59 = (f32[2048,512]{1,0:T(8,128)S(1)}, f32[512,512]{1,0:T(8,128)S(1)}, f32[512,512]{1,0:T(8,128)S(1)}) custom-call(f32[2048,512]{1,0:T(8,128)S(1)} %copy-done), custom_call_target="tpu_custom_call" | custom-call | tf_op jit(solution)/shard_map/pallas_call | solution.py:694
  33.1 2.0 copy-done.1
  35.1 1.0 copy-done.7
  36.1 1.0 copy-done.8
  37.1 27.0 %shard_map.60 = (f32[2048,512]{1,0:T(8,128)}, f32[4,2048,128]{2,1,0:T(8,128)}) custom-call(s32[10]{0:T(128)} %pad_add_fusion.tab, f32[2048,512]{1,0:T(8,128)} %front.3, f32[2048,512]{1,0:T(8,128)} %copy-done.1, f32[512,512]{1,0:T(8,128)} %copy-done.7, f32[512,512]{1,0:T(8,128)} %copy-done.8), custom_call_target="tpu_custom_call" | custom-call | tf_op jit(solution)/shard_map/pallas_call | solution.py:173
  64.3 0.7 pad_add_fusion.1.tab
  67.1 180.6 %shard_map.61 = (f32[32,16,768]{2,1,0:T(8,128)}, f32[32,16,768]{2,1,0:T(8,128)}, f32[32,16,768]{2,1,0:T(8,128)}, f32[32,16,768]{2,1,0:T(8,128)}, f32[8,24,16,128...) custom-call(s32[320]{0:T(512)} %broadcast_maximum_fusion.tab, ...), custom_call_target="tpu_custom_call" | custom-call | tf_op jit(solution)/shard_map/pallas_call | solution.py:360
  247.6 11.3 %shard_map.62 = f32[12,128,768]{2,1,0:T(8,128)} custom-call(s32[320]{0:T(512)} %copy-done.9, f32[12,128,768]{2,1,0:T(8,128)} %bitcast.119, f32[32,16,768]{2,1,0:T(8,128)} %get-tuple-element.39.refs_0_.refs_8_, f32[32,16,768]{2,1,0:T(8,128)} %get-tuple-element.40.refs_1_.refs_9_, f32[32,16,768]{2,1,0:T(8,128)} %get-tuple-element.41.refs_2_.refs_10_, ...), custom_call_target="tpu_custom_call" | custom-call | tf_op jit(solution)/shard_map/pallas_call | solution.py:173
  259.0 0.7 fusion.19
  259.7 6.3 %constant_dynamic-slice_fusion.14 = (f32[1536,256]{1,0:T(8,128)S(1)}, f32[1536,256]{1,0:T(8,128)S(1)}, f32[1536,256]{1,0:T(8,128)S(1)}) fusion(f32[1536,768]{1,0:T(8,128)} %bitcast.114, u32[]{:T(128)} %bitcast.14, u32[]{:T(128)} %bitcast.16, u32[]{:T(128)} %bitcast.15), kind=kLoop, calls=%fused_computation.69 | loop fusion | bytes 9437196 | tf_op jit(solution)/shard_map/dynamic_slice | solution.py:834
  266.3 0.7 fusion.17
  267.0 2.2 constant_dynamic-slice_fusion.11
  269.4 30.0 %shard_map.63 = (f32[4,192,768]{2,1,0:T(8,128)S(1)}, f32[4,192,768]{2,1,0:T(8,128)S(1)}, f32[8,3,32,768]{3,2,1,0:T(8,128)S(1)}) custom-call(f32[2,4,192,768]{3,2,1,0:T(8,128)S(1)} %bitcast.105, f32[2,4,192,768]{3,2,1,0:T(8,128)S(1)} %bitcast.106, f32[3,8,32,768]{3,2,1,0:T(8,128)S(1)} %pad_maximum_fusion.1.refs_2_), custom_call_target="tpu_custom_call" | custom-call | tf_op jit(solution)/shard_map/pallas_call | solution.py:109
  299.6 0.6 constant_dynamic-slice_fusion.6
  300.2 0.7 constant_dynamic-slice_fusion.7
  301.0 0.7 constant_dynamic-slice_fusion.8
  302.0 0.7 fusion.15
  302.6 0.6 constant_dynamic-slice_fusion.3
  303.3 0.7 constant_dynamic-slice_fusion.4
  304.0 0.7 constant_dynamic-slice_fusion.5
  305.6 0.7 dynamic-slice_bitcast_fusion.1
  306.3 0.6 dynamic-slice_bitcast_fusion.2
  307.0 2.1 constant_dynamic-slice_fusion.2
  309.2 18.3 %shard_map.64 = (f32[4,48,768]{2,1,0:T(8,128)S(1)}, f32[4,48,768]{2,1,0:T(8,128)S(1)}, f32[4,3,16,768]{3,2,1,0:T(8,128)S(1)}, f32[4,3,16,768]{3,2,1,0:T(8,128)S(1)}, f32[3,8,32,384]{3,2,1,0:T(8,128)S(1)}) custom-call(f32[4,48,768]{2,1,0:T(8,128)S(1)} %pad_maximum_fusion.2.refs_0_, f32[4,48,768]{2,1,0:T(8,128)S(1)} %pad_maximum_fusion.3.refs_1_, ...), custom_call_target="tpu_custom_call" | custom-call | tf_op jit(solution)/shard_map/pallas_call | solution.py:109
  327.5 0.6 dynamic-slice_bitcast_fusion.18
  328.2 0.7 dynamic-slice_bitcast_fusion.19
  328.9 0.7 dynamic-slice_bitcast_fusion.20
  329.6 0.6 dynamic-slice_bitcast_fusion.15
  330.3 0.7 dynamic-slice_bitcast_fusion.16
  331.0 0.7 dynamic-slice_bitcast_fusion.17
  332.4 0.7 dynamic-slice_bitcast_fusion.13
  333.1 0.7 dynamic-slice_bitcast_fusion.14
  333.9 0.6 dynamic-slice_bitcast_fusion.9
  334.6 0.7 dynamic-slice_bitcast_fusion.10
  335.3 0.7 dynamic-slice_bitcast_fusion.11
  336.0 18.5 %shard_map.65 = (f32[4,48,768]{2,1,0:T(8,128)S(1)}, f32[4,48,768]{2,1,0:T(8,128)S(1)}, f32[4,3,16,768]{3,2,1,0:T(8,128)S(1)}, f32[4,3,16,768]{3,2,1,0:T(8,128)S(1)}, f32[3,8,32,384]{3,2,1,0:T(8,128)S(1)}) custom-call(f32[48,768]{1,0:T(8,128)S(1)} %pad_maximum_fusion.6.refs_0_, f32[48,768]{1,0:T(8,128)S(1)} %pad_maximum_fusion.7.refs_1_, ...), custom_call_target="tpu_custom_call" | custom-call | tf_op jit(solution)/shard_map/pallas_call | solution.py:109
  354.6 0.6 dynamic-slice_bitcast_fusion.3
  355.2 0.7 dynamic-slice_bitcast_fusion.4
  355.9 0.7 dynamic-slice_bitcast_fusion.5
  356.7 0.6 dynamic-slice_bitcast_fusion.6
  357.4 0.7 dynamic-slice_bitcast_fusion.7
  358.1 0.7 dynamic-slice_bitcast_fusion.8
  358.8 30.2 %shard_map.66 = (f32[4,192,768]{2,1,0:T(8,128)S(1)}, f32[4,192,768]{2,1,0:T(8,128)S(1)}, f32[3,8,32,768]{3,2,1,0:T(8,128)S(1)}) custom-call(f32[192,768]{1,0:T(8,128)S(1)} %bitcast.112, f32[192,768]{1,0:T(8,128)S(1)} %bitcast.113, f32[3,32,768]{2,1,0:T(8,128)S(1)} %maximum_maximum_fusion.refs_2_), custom_call_target="tpu_custom_call" | custom-call | tf_op jit(solution)/shard_map/pallas_call | solution.py:109
  389.0 1.4 copy-done.2
  390.4 1.5 copy-done.3
  391.9 1.4 copy-done.4
  393.3 35.5 %shard_map.67 = f32[1536,768]{1,0:T(8,128)} custom-call(s32[9]{0:T(128)} %pad_add_fusion.1.tab, f32[1536,768]{1,0:T(8,128)} %bitcast.115, f32[768,768]{1,0:T(8,128)} %bitcast.107, f32[768,768]{1,0:T(8,128)} %bitcast.108, f32[768,384]{1,0:T(8,128)} %bitcast.110, f32[768,384]{1,0:T(8,128)} %bitcast.111, f32[768,768]{1,0:T(8,128)} %bitcast.109), custom_call_target="tpu_custom_call" | custom-call | tf_op jit(solution)/shard_map/pallas_call | solution.py:173
  (86 shorter events, 6.0 us)
Async XLA Ops:
  1.3 2.2 copy-start
  33.1 2.0 copy-start.1
  35.1 1.0 copy-start.7
  36.1 1.0 copy-start.8
  37.1 27.0 %copy-start.11 = (s32[3]{0:T(128)S(1)}, s32[3]{0:T(128)}, u32[]{:S(2)}) copy-start(s32[3]{0:T(128)} %param.13) | copy-start | bytes 40
  37.1 27.9 %copy-start.10 = (s32[2,60]{1,0:T(2,128)S(1)}, s32[2,60]{1,0:T(2,128)}, u32[]{:S(2)}) copy-start(s32[2,60]{1,0:T(2,128)} %param.12) | copy-start | bytes 1444
  66.5 181.2 %copy-start.9 = (s32[320]{0:T(512)}, s32[320]{0:T(512)S(1)}, u32[]{:S(2)}) copy-start(s32[320]{0:T(512)S(1)} %sub.69.tab) | copy-start | bytes 3844
  259.7 7.3 %slice-start = ((s8[4718592]{0:T(1024)(128)(4,1)}), s8[4194304]{0:T(1024)(128)(4,1)S(1)}, s32[]{:S(2)}) async-start(s8[4718592]{0:T(1024)(128)(4,1)} %bitcast.116), calls=%async_computation | async-start | bytes 8388608
  265.9 1.0 slice-start.1
  327.5 4.3 %copy-start.5 = (f32[3,8,32,384]{3,2,1,0:T(8,128)}, f32[3,8,32,384]{3,2,1,0:T(8,128)S(1)}, u32[]{:S(2)}) copy-start(f32[3,8,32,384]{3,2,1,0:T(8,128)S(1)} %get-tuple-element.60) | copy-start | bytes 3538948
  354.5 4.2 copy-start.6
  389.0 1.4 copy-start.2
  390.4 1.5 copy-start.3
  391.9 1.4 copy-start.4

commit v6 on v5

--- a/solution.py
+++ b/solution.py
@@ -31,96 +31,6 @@
         me = lax.rem(y, 2) * 2 + core
         return me, 4, lambda p: {"y": pair + p // 2, "core": lax.rem(p, 2)}
     return lax.axis_index(axes), 4, lambda p: {axes: p}
-
-
-def swap(array, axes):
-    return (array, axes, lambda ref, p: ref.at[p], lambda ref, p: ref.at[p], array.shape, array.shape[1:])
-
-
-def swap_inner(array, axes):
-    shape = (array.shape[1], array.shape[0]) + array.shape[2:]
-    return (array, axes, lambda ref, p: ref.at[:, p], lambda ref, p: ref.at[p], shape, shape[1:])
-
-
-def swap_half(array, axes, half):
-    return (
-        array, axes, lambda ref, p: ref.at[half, p], lambda ref, p: ref.at[p], array.shape[1:],
-        array.shape[2:],
-    )
-
-
-def share(array, axes, size):
-    return (
-        array, axes, lambda ref, p: ref, lambda ref, p: ref.at[p], (size,) + array.shape, array.shape
-    )
-
-
-def share_inner(array, axes, size):
-    shape = (array.shape[0], size) + array.shape[1:]
-    return (array, axes, lambda ref, p: ref, lambda ref, p: ref.at[:, p], shape, array.shape)
-
-
-def exchange(moves, collective_id):
-    n = len(moves)
-    greeted = list(dict.fromkeys(m[1] for m in moves))
-
-    def kernel(*refs):
-        ins, outs = refs[:n], refs[n : 2 * n]
-        send_sem, recv_sem, own_sem = refs[2 * n : 2 * n + 3]
-        stages = refs[2 * n + 3 :]
-        barrier = pltpu.get_barrier_semaphore()
-        total = 0
-        for ax in greeted:
-            me, size, ident = peers_of(ax)
-            for d in range(1, size):
-                pl.semaphore_signal(
-                    barrier, inc=1, device_id=ident(lax.rem(me + d, size)), device_id_type=MESH
-                )
-            total += size - 1
-        loads, stores = [], []
-        for i, (_, ax, src, dst, _, _) in enumerate(moves):
-            me = peers_of(ax)[0]
-            loads.append(pltpu.make_async_copy(src(ins[i], me), stages[i], own_sem.at[i]))
-            stores.append(pltpu.make_async_copy(stages[i], dst(outs[i], me), own_sem.at[i]))
-        for copy in loads:
-            copy.start()
-        pl.semaphore_wait(barrier, total)
-        copies = []
-        for i, (_, ax, src, dst, _, _) in enumerate(moves):
-            me, size, ident = peers_of(ax)
-            for d in sorted(range(1, size), key=lambda d: -min(d, size - d)):
-                p = lax.rem(me + d, size)
-                copy = pltpu.make_async_remote_copy(
-                    src_ref=src(ins[i], p),
-                    dst_ref=dst(outs[i], me),
-                    send_sem=send_sem.at[i, d],
-                    recv_sem=recv_sem.at[i, d],
-                    device_id=ident(p),
-                    device_id_type=MESH,
-                )
-                copy.start()
-                copies.append(copy)
-        for load, store in zip(loads, stores):
-            load.wait()
-            store.start()
-        for copy in stores + copies:
-            copy.wait()
-
-    return pl.pallas_call(
-        kernel,
-        out_shape=[jax.ShapeDtypeStruct(m[4], jnp.float32) for m in moves],
-        in_specs=[pl.BlockSpec(memory_space=pl.ANY)] * n,
-        out_specs=[pl.BlockSpec(memory_space=pl.ANY)] * n,
-        scratch_shapes=[
-            pltpu.SemaphoreType.DMA((n, 8)),
-            pltpu.SemaphoreType.DMA((n, 8)),
-            pltpu.SemaphoreType.DMA((n,)),
-            *[pltpu.VMEM(m[5], jnp.float32) for m in moves],
-        ],
-        compiler_params=pltpu.CompilerParams(
-            collective_id=collective_id, has_side_effects=True, vmem_limit_bytes=32 * 1024 * 1024
-        ),
-    )(*[m[0] for m in moves])
 
 
 def rank_in(key, group, valid):
@@ -388,59 +298,147 @@
     return assembled.reshape(root_front.shape)
 
 
-def pick(arrived, owners):
-    parts = [
-        lax.dynamic_index_in_dim(arrived[..., q * PANEL : (q + 1) * PANEL], owner, 0, keepdims=False)
-        for q, owner in enumerate(owners)
+def gather_kernel(tab, cols, rows, upper, lower, rows_out, cross_out, *refs):
+    (arrived_a, arrived_b, arrived_rows, mine, mine_blocks, cross_a, cross_b, cross_a1, cross_b1,
+     cross_a2, cross_b2, cross_a3, cross_b3, cross_all, a1, b1, a2, b2, a3, b3, a4, b4) = refs[:-3]
+    send_sem, recv_sem, own_sem = refs[-3:]
+    barrier = pltpu.get_barrier_semaphore()
+    total = 0
+    for ax in ("z", "x", ROW):
+        me, size, ident = peers_of(ax)
+        for d in range(1, size):
+            pl.semaphore_signal(
+                barrier, inc=1, device_id=ident(lax.rem(me + d, size)), device_id_type=MESH
+            )
+        total += size - 1
+    started = []
+
+    def send(number, src, dst, axes):
+        me, size, ident = peers_of(axes)
+        own = pltpu.make_async_copy(src(me), dst(me), own_sem.at[number])
+        own.start()
+        copies = []
+        for d in sorted(range(1, size), key=lambda d: -min(d, size - d)):
+            p = lax.rem(me + d, size)
+            copy = pltpu.make_async_remote_copy(
+                src_ref=src(p),
+                dst_ref=dst(me),
+                send_sem=send_sem.at[number, d],
+                recv_sem=recv_sem.at[number, d],
+                device_id=ident(p),
+                device_id_type=MESH,
+            )
+            copy.start()
+            copies.append(copy)
+        started.extend(copies)
+        return own, copies
+
+    def arrive(*transfers):
+        for own, copies in transfers:
+            own.wait()
+            for copy in copies:
+                copy.wait_recv()
+
+    def slot(ref):
+        return lambda p: ref.at[p]
+
+    def inner(ref):
+        return lambda p: ref.at[:, p]
+
+    def same(ref):
+        return lambda p: ref
+
+    owner_x = [tab[k] for k in range(RPAN)]
+    owner_z = [tab[RPAN + k] for k in range(RPAN)]
+    owner_row = [tab[2 * RPAN + k] for k in range(RPAN)]
+    owned = [tab[3 * RPAN + k] for k in range(RPAN)]
+
+    pl.semaphore_wait(barrier, total)
+    t_rows = send(0, inner(rows), slot(arrived_rows), ROW)
+    t_a = send(1, lambda p: cols.at[0, p], slot(arrived_a), "z")
+    t_b = send(2, lambda p: cols.at[1, p], slot(arrived_b), "x")
+
+    arrive(t_rows)
+    for k in range(RPAN):
+        mine[k] = arrived_rows[owner_row[k], k]
+        for j in range(3):
+            mine_blocks[j, k] = arrived_rows[owner_row[k], k, :, panel(j)]
+    half = mine.shape[1] // 2
+    for q in range(RPAN):
+        block = mine_blocks[owned[q]]
+        cross_a[:, :, panel(q)] = block[:, :half]
+        cross_b[:, :, panel(q)] = block[:, half:]
+    t_cross_a = send(3, same(cross_a), slot(cross_a1), "z")
+    t_cross_b = send(4, same(cross_b), slot(cross_b1), "x")
+    t_mine = send(5, same(mine), inner(rows_out), ROW)
+
+    piece = a1.shape[1]
+
+    def split(transfer, arrived, owners, out):
+        arrive(transfer)
+        for q in range(RPAN):
+            for p in range(4):
+                out[p, :, panel(q)] = arrived[owners[q], p * piece : (p + 1) * piece, panel(q)]
+
+    def select(transfer, arrived, owners, out):
+        arrive(transfer)
+        for q in range(RPAN):
+            out[..., panel(q)] = arrived[owners[q], ..., panel(q)]
+
+    split(t_a, arrived_a, owner_z, a1)
+    t_a = send(6, slot(a1), slot(a2), "x")
+    split(t_b, arrived_b, owner_x, b1)
+    t_b = send(7, slot(b1), slot(b2), "z")
+    select(t_cross_a, cross_a1, owner_z, cross_a2)
+    t_cross_a = send(8, same(cross_a2), slot(cross_a3), "x")
+    select(t_cross_b, cross_b1, owner_x, cross_b2)
+    t_cross_b = send(9, same(cross_b2), slot(cross_b3), "z")
+    select(t_a, a2, owner_x, a3)
+    t_a = send(10, same(a3), slot(a4), "x")
+    select(t_b, b2, owner_z, b3)
+    t_b = send(11, same(b3), slot(b4), "z")
+    arrive(t_cross_a, t_cross_b)
+    for q in range(RPAN):
+        cross_all[:, :half, panel(q)] = cross_a3[owner_x[q], :, :, panel(q)]
+        cross_all[:, half:, panel(q)] = cross_b3[owner_z[q], :, :, panel(q)]
+    t_cross = send(12, same(cross_all), inner(cross_out), ROW)
+    arrive(t_a)
+    t_a = send(13, same(a4), slot(upper), "z")
+    arrive(t_b)
+    t_b = send(14, same(b4), slot(lower), "x")
+    arrive(t_mine, t_cross, t_a, t_b)
+    for copy in started:
+        copy.wait_send()
+
+
+def gather_bands(cols, rows, table, collective_id):
+    count, width = cols.shape
+    piece, span = PANEL // 8, rows.shape[2]
+    band, ring = (RPAN, 8, piece, span), (4, count // 8, width)
+    small, cross = (4, count // 32, width), (RPAN, piece // 2, width)
+    full = (4,) + small
+    buffers = [
+        ring, ring, (8, RPAN, piece, span), (RPAN, piece, span), (3, RPAN, piece, PANEL),
+        cross, cross, (4,) + cross, (4,) + cross, cross, cross, (4,) + cross, (4,) + cross,
+        (RPAN, piece, width), small, small, small, small, small[1:], small[1:], small, small,
     ]
-    return jnp.concatenate(parts, axis=-1)
-
-
-def gather_bands(cols, rows, col_off, xs, zs, row_owners, axes, size, first_id):
-    count, width = cols.shape
-    panels, _, span = rows.shape
-    piece = PANEL // size
-    cols = cols.reshape(2, 4, count // 8, width)
-    rows = rows.reshape(panels, size, piece, span)
-    first, second, slices = exchange(
-        [swap_half(cols, "z", 0), swap_half(cols, "x", 1), swap_inner(rows, axes)], first_id
-    )
-    first, second = pick(first, zs), pick(second, xs)
-    slices = jnp.stack(
-        [lax.dynamic_index_in_dim(slices[:, k], owner, 0, keepdims=False) for k, owner in enumerate(row_owners)]
-    )
-    cross = jnp.concatenate(
-        [lax.dynamic_slice_in_dim(slices, off, PANEL, 2) for off in col_off], axis=2
-    )
-    split = lambda a: a.reshape(4, count // 32, width)
-    half = span // 2
-    first, second, upper, lower, left = exchange(
-        [
-            swap(split(first), "x"), swap(split(second), "z"),
-            share(cross[:, : piece // 2], "z", 4), share(cross[:, piece // 2 :], "x", 4),
-            share_inner(slices[..., :half], axes, size),
+    upper, lower, pivot_rows, cross = pl.pallas_call(
+        gather_kernel,
+        out_shape=[jax.ShapeDtypeStruct(s, jnp.float32) for s in (full, full, band, band)],
+        in_specs=[pl.BlockSpec(memory_space=pltpu.SMEM)] + [pl.BlockSpec(memory_space=pl.ANY)] * 2,
+        out_specs=[pl.BlockSpec(memory_space=pl.ANY)] * 4,
+        scratch_shapes=[
+            *[pltpu.VMEM(s, jnp.float32) for s in buffers],
+            pltpu.SemaphoreType.DMA((15, 8)),
+            pltpu.SemaphoreType.DMA((15, 8)),
+            pltpu.SemaphoreType.DMA((15,)),
         ],
-        first_id + 1,
-    )
-    first, second = pick(first, xs), pick(second, zs)
-    upper, lower = pick(upper, zs), pick(lower, xs)
-    first, second, upper, lower, right = exchange(
-        [
-            share(first, "x", 4), share(second, "z", 4),
-            share(upper, "x", 4), share(lower, "z", 4),
-            share_inner(slices[..., half:], axes, size),
-        ],
-        first_id + 2,
-    )
-    cross = jnp.concatenate([pick(upper, xs), pick(lower, zs)], axis=1)
-    join = lambda a: a.reshape(count // 8, width)
-    first, second, cross = exchange(
-        [share(join(first), "z", 4), share(join(second), "x", 4), share_inner(cross, axes, size)],
-        first_id + 3,
-    )
-    halves = [a.reshape(count // 2, width) for a in (first, second)]
-    left, right = (a.reshape(width, half) for a in (left, right))
-    return halves, left, right, cross.reshape(width, width)
+        compiler_params=pltpu.CompilerParams(
+            collective_id=collective_id, has_side_effects=True, vmem_limit_bytes=40 * 1024 * 1024
+        ),
+    )(table, cols.reshape(2, 4, count // 8, width), rows.reshape(band))
+    halves = [a.reshape(count // 2, width) for a in (upper, lower)]
+    return halves, pivot_rows.reshape(width, span), cross.reshape(width, width)
 
 
 PARENT = {
@@ -829,13 +827,15 @@
     each = lambda a: [a[k] for k in range(RPAN)]
     col_off = each(order % col_panels * PANEL)
     row_off = each(order % row_panels * PANEL)
-    owner_x, owner_z = each(order // (4 * col_panels)), each(order // col_panels % 4)
-    owner_row = each(order // row_panels)
+    table = jnp.concatenate(
+        [
+            order // (4 * col_panels), order // col_panels % 4, order // row_panels,
+            order % col_panels,
+        ]
+    ).astype(jnp.int32)
     cols = jnp.concatenate([lax.dynamic_slice_in_dim(assembled, off, PANEL, 1) for off in col_off], 1)
     rows = jnp.stack([lax.dynamic_slice_in_dim(assembled, off, PANEL, 0) for off in row_off])
-    halves, left, right, cross = gather_bands(
-        cols, rows, col_off, owner_x, owner_z, owner_row, ROW, 8, 20,
-    )
+    halves, pivot_rows, cross = gather_bands(cols, rows, table, 20)
 
     def steps(places):
         match = places[:, None] == panel_order[None, :]
@@ -843,7 +843,7 @@
 
     row_step = steps(r * row_panels + jnp.arange(row_panels))
     col_step = steps(o * col_panels + jnp.arange(col_panels))
-    return factored, finish(assembled, halves, [left, right], cross, row_step, col_step, HIGH)[0]
+    return factored, finish(assembled, halves, [pivot_rows], cross, row_step, col_step, HIGH)[0]
 
 
 def solution(mesh):

time: 430 us -> 404 us (0.940)
  local copies, waits for them, and re-layouts: 42.4 us -> 21.6 us
  Pallas kernels: 381 us -> 372 us
  other arithmetic: 4.13 us -> 8.86 us
    squeeze x18 -> x0, local copies, waits for them, and re-layouts: 12.1 us -> none  [pick(): lax.dynamic_index_in_dim(arrived[..., q * PANEL:(q + 1) * PANEL], owner,...]
    pallas_call x4 -> x1, Pallas kernels: 96.9 us -> 88.5 us  [gather_bands(): pl.pallas_call(gather_kernel, out_shape=[jax.ShapeDtypeStruct(s, jnp.floa...]
    dynamic_slice x10 -> x0, local copies, waits for them, and re-layouts: 8.16 us -> none  [the longest x6 4.09 us: pick(): lax.dynamic_index_in_dim(arrived[..., q * PANEL:(q + 1) * PANEL], owner,...]
    unnamed x32 -> x24, local copies, waits for them, and re-layouts: 10.6 us -> 14.1 us
where the time goes in v6:
time: 404 us; the launch traced here: 403 us
  Pallas kernels  372 us (92%)
  local copies, waits for them, and re-layouts  21.6 us (5%)
  other arithmetic  8.86 us (2%)
    pallas_call x1, Pallas kernels, extend_add(): pl.pallas_call(extend_kernel, out_shape=[jax.ShapeDtypeStruct(s, jnp.floa...  181 us
    pallas_call x1, Pallas kernels, gather_bands(): pl.pallas_call(gather_kernel, out_shape=[jax.ShapeDtypeStruct(s, jnp.floa...  88.5 us
    pallas_call x3, Pallas kernels, local_call(): pl.pallas_call(kernel, grid_spec=pltpu.PrefetchScalarGridSpec(num_scalar_...  73.4 us
    pallas_call x1, Pallas kernels, spread(): pl.pallas_call(spread_kernel, out_shape=[jax.ShapeDtypeStruct(s, jnp.floa...  29.6 us
    unnamed x24, local copies, waits for them, and re-layouts  14.1 us

profile of v6, /device:TPU:1, one launch (start us, length us, event | category | flops | bytes accessed | tf_op | source)
XLA Modules:
  0.0 403.4 jit_solution(16239351103824440652)
XLA Ops:
  0.7 0.7 select_reduce_fusion.2
  1.4 0.6 pad_add_fusion.tab
  2.1 0.8 select_reduce_fusion.1
  2.9 0.6 pad_add_fusion.1.tab
  3.6 0.7 fusion.1
  4.3 0.1 constant_dynamic-update-slice_fusion.3
  4.4 0.1 constant_dynamic-update-slice_fusion.2
  4.6 0.7 remainder_multiply_fusion
  5.2 0.1 add_convert_fusion.tab
  5.3 0.7 fusion.4
  5.9 0.1 broadcast_compare_fusion.1
  6.0 0.1 iota_compare_fusion.1
  6.1 0.3 convert_reduce_fusion
  6.4 0.1 constant_dynamic-update-slice_fusion.7
  6.5 0.1 constant_dynamic-update-slice_fusion.6
  6.6 0.1 constant_dynamic-update-slice_fusion.5
  6.7 0.3 select_reduce_fusion
  7.0 0.1 sub.69.tab
  7.1 0.0 copy-start.9
  7.1 0.6 broadcast_maximum_fusion.tab
  7.7 0.0 copy-start
  7.7 2.2 copy-done
  9.8 29.6 %shard_map.59 = (f32[2048,512]{1,0:T(8,128)S(1)}, f32[512,512]{1,0:T(8,128)S(1)}, f32[512,512]{1,0:T(8,128)S(1)}) custom-call(f32[2048,512]{1,0:T(8,128)S(1)} %copy-done), custom_call_target="tpu_custom_call" | custom-call | tf_op jit(solution)/shard_map/pallas_call | solution.py:692
  39.5 0.0 copy-start.1
  39.5 2.0 copy-done.1
  41.5 0.0 copy-start.6
  41.5 1.0 copy-done.6
  42.5 0.0 copy-start.7
  42.5 1.0 copy-done.7
  43.5 26.8 %shard_map.60 = (f32[2048,512]{1,0:T(8,128)}, f32[4,2048,128]{2,1,0:T(8,128)}) custom-call(s32[10]{0:T(128)} %pad_add_fusion.tab, f32[2048,512]{1,0:T(8,128)} %front.3, f32[2048,512]{1,0:T(8,128)} %copy-done.1, f32[512,512]{1,0:T(8,128)} %copy-done.6, f32[512,512]{1,0:T(8,128)} %copy-done.7), custom_call_target="tpu_custom_call" | custom-call | tf_op jit(solution)/shard_map/pallas_call | solution.py:83
  70.2 0.0 copy-done.9
  70.2 180.6 %shard_map.61 = (f32[32,16,768]{2,1,0:T(8,128)}, f32[32,16,768]{2,1,0:T(8,128)}, f32[32,16,768]{2,1,0:T(8,128)}, f32[32,16,768]{2,1,0:T(8,128)}, f32[8,24,16,128...) custom-call(s32[320]{0:T(512)} %broadcast_maximum_fusion.tab, ...), custom_call_target="tpu_custom_call" | custom-call | tf_op jit(solution)/shard_map/pallas_call | solution.py:270
  250.8 11.1 %shard_map.62 = f32[12,128,768]{2,1,0:T(8,128)} custom-call(s32[320]{0:T(512)} %copy-done.9, f32[12,128,768]{2,1,0:T(8,128)} %bitcast.53, f32[32,16,768]{2,1,0:T(8,128)} %get-tuple-element.27.refs_0_.refs_8_, f32[32,16,768]{2,1,0:T(8,128)} %get-tuple-element.28.refs_1_.refs_9_, f32[32,16,768]{2,1,0:T(8,128)} %get-tuple-element.29.refs_2_.refs_10_, ...), custom_call_target="tpu_custom_call" | custom-call | tf_op jit(solution)/shard_map/pallas_call | solution.py:83
  262.0 3.7 constant_dynamic-slice_fusion.2
  265.7 0.0 copy-start.8
  265.7 0.2 pad_maximum_fusion.1.rows
  265.9 2.1 copy-done.8
  268.0 3.1 constant_dynamic-slice_fusion.5
  271.1 2.5 pad_maximum_fusion
  273.6 88.5 %shard_map.63 = (f32[4,4,48,768]{3,2,1,0:T(8,128)S(1)}, f32[4,4,48,768]{3,2,1,0:T(8,128)S(1)}, f32[3,8,32,768]{3,2,1,0:T(8,128)S(1)}, f32[3,8,32,768]{3,2,1,0:T(8,128)S(1)}) custom-call(s32[12]{0:T(128)S(1)} %add_convert_fusion.tab, f32[2,4,192,768]{3,2,1,0:T(8,128)} %bitcast.52, f32[3,8,32,768]{3,2,1,0:T(8,128)S(1)} %pad_maximum_fusion.1.rows), custom_call_target="tpu_custom_call" | custom-call | tf_op jit(solution)/shard_map/pallas_call | solution.py:425
  362.1 0.0 copy-start.2
  362.1 1.4 copy-done.2
  363.5 0.0 copy-start.3
  363.5 1.5 copy-done.3
  365.0 0.0 copy-start.4
  365.0 1.4 copy-done.4
  366.4 1.5 copy-done.5
  367.9 35.5 %shard_map.64 = f32[1536,768]{1,0:T(8,128)} custom-call(s32[9]{0:T(128)} %pad_add_fusion.1.tab, f32[1536,768]{1,0:T(8,128)} %bitcast.50, f32[768,768]{1,0:T(8,128)} %bitcast.45, f32[768,768]{1,0:T(8,128)} %bitcast.46, f32[768,768]{1,0:T(8,128)} %bitcast.47, f32[768,768]{1,0:T(8,128)} %bitcast.48), custom_call_target="tpu_custom_call" | custom-call | tf_op jit(solution)/shard_map/pallas_call | solution.py:83
  (25 shorter events, 0.2 us)
Async XLA Ops:
  7.1 63.2 %copy-start.9 = (s32[320]{0:T(512)}, s32[320]{0:T(512)S(1)}, u32[]{:S(2)}) copy-start(s32[320]{0:T(512)S(1)} %sub.69.tab) | copy-start | bytes 3844
  7.7 2.2 copy-start
  39.5 2.0 copy-start.1
  41.5 1.0 copy-start.6
  42.5 1.0 copy-start.7
  265.7 2.3 copy-start.8
  362.1 1.4 copy-start.2
  363.5 1.5 copy-start.3
  365.0 1.4 copy-start.4
  366.4 1.5 copy-start.5

commit v7 on v6

--- a/solution.py
+++ b/solution.py
@@ -87,7 +87,7 @@
             scratch_shapes=list(scratch),
         ),
         out_shape=[jax.ShapeDtypeStruct(s, jnp.float32) for s in out_shapes],
-        compiler_params=pltpu.CompilerParams(vmem_limit_bytes=56 * 1024 * 1024),
+        compiler_params=pltpu.CompilerParams(vmem_limit_bytes=62 * 1024 * 1024),
     )(table, *operands)
 
 
@@ -281,7 +281,7 @@
             pltpu.SemaphoreType.DMA((6 * PARTS,)),
         ],
         compiler_params=pltpu.CompilerParams(
-            collective_id=1, has_side_effects=True, vmem_limit_bytes=58 * 1024 * 1024
+            collective_id=1, has_side_effects=True, vmem_limit_bytes=62 * 1024 * 1024
         ),
     )(jnp.maximum(table, 0), front.reshape(4, 16, BLK, BLK))
     operands, specs = [], []
@@ -434,7 +434,7 @@
             pltpu.SemaphoreType.DMA((15,)),
         ],
         compiler_params=pltpu.CompilerParams(
-            collective_id=collective_id, has_side_effects=True, vmem_limit_bytes=40 * 1024 * 1024
+            collective_id=collective_id, has_side_effects=True, vmem_limit_bytes=62 * 1024 * 1024
         ),
     )(table, cols.reshape(2, 4, count // 8, width), rows.reshape(band))
     halves = [a.reshape(count // 2, width) for a in (upper, lower)]
@@ -699,7 +699,7 @@
             dma((U_PARTS,)), dma((2, U_PARTS)), dma((3,)), pltpu.VMEM(front.shape, jnp.float32),
         ],
         compiler_params=pltpu.CompilerParams(
-            collective_id=collective_id, has_side_effects=True, vmem_limit_bytes=32 * 1024 * 1024
+            collective_id=collective_id, has_side_effects=True, vmem_limit_bytes=62 * 1024 * 1024
         ),
     )(front)
 

time: 404 us -> 397 us (0.983)
  local copies, waits for them, and re-layouts: 21.6 us -> 9.1 us
    unnamed x24 -> x8, local copies, waits for them, and re-layouts: 14.1 us -> 1.53 us
where the time goes in v7:
time: 397 us; the launch traced here: 396 us
  Pallas kernels  375 us (94%)
  other arithmetic  10.8 us (3%)
  local copies, waits for them, and re-layouts  9.1 us (2%)
    pallas_call x1, Pallas kernels, extend_add(): pl.pallas_call(extend_kernel, out_shape=[jax.ShapeDtypeStruct(s, jnp.floa...  183 us
    pallas_call x1, Pallas kernels, gather_bands(): pl.pallas_call(gather_kernel, out_shape=[jax.ShapeDtypeStruct(s, jnp.floa...  88 us
    pallas_call x3, Pallas kernels, local_call(): pl.pallas_call(kernel, grid_spec=pltpu.PrefetchScalarGridSpec(num_scalar_...  73.8 us
    pallas_call x1, Pallas kernels, spread(): pl.pallas_call(spread_kernel, out_shape=[jax.ShapeDtypeStruct(s, jnp.floa...  31.1 us

profile of v7, /device:TPU:1, one launch (start us, length us, event | category | flops | bytes accessed | tf_op | source)
XLA Modules:
  0.0 396.2 jit_solution(22837523386197329)
XLA Ops:
  0.7 0.7 select_reduce_fusion.2
  1.4 0.6 pad_add_fusion.tab
  2.1 0.8 select_reduce_fusion.1
  2.9 0.6 pad_add_fusion.1.tab
  3.6 0.7 fusion.1
  4.3 0.1 constant_dynamic-update-slice_fusion.3
  4.4 0.1 constant_dynamic-update-slice_fusion.2
  4.5 0.7 remainder_multiply_fusion
  5.2 0.7 add_convert_fusion.tab
  5.8 0.7 fusion.4
  6.5 0.1 broadcast_compare_fusion.1
  6.6 0.1 iota_compare_fusion.1
  6.7 0.3 convert_reduce_fusion
  7.0 0.1 constant_dynamic-update-slice_fusion.7
  7.1 0.1 constant_dynamic-update-slice_fusion.6
  7.2 0.1 constant_dynamic-update-slice_fusion.5
  7.3 0.3 select_reduce_fusion
  7.5 0.1 sub.69.tab
  7.6 0.0 copy-start.1
  7.6 0.6 broadcast_maximum_fusion.tab
  8.2 31.1 %shard_map.59 = (f32[2048,512]{1,0:T(8,128)}, f32[512,512]{1,0:T(8,128)}, f32[512,512]{1,0:T(8,128)}) custom-call(f32[2048,512]{1,0:T(8,128)} %front.3), custom_call_target="tpu_custom_call" | custom-call | tf_op jit(solution)/shard_map/pallas_call | solution.py:692
  39.3 26.8 %shard_map.60 = (f32[2048,512]{1,0:T(8,128)}, f32[4,2048,128]{2,1,0:T(8,128)}) custom-call(s32[10]{0:T(128)} %pad_add_fusion.tab, f32[2048,512]{1,0:T(8,128)} %front.3, f32[2048,512]{1,0:T(8,128)} %get-tuple-element.22.refs_0_, f32[512,512]{1,0:T(8,128)} %get-tuple-element.23.refs_1_, f32[512,512]{1,0:T(8,128)} %get-tuple-element.24.refs_2_), custom_call_target="tpu_custom_call" | custom-call | tf_op jit(solution)/shard_map/pallas_call | solution.py:83
  66.1 0.0 copy-done.1
  66.1 182.6 %shard_map.61 = (f32[32,16,768]{2,1,0:T(8,128)}, f32[32,16,768]{2,1,0:T(8,128)}, f32[32,16,768]{2,1,0:T(8,128)}, f32[32,16,768]{2,1,0:T(8,128)}, f32[8,24,16,128...) custom-call(s32[320]{0:T(512)} %broadcast_maximum_fusion.tab, ...), custom_call_target="tpu_custom_call" | custom-call | tf_op jit(solution)/shard_map/pallas_call | solution.py:270
  248.7 11.5 %shard_map.62 = f32[12,128,768]{2,1,0:T(8,128)} custom-call(s32[320]{0:T(512)} %copy-done.1, f32[12,128,768]{2,1,0:T(8,128)} %bitcast.49, f32[32,16,768]{2,1,0:T(8,128)} %get-tuple-element.27.refs_0_.refs_8_, f32[32,16,768]{2,1,0:T(8,128)} %get-tuple-element.28.refs_1_.refs_9_, f32[32,16,768]{2,1,0:T(8,128)} %get-tuple-element.29.refs_2_.refs_10_, ...), custom_call_target="tpu_custom_call" | custom-call | tf_op jit(solution)/shard_map/pallas_call | solution.py:83
  260.2 3.8 constant_dynamic-slice_fusion.2
  263.9 0.0 copy-start
  263.9 1.7 pad_maximum_fusion.1.rows
  265.6 1.5 copy-done
  267.1 3.1 constant_dynamic-slice_fusion.5
  270.2 2.5 pad_maximum_fusion
  272.7 88.0 %shard_map.63 = (f32[4,4,48,768]{3,2,1,0:T(8,128)}, f32[4,4,48,768]{3,2,1,0:T(8,128)}, f32[3,8,32,768]{3,2,1,0:T(8,128)}, f32[3,8,32,768]{3,2,1,0:T(8,128)}) custom-call(s32[12]{0:T(128)} %add_convert_fusion.tab, f32[2,4,192,768]{3,2,1,0:T(8,128)} %bitcast.48, f32[3,8,32,768]{3,2,1,0:T(8,128)} %pad_maximum_fusion.1.rows), custom_call_target="tpu_custom_call" | custom-call | tf_op jit(solution)/shard_map/pallas_call | solution.py:425
  360.7 35.5 %shard_map.64 = f32[1536,768]{1,0:T(8,128)} custom-call(s32[9]{0:T(128)} %pad_add_fusion.1.tab, f32[1536,768]{1,0:T(8,128)} %bitcast.46, f32[768,768]{1,0:T(8,128)} %bitcast.54, f32[768,768]{1,0:T(8,128)} %bitcast.55, f32[768,768]{1,0:T(8,128)} %bitcast.56, f32[768,768]{1,0:T(8,128)} %bitcast.57), custom_call_target="tpu_custom_call" | custom-call | tf_op jit(solution)/shard_map/pallas_call | solution.py:83
  (24 shorter events, 0.2 us)
Async XLA Ops:
  7.6 58.5 %copy-start.1 = (s32[320]{0:T(512)}, s32[320]{0:T(512)S(1)}, u32[]{:S(2)}) copy-start(s32[320]{0:T(512)S(1)} %sub.69.tab) | copy-start | bytes 3844
  263.9 3.2 copy-start

commit v8 on v7

--- a/solution.py
+++ b/solution.py
@@ -298,6 +298,11 @@
     return assembled.reshape(root_front.shape)
 
 
+def copy_bands(tab, col_in, row_in, col_out, row_out):
+    col_out[...] = col_in[...]
+    row_out[0] = row_in[...]
+
+
 def gather_kernel(tab, cols, rows, upper, lower, rows_out, cross_out, *refs):
     (arrived_a, arrived_b, arrived_rows, mine, mine_blocks, cross_a, cross_b, cross_a1, cross_b1,
      cross_a2, cross_b2, cross_a3, cross_b3, cross_all, a1, b1, a2, b2, a3, b3, a4, b4) = refs[:-3]
@@ -824,17 +829,21 @@
 
     row_panels, col_panels = 6, 3
     order = panel_order.astype(jnp.uint32)
-    each = lambda a: [a[k] for k in range(RPAN)]
-    col_off = each(order % col_panels * PANEL)
-    row_off = each(order % row_panels * PANEL)
     table = jnp.concatenate(
         [
             order // (4 * col_panels), order // col_panels % 4, order // row_panels,
-            order % col_panels,
+            order % col_panels, order % row_panels,
         ]
     ).astype(jnp.int32)
-    cols = jnp.concatenate([lax.dynamic_slice_in_dim(assembled, off, PANEL, 1) for off in col_off], 1)
-    rows = jnp.stack([lax.dynamic_slice_in_dim(assembled, off, PANEL, 0) for off in row_off])
+    cols, rows = local_call(
+        copy_bands, RPAN, table, (assembled, assembled),
+        [
+            pl.BlockSpec((1536, PANEL), lambda k, tab: (0, tab[3 * RPAN + k])),
+            pl.BlockSpec((PANEL, 768), lambda k, tab: (tab[4 * RPAN + k], 0)),
+        ],
+        [(1536, RPAN * PANEL), (RPAN, PANEL, 768)],
+        [pl.BlockSpec((1536, PANEL), lambda k, tab: (0, k)), part((PANEL, 768))],
+    )
     halves, pivot_rows, cross = gather_bands(cols, rows, table, 20)
 
     def steps(places):

time: 397 us -> 391 us (0.985)
  local copies, waits for them, and re-layouts: 9.1 us -> 0.19 us
  Pallas kernels: 375 us -> 383 us
  other arithmetic: 10.8 us -> 6.59 us
    pallas_call x3 -> x4, Pallas kernels: 73.8 us -> 81.2 us  [local_call(): pl.pallas_call(kernel, grid_spec=pltpu.PrefetchScalarGridSpec(num_scalar_...]
    dynamic_slice x2 -> x0, local copies, waits for them, and re-layouts: 6.82 us -> none  [the longest x1 3.76 us: body(): lax.dynamic_slice_in_dim(assembled, off, PANEL, 0)]
where the time goes in v8:
time: 391 us
  Pallas kernels  383 us (98%)
  other arithmetic  6.59 us (2%)
    pallas_call x1, Pallas kernels, extend_add(): pl.pallas_call(extend_kernel, out_shape=[jax.ShapeDtypeStruct(s, jnp.floa...  183 us
    pallas_call x1, Pallas kernels, gather_bands(): pl.pallas_call(gather_kernel, out_shape=[jax.ShapeDtypeStruct(s, jnp.floa...  88.3 us
    pallas_call x4, Pallas kernels, local_call(): pl.pallas_call(kernel, grid_spec=pltpu.PrefetchScalarGridSpec(num_scalar_...  81.2 us
    pallas_call x1, Pallas kernels, spread(): pl.pallas_call(spread_kernel, out_shape=[jax.ShapeDtypeStruct(s, jnp.floa...  31.1 us

profile of v8, /device:TPU:1, one launch (start us, length us, event | category | flops | bytes accessed | tf_op | source)
XLA Modules:
  0.0 390.9 jit_solution(11381690211342713967)
XLA Ops:
  0.7 0.7 select_reduce_fusion.2
  1.4 0.6 pad_add_fusion.tab
  2.1 0.8 select_reduce_fusion.1
  2.9 0.7 pad_add_fusion.1.tab
  3.7 0.7 fusion.1
  4.4 0.1 constant_dynamic-update-slice_fusion.3
  4.5 0.1 constant_dynamic-update-slice_fusion.2
  4.6 0.7 convert_remainder_fusion
  5.2 0.1 concatenate.27
  5.3 0.5 convert_element_type.26.tab
  5.8 0.1 broadcast_compare_fusion.1
  5.9 0.1 iota_compare_fusion.1
  6.0 0.3 convert_reduce_fusion
  6.3 0.1 constant_dynamic-update-slice_fusion.7
  6.4 0.1 constant_dynamic-update-slice_fusion.6
  6.5 0.1 constant_dynamic-update-slice_fusion.5
  6.6 0.3 select_reduce_fusion
  6.9 0.1 sub.69.tab
  6.9 0.0 copy-start
  7.0 0.6 broadcast_maximum_fusion.tab
  7.5 31.1 %shard_map.59 = (f32[2048,512]{1,0:T(8,128)}, f32[512,512]{1,0:T(8,128)}, f32[512,512]{1,0:T(8,128)}) custom-call(f32[2048,512]{1,0:T(8,128)} %front.3), custom_call_target="tpu_custom_call" | custom-call | tf_op jit(solution)/shard_map/pallas_call | solution.py:697
  38.7 26.8 %shard_map.60 = (f32[2048,512]{1,0:T(8,128)}, f32[4,2048,128]{2,1,0:T(8,128)}) custom-call(s32[10]{0:T(128)} %pad_add_fusion.tab, f32[2048,512]{1,0:T(8,128)} %front.3, f32[2048,512]{1,0:T(8,128)} %get-tuple-element.24.refs_0_, f32[512,512]{1,0:T(8,128)} %get-tuple-element.25.refs_1_, f32[512,512]{1,0:T(8,128)} %get-tuple-element.26.refs_2_), custom_call_target="tpu_custom_call" | custom-call | tf_op jit(solution)/shard_map/pallas_call | solution.py:83
  65.4 0.0 copy-done
  65.4 182.7 %shard_map.61 = (f32[32,16,768]{2,1,0:T(8,128)}, f32[32,16,768]{2,1,0:T(8,128)}, f32[32,16,768]{2,1,0:T(8,128)}, f32[32,16,768]{2,1,0:T(8,128)}, f32[8,24,16,128...) custom-call(s32[320]{0:T(512)} %broadcast_maximum_fusion.tab, ...), custom_call_target="tpu_custom_call" | custom-call | tf_op jit(solution)/shard_map/pallas_call | solution.py:270
  248.1 11.4 %shard_map.62 = f32[12,128,768]{2,1,0:T(8,128)} custom-call(s32[320]{0:T(512)} %copy-done, f32[12,128,768]{2,1,0:T(8,128)} %bitcast.40, f32[32,16,768]{2,1,0:T(8,128)} %get-tuple-element.29.refs_0_.refs_8_, f32[32,16,768]{2,1,0:T(8,128)} %get-tuple-element.30.refs_1_.refs_9_, f32[32,16,768]{2,1,0:T(8,128)} %get-tuple-element.31.refs_2_.refs_10_, ...), custom_call_target="tpu_custom_call" | custom-call | tf_op jit(solution)/shard_map/pallas_call | solution.py:83
  259.5 7.4 %shard_map.63 = (f32[1536,768]{1,0:T(8,128)}, f32[3,256,768]{2,1,0:T(8,128)}) custom-call(s32[15]{0:T(128)} %convert_element_type.26.tab, f32[1536,768]{1,0:T(8,128)} %bitcast.37, f32[1536,768]{1,0:T(8,128)} %bitcast.38), custom_call_target="tpu_custom_call" | custom-call | tf_op jit(solution)/shard_map/pallas_call | solution.py:83
  266.9 88.3 %shard_map.64 = (f32[4,4,48,768]{3,2,1,0:T(8,128)}, f32[4,4,48,768]{3,2,1,0:T(8,128)}, f32[3,8,32,768]{3,2,1,0:T(8,128)}, f32[3,8,32,768]{3,2,1,0:T(8,128)}) custom-call(s32[15]{0:T(128)} %convert_element_type.26.tab, f32[2,4,192,768]{3,2,1,0:T(8,128)} %bitcast.41, f32[3,8,32,768]{3,2,1,0:T(8,128)} %bitcast.43), custom_call_target="tpu_custom_call" | custom-call | tf_op jit(solution)/shard_map/pallas_call | solution.py:430
  355.2 35.7 %shard_map.65 = f32[1536,768]{1,0:T(8,128)} custom-call(s32[9]{0:T(128)} %pad_add_fusion.1.tab, f32[1536,768]{1,0:T(8,128)} %bitcast.39, f32[768,768]{1,0:T(8,128)} %bitcast.44, f32[768,768]{1,0:T(8,128)} %bitcast.45, f32[768,768]{1,0:T(8,128)} %bitcast.46, f32[768,768]{1,0:T(8,128)} %bitcast.47), custom_call_target="tpu_custom_call" | custom-call | tf_op jit(solution)/shard_map/pallas_call | solution.py:83
  (24 shorter events, 0.2 us)
Async XLA Ops:
  6.9 58.5 %copy-start = (s32[320]{0:T(512)}, s32[320]{0:T(512)S(1)}, u32[]{:S(2)}) copy-start(s32[320]{0:T(512)S(1)} %sub.69.tab) | copy-start | bytes 3844
